TPU v7x, 32 devices: a whole 2x2x4 slice. The times are simulated.
32 devices in a mesh: tile: 8 (over y, x, core), dp: 4 (over z).
Axes of the slice: x: 2, y: 2, z: 4, core: 2. Of those that a mesh axis runs over, the one named last changes fastest.
Arguments:
- scan_pixels: bfloat16 [4, 20, 2048, 128], P('dp', None, 'tile'), may hold values from -6 to 6
- labels: int32 [4, 10, 2048], P('dp', None, 'tile'), may hold values from 0 to 7
- conv1_weight: bfloat16 [3, 192, 128], replicated, may hold values from -0.25 to 0.25
- conv2_weight: bfloat16 [3, 384, 256], replicated, may hold values from -0.1875 to 0.1875
- context_weight: bfloat16 [7, 1792, 256], replicated, may hold values from -0.0546875 to 0.0546875
- up_weight: bfloat16 [256, 128], replicated, may hold values from -0.375 to 0.375
- skip_weight: bfloat16 [128, 128], replicated, may hold values from -0.5 to 0.5
- class_weight: bfloat16 [8, 128], replicated, may hold values from -0.12374368670764582 to 0.12374368670764582
Outputs:
- logits: float32 [4, 8, 10, 2048], P('dp', None, None, 'tile')
- grad_features: float32 [4, 10, 2048, 128], P('dp', None, 'tile')
- grad_conv1: float32 [3, 192, 128], replicated
- grad_conv2: float32 [3, 384, 256], replicated
- grad_context: float32 [7, 1792, 256], replicated
- grad_up: float32 [256, 128], replicated
- grad_skip: float32 [128, 128], replicated
- grad_out: float32 [8, 128], replicated
All inputs are finite; a program needn't handle non-finite values.
Results may differ from a plain program's by a relative error of at most 0.01.
Values may be sent and summed in bfloat16 or wider, within the bound.
No kernel may reach another device: no remote copies, remote signals or barrier semaphores. Data moves between devices by JAX's collectives and lax.ppermute only.
A program may use at most 128 MiB of HBM per device.

v0:
```python
import jax
import jax.numpy as jnp
from jax import lax
from jax.sharding import PartitionSpec as P

K = 8
COLUMN_SPREAD = 16


def shifted(block, axis, distance):
    devices = range(lax.axis_size(axis))
    route = [(i - distance, i) for i in devices if i - distance in devices]
    return lax.ppermute(block, axis, route)


def padded(value, sides, width):
    for axis, dim in sides:
        peers, length = (lax.axis_size(axis), value.shape[dim])
        up = [(i, (i + 1) % peers) for i in range(peers - 1)]
        down = [(j, i) for i, j in up]
        last = lax.slice_in_dim(value, length - width, length, axis=dim)
        initial = lax.slice_in_dim(value, 0, width, axis=dim)
        before = lax.ppermute(last, axis, up)
        after = lax.ppermute(initial, axis, down)
        value = jnp.concatenate([before, value, after], axis=dim)
    return value


def product(pattern, lhs_array, rhs_array):
    return jnp.einsum(pattern, lhs_array, rhs_array, preferred_element_type=jnp.float32)


def silu_slope(inputs):
    sigmoid_value = jax.nn.sigmoid(inputs)
    return sigmoid_value + inputs * sigmoid_value * (1.0 - sigmoid_value)


def column_taps(feature_map, left_edge):
    channels = feature_map.shape[-1] // 2
    even_cols = feature_map[..., :channels]
    odd_cols = feature_map[..., channels:]
    before_cols = jnp.concatenate([left_edge, odd_cols[:, :-1]], axis=1)
    joined = jnp.concatenate([before_cols, even_cols, odd_cols], axis=-1)
    paired = joined.reshape(joined.shape[0] // 2, 2, joined.shape[1], joined.shape[2])
    row_even = paired[:, 0]
    row_odd = paired[:, 1]
    row_before = jnp.concatenate([jnp.zeros_like(row_odd[:1]), row_odd[:-1]], axis=0)
    return (row_before, row_even, row_odd)


def conv_apply(taps, weight):
    running = product("rwc,cd->rwd", taps[0], weight[0])
    for tap_index in range(1, 3):
        running = running + product("rwc,cd->rwd", taps[tap_index], weight[tap_index])
    return running


def conv_weight_grad(taps, gradient):
    return jnp.stack([product("rwc,rwd->cd", taps[tap_index], gradient) for tap_index in range(3)])


def taps_back(gradient, weight, channels):
    grad_taps = [product("rwd,cd->rwc", gradient, weight[tap_index]) for tap_index in range(3)]
    grad_before, grad_even, grad_odd = grad_taps
    grad_odd = grad_odd + jnp.concatenate(
        [grad_before[1:], jnp.zeros_like(grad_before[:1])], axis=0
    )
    joined = jnp.stack([grad_even, grad_odd], axis=1)
    joined = joined.reshape(2 * grad_even.shape[0], grad_even.shape[1], grad_even.shape[2])
    col_before = joined[..., :channels]
    col_even = joined[..., channels : 2 * channels]
    col_odd = joined[..., 2 * channels :]
    col_odd = col_odd + jnp.concatenate(
        [col_before[:, 1:], jnp.zeros_like(col_before[:, :1])], axis=1
    )
    return (jnp.concatenate([col_even, col_odd], axis=-1), col_before[:, :1])


def context_taps(widened_map, slab_height, slab_width):
    bordered_map = jnp.pad(widened_map, ((3, 3), (0, 0), (0, 0)))
    return [
        jnp.concatenate(
            [
                bordered_map[
                    row_offset : row_offset + slab_height,
                    column_offset * COLUMN_SPREAD : column_offset * COLUMN_SPREAD + slab_width,
                ]
                for column_offset in range(7)
            ],
            axis=-1,
        )
        for row_offset in range(7)
    ]


def context_apply(stacks, weight):
    running = product("rwc,cd->rwd", stacks[0], weight[0])
    for row_offset in range(1, 7):
        running = running + product("rwc,cd->rwd", stacks[row_offset], weight[row_offset])
    return running


def context_back(widened_gradient, weight, slab_height, slab_width, channels):
    bordered_map = jnp.pad(widened_gradient, ((3, 3), (0, 0), (0, 0)))
    running = jnp.zeros((slab_height, slab_width, channels), jnp.float32)
    for row_offset in range(7):
        leading_row = 6 - row_offset
        picked_values = jnp.concatenate(
            [
                bordered_map[
                    leading_row : leading_row + slab_height,
                    (6 - column_offset) * COLUMN_SPREAD : (6 - column_offset) * COLUMN_SPREAD
                    + slab_width,
                ]
                for column_offset in range(7)
            ],
            axis=-1,
        )
        picked_values = picked_values.reshape(slab_height, slab_width, 7, channels)
        running = running + product(
            "rwbd,bcd->rwc", picked_values, weight[row_offset].reshape(7, channels, channels)
        )
    return running


def body(
    scan_pixels,
    labels,
    conv1_weight,
    conv2_weight,
    context_weight,
    up_weight,
    skip_weight,
    class_weight,
):
    image_tile = scan_pixels[0]
    label_tile = labels[0]
    channels_in = image_tile.shape[-1] // 2
    first_edge = shifted(image_tile[:, -1:, channels_in:], "tile", 1)
    first_taps = column_taps(image_tile, first_edge)
    first_pre = conv_apply(first_taps, conv1_weight)
    first_map = jax.nn.silu(first_pre).astype(jnp.bfloat16)
    half_rows, first_cols, width_one = first_map.shape
    second_field = first_map.reshape(half_rows, first_cols // 2, 2 * width_one)
    second_edge = shifted(second_field[:, -1:, width_one:], "tile", 1)
    second_taps = column_taps(second_field, second_edge)
    second_pre = conv_apply(second_taps, conv2_weight)
    later_feature_map = jax.nn.silu(second_pre).astype(jnp.bfloat16)
    slab_height, slab_width, width_two = later_feature_map.shape
    widened_map = padded(later_feature_map, (("tile", 1),), 3 * COLUMN_SPREAD)
    stacks = context_taps(widened_map, slab_height, slab_width)
    context_pre = context_apply(stacks, context_weight)
    context = (later_feature_map.astype(jnp.float32) + jax.nn.silu(context_pre)).astype(
        jnp.bfloat16
    )
    coarse_mix = product("rwc,cd->rwd", context, up_weight)
    upsampled = jnp.broadcast_to(
        coarse_mix[:, None, :, None, :], (slab_height, 2, slab_width, 2, width_one)
    ).reshape(half_rows, first_cols, width_one)
    decoder_pre = product("rwc,cd->rwd", first_map, skip_weight) + upsampled
    decoded = jax.nn.silu(decoder_pre).astype(jnp.bfloat16)
    logits = product("rwc,kc->krw", decoded, class_weight)
    target = (label_tile[None] == jnp.arange(K, dtype=jnp.int32)[:, None, None]).astype(jnp.float32)
    grad_logits = (jax.nn.sigmoid(logits) - target).astype(jnp.bfloat16)
    out_term = product("krw,rwc->kc", grad_logits, decoded)
    grad_decoded = product("krw,kc->rwc", grad_logits, class_weight)
    grad_decoder = (grad_decoded * silu_slope(decoder_pre)).astype(jnp.bfloat16)
    skip_term = product("rwc,rwd->cd", first_map, grad_decoder)
    pooled = (
        grad_decoder.astype(jnp.float32)
        .reshape(slab_height, 2, slab_width, 2, width_one)
        .sum(axis=(1, 3))
        .astype(jnp.bfloat16)
    )
    up_term = product("rwc,rwd->cd", context, pooled)
    grad_context_map = product("rwd,cd->rwc", pooled, up_weight)
    skip_features = product("rwd,cd->rwc", grad_decoder, skip_weight)
    context_input_gradient = (grad_context_map * silu_slope(context_pre)).astype(jnp.bfloat16)
    context_term = jnp.stack(
        [
            product("rwc,rwd->cd", stacks[row_offset], context_input_gradient)
            for row_offset in range(7)
        ]
    )
    widened_gradient = padded(context_input_gradient, (("tile", 1),), 3 * COLUMN_SPREAD)
    grad_second = grad_context_map + context_back(
        widened_gradient, context_weight, slab_height, slab_width, width_two
    )
    second_grad = (grad_second * silu_slope(second_pre)).astype(jnp.bfloat16)
    conv2_term = conv_weight_grad(second_taps, second_grad)
    grad_field, grad_edge = taps_back(second_grad, conv2_weight, width_one)
    returned = shifted(grad_edge, "tile", -1)
    last_pair = grad_field[:, -1:] + jnp.concatenate([jnp.zeros_like(returned), returned], axis=-1)
    grad_field = jnp.concatenate([grad_field[:, :-1], last_pair], axis=1)
    grad_features = skip_features + grad_field.reshape(half_rows, first_cols, width_one)
    first_grad = (grad_features * silu_slope(first_pre)).astype(jnp.bfloat16)
    conv1_term = conv_weight_grad(first_taps, first_grad)
    tile_count = lax.axis_size("tile")
    pixel_count = lax.axis_size("dp") * half_rows * first_cols * tile_count
    summed = lax.psum(
        (conv1_term, conv2_term, context_term, up_term, skip_term, out_term), ("tile", "dp")
    )
    scaled = tuple((running / pixel_count for running in summed))
    return (
        logits[None],
        grad_features[None],
        scaled[0],
        scaled[1],
        scaled[2],
        scaled[3],
        scaled[4],
        scaled[5],
    )


def solution(mesh):
    in_specs = (P("dp", None, "tile", None), P("dp", None, "tile"), P(), P(), P(), P(), P(), P())
    out_specs = (
        P("dp", None, None, "tile"),
        P("dp", None, "tile", None),
        P(),
        P(),
        P(),
        P(),
        P(),
        P(),
    )
    return jax.shard_map(body, mesh=mesh, in_specs=in_specs, out_specs=out_specs, check_vma=False)
```

profile of v0, /device:TPU:0, one launch (start us, length us, event | category | flops | bytes accessed | tf_op | source)
XLA Modules:
  0.0 438.2 jit_solution(13329895807192602287)
XLA Ops:
  7.2 1.7 copy.36
  9.1 3.1 collective-permute-start
  13.7 2.0 pad_maximum_fusion.4
  16.9 1.7 fusion.39
  18.8 5.8 %collective-permute-start.1 = (bf16[10,1,128]{2,1,0:T(2,128)(2,1)S(1)}, bf16[10,1,128]{2,1,0:T(2,128)(2,1)S(1)}, u32[]{:S(2)}, u32[]{:S(2)}) collective-permute-start(bf16[10,1,128]{2,1,0:T(2,128)(2,1)S(1)} %slice.585), channel_id=1, source_target_pairs={{0,4},{4,8},{8,12},{12,16},{16,20},{20,24},{24,28},{1,5},{5,9},{9,... | collective-permute-start | bytes 7688 | tf_op jit(solution)/shard_map/ppermute | solution.py:13
  28.7 5.2 %collective-permute-start.2 = (bf16[5,48,256]{2,1,0:T(8,128)(2,1)S(1)}, bf16[5,48,256]{2,1,0:T(8,128)(2,1)S(1)}, u32[]{:S(2)}, u32[]{:S(2)}) collective-permute-start(bf16[5,48,256]{2,1,0:T(8,128)(2,1)S(1)} %get-tuple-element.109), channel_id=1, source_target_pairs={{0,4},{4,8},{8,12},{12,16},{16,20},{20,24},{24,28},{1,5},{5,9},{9,... | collective-permute-start | bytes 368648 | tf_op jit(solution)/shard_map/ppermute | solution.py:23
  33.9 5.6 %fusion.131 = (bf16[1,1792,256]{2,1,0:T(8,128)(2,1)}, bf16[1,1792,256]{2,1,0:T(8,128)(2,1)}, bf16[1,1792,256]{2,1,0:T(8,128)(2,1)}, bf16[1,1792,256]{2,1,0:T(8,1...) fusion(bf16[7,1792,256]{2,1,0:T(8,128)(2,1)} %param.12), kind=kLoop, calls=%fused_computation.300 | loop fusion | bytes 12845056 | tf_op jit(solution)/shard_map/slice | solution.py:97
  41.0 3.4 slice-done
  44.3 2.2 slice-done.1
  52.1 1.6 add_convert_fusion
  58.8 2.4 multiply_convert_fusion.1
  64.5 5.2 %collective-permute-start.4 = (bf16[5,48,256]{2,1,0:T(8,128)(2,1)S(1)}, bf16[5,48,256]{2,1,0:T(8,128)(2,1)S(1)}, u32[]{:S(2)}, u32[]{:S(2)}) collective-permute-start(bf16[5,48,256]{2,1,0:T(8,128)(2,1)S(1)} %get-tuple-element.107), channel_id=1, source_target_pairs={{0,4},{4,8},{8,12},{12,16},{16,20},{20,24},{24,28},{1,5},{5,9},{9,... | collective-permute-start | bytes 368648 | tf_op jit(solution)/shard_map/ppermute | solution.py:23
  79.4 3.7 copy-done.2
  85.8 1.5 slice_dynamic-update-slice_fusion.39
  87.3 1.4 slice_dynamic-update-slice_fusion.38
  88.7 1.4 slice_dynamic-update-slice_fusion.37
  90.1 1.5 slice_dynamic-update-slice_fusion.36
  93.7 4.4 %copy.53 = bf16[5,128,1792]{1,2,0:T(8,128)(2,1)} copy(bf16[5,128,1792]{2,1,0:T(8,128)(2,1)} %slice_dynamic-update-slice_fusion) | data formatting | bytes 4587520 | tf_op jit(solution)/shard_map/concatenate | solution.py:108
  98.1 4.2 copy.51
  102.3 4.2 copy.49
  112.0 4.1 copy.47
  116.1 4.2 copy.45
  120.3 4.2 copy.43
  124.4 3.4 copy.41
  127.9 2.8 convolution_bitcast_fusion.8
  144.1 1.8 collective-permute-done.6
  146.2 3.4 multiply_convert_fusion
  152.8 47.0 %psum.47 = f32[8,128]{1,0:T(8,128)S(1)} all-reduce(f32[8,128]{1,0:T(8,128)S(1)} %convolution_bitcast_fusion.23), channel_id=1, replica_groups=mesh['tile'=8,'dp'=4] {'tile','dp'}, use_global_device_ids=true, to_apply=%region_6.7 | all-reduce | flops 1024 | bytes 8192 | tf_op jit(solution)/shard_map/psum | solution.py:200
  200.4 214.3 %all-reduce.10.cloned.1.call-done = (f32[3,192,128]{2,1,0:T(8,128)}, f32[3,384,256]{2,1,0:T(8,128)}, f32[7,1792,256]{2,1,0:T(8,128)}, f32[256,128]{1,0:T(8,128)}, f32[128,128]{1,0:T(8,128)}) async-done(((f32[3,192,128]{2,1,0:T(8,128)}, f32[3,384,256]{2,1,0:T(8,128)}, f32[7,1792,256]{2,1,0:T(8,128)}, f32[256,128]{1,0:T(8,128)}, f32[128,128]{1,0:T(8,128)}), (f32[3,192,128]{2,1,0:T(8,128)}, ...) | async-done | bytes 14516240 | tf_op jit(solution)/shard_map/psum | solution.py:200
  414.7 1.7 broadcast_multiply_fusion.2
  416.4 2.4 broadcast_multiply_fusion.1
  418.8 10.7 %broadcast_multiply_fusion = f32[7,1792,256]{2,1,0:T(8,128)} fusion(f32[7,1792,256]{2,1,0:T(8,128)} %get-tuple-element.10), kind=kLoop, calls=%fused_computation | loop fusion | flops 3211264 | bytes 25690112 | tf_op jit(solution)/shard_map/div | solution.py:203
  (200 shorter events, 60.5 us)
Async XLA Ops:
  7.2 46.6 %copy-start = (bf16[256,128]{1,0:T(8,128)(2,1)S(1)}, bf16[256,128]{1,0:T(8,128)(2,1)}, u32[]{:S(2)}) copy-start(bf16[256,128]{1,0:T(8,128)(2,1)} %param.13) | copy-start | bytes 196612
  7.2 5.9 %copy-start.3 = (bf16[1,20,256,128]{3,2,1,0:T(8,128)(2,1)S(1)}, bf16[1,20,256,128]{3,2,1,0:T(8,128)(2,1)}, u32[]{:S(2)}) copy-start(bf16[1,20,256,128]{3,2,1,0:T(8,128)(2,1)} %param.8) | copy-start | bytes 3932164
  7.2 407.5 %all-reduce.10.cloned.1.call-start = ((), (), s32[]{:S(2)}) async-start(), calls=%async_computation | async-start | bytes 29032448 | tf_op jit(solution)/shard_map/psum | solution.py:200
  9.1 4.6 %collective-permute-start = (bf16[20,1,64]{1,2,0:T(8,128)(2,1)S(1)}, bf16[20,1,64]{1,2,0:T(8,128)(2,1)}, u32[]{:S(2)}, u32[]{:S(2)}) collective-permute-start(bf16[20,1,64]{1,2,0:T(8,128)(2,1)S(1)} %slice.579), channel_id=1, source_target_pairs={{0,4},{4,8},{8,12},{12,16},{16,20},{20,24},{24,28},{1,5},{5,9},{9,... | collective-permute-start | bytes 7688 | tf_op jit(solution)/shard_map/ppermute | solution.py:13
  13.7 3.2 copy-start.4
  18.6 6.9 %copy-start.16 = (bf16[3,384,256]{2,1,0:T(8,128)(2,1)S(1)}, bf16[3,384,256]{2,1,0:T(8,128)(2,1)}, u32[]{:S(2)}) copy-start(bf16[3,384,256]{2,1,0:T(8,128)(2,1)} %param.11) | copy-start | bytes 1769476
  18.8 6.6 %collective-permute-start.1 = (bf16[10,1,128]{2,1,0:T(2,128)(2,1)S(1)}, bf16[10,1,128]{2,1,0:T(2,128)(2,1)S(1)}, u32[]{:S(2)}, u32[]{:S(2)}) collective-permute-start(bf16[10,1,128]{2,1,0:T(2,128)(2,1)S(1)} %slice.585), channel_id=1, source_target_pairs={{0,4},{4,8},{8,12},{12,16},{16,20},{20,24},{24,28},{1,5},{5,9},{9,... | collective-permute-start | bytes 7688 | tf_op jit(solution)/shard_map/ppermute | solution.py:13
  27.4 12.2 %collective-permute-start.3 = (bf16[5,48,256]{2,1,0:T(8,128)(2,1)S(1)}, bf16[5,48,256]{2,1,0:T(8,128)(2,1)S(1)}, u32[]{:S(2)}, u32[]{:S(2)}) collective-permute-start(bf16[5,48,256]{2,1,0:T(8,128)(2,1)S(1)} %get-tuple-element.110), channel_id=1, source_target_pairs={{4,0},{8,4},{12,8},{16,12},{20,16},{24,20},{28,24},{5,1},{9,5},{13... | collective-permute-start | bytes 368648 | tf_op jit(solution)/shard_map/ppermute | solution.py:24
  28.7 10.9 %copy-start.44 = (s32[1,10,256]{2,0,1:T(1,128)S(1)}, s32[1,10,256]{2,0,1:T(1,128)}, u32[]{:S(2)}) copy-start(s32[1,10,256]{2,0,1:T(1,128)} %param.9) | copy-start | bytes 30724
  28.7 10.9 %collective-permute-start.2 = (bf16[5,48,256]{2,1,0:T(8,128)(2,1)S(1)}, bf16[5,48,256]{2,1,0:T(8,128)(2,1)S(1)}, u32[]{:S(2)}, u32[]{:S(2)}) collective-permute-start(bf16[5,48,256]{2,1,0:T(8,128)(2,1)S(1)} %get-tuple-element.109), channel_id=1, source_target_pairs={{0,4},{4,8},{8,12},{12,16},{16,20},{20,24},{24,28},{1,5},{5,9},{9,... | collective-permute-start | bytes 368648 | tf_op jit(solution)/shard_map/ppermute | solution.py:23
  40.4 4.0 slice-start
  40.6 6.0 %slice-start.1 = ((s8[6422528]{0:T(1024)(128)(4,1)}), s8[2228224]{0:T(1024)(128)(4,1)S(1)}, s32[]{:S(2)}) async-start(s8[6422528]{0:T(1024)(128)(4,1)} %bitcast.330), calls=%async_computation.2 | async-start | bytes 4456448
  40.9 7.2 %copy-start.34 = (bf16[5,128,1792]{2,1,0:T(8,128)(2,1)}, bf16[5,128,1792]{2,1,0:T(8,128)(2,1)S(1)}, u32[]{:S(2)}) copy-start(bf16[5,128,1792]{2,1,0:T(8,128)(2,1)S(1)} %get-tuple-element.67) | copy-start | bytes 6881284
  40.9 7.3 %copy-start.38 = (bf16[5,128,1792]{2,1,0:T(8,128)(2,1)}, bf16[5,128,1792]{2,1,0:T(8,128)(2,1)S(1)}, u32[]{:S(2)}) copy-start(bf16[5,128,1792]{2,1,0:T(8,128)(2,1)S(1)} %get-tuple-element.69) | copy-start | bytes 6881284
  40.9 8.1 %copy-start.40 = (bf16[5,128,1792]{2,1,0:T(8,128)(2,1)}, bf16[5,128,1792]{2,1,0:T(8,128)(2,1)S(1)}, u32[]{:S(2)}) copy-start(bf16[5,128,1792]{2,1,0:T(8,128)(2,1)S(1)} %get-tuple-element.70) | copy-start | bytes 6881284
  41.0 8.1 %copy-start.36 = (bf16[5,128,1792]{2,1,0:T(8,128)(2,1)}, bf16[5,128,1792]{2,1,0:T(8,128)(2,1)S(1)}, u32[]{:S(2)}) copy-start(bf16[5,128,1792]{2,1,0:T(8,128)(2,1)S(1)} %get-tuple-element.68) | copy-start | bytes 6881284
  41.0 10.4 %copy-start.32 = (bf16[5,128,1792]{2,1,0:T(8,128)(2,1)}, bf16[5,128,1792]{2,1,0:T(8,128)(2,1)S(1)}, u32[]{:S(2)}) copy-start(bf16[5,128,1792]{2,1,0:T(8,128)(2,1)S(1)} %get-tuple-element.66) | copy-start | bytes 6881284
  41.0 11.1 %copy-start.30 = (bf16[5,128,1792]{2,1,0:T(8,128)(2,1)}, bf16[5,128,1792]{2,1,0:T(8,128)(2,1)S(1)}, u32[]{:S(2)}) copy-start(bf16[5,128,1792]{2,1,0:T(8,128)(2,1)S(1)} %get-tuple-element.65) | copy-start | bytes 6881284
  55.5 96.1 %copy-start.27 = (f32[10,256,8]{1,2,0:T(8,128)}, f32[10,256,8]{1,2,0:T(8,128)S(1)}, u32[]{:S(2)}) copy-start(f32[10,256,8]{1,2,0:T(8,128)S(1)} %fusion.108) | copy-start | bytes 245764
  61.3 8.4 %copy-start.39 = (bf16[5,128,1792]{2,1,0:T(8,128)(2,1)S(1)}, bf16[5,128,1792]{2,1,0:T(8,128)(2,1)}, u32[]{:S(2)}) copy-start(bf16[5,128,1792]{2,1,0:T(8,128)(2,1)} %copy-done.38) | copy-start | bytes 6881284
  63.2 16.2 %collective-permute-start.5 = (bf16[5,48,256]{2,1,0:T(8,128)(2,1)S(1)}, bf16[5,48,256]{2,1,0:T(8,128)(2,1)S(1)}, u32[]{:S(2)}, u32[]{:S(2)}) collective-permute-start(bf16[5,48,256]{2,1,0:T(8,128)(2,1)S(1)} %get-tuple-element.108), channel_id=1, source_target_pairs={{4,0},{8,4},{12,8},{16,12},{20,16},{24,20},{28,24},{5,1},{9,5},{13... | collective-permute-start | bytes 368648 | tf_op jit(solution)/shard_map/ppermute | solution.py:24
  64.5 6.1 %copy-start.37 = (bf16[5,128,1792]{2,1,0:T(8,128)(2,1)S(1)}, bf16[5,128,1792]{2,1,0:T(8,128)(2,1)}, u32[]{:S(2)}) copy-start(bf16[5,128,1792]{2,1,0:T(8,128)(2,1)} %copy-done.36) | copy-start | bytes 6881284
  64.5 18.6 %collective-permute-start.4 = (bf16[5,48,256]{2,1,0:T(8,128)(2,1)S(1)}, bf16[5,48,256]{2,1,0:T(8,128)(2,1)S(1)}, u32[]{:S(2)}, u32[]{:S(2)}) collective-permute-start(bf16[5,48,256]{2,1,0:T(8,128)(2,1)S(1)} %get-tuple-element.107), channel_id=1, source_target_pairs={{0,4},{4,8},{8,12},{12,16},{16,20},{20,24},{24,28},{1,5},{5,9},{9,... | collective-permute-start | bytes 368648 | tf_op jit(solution)/shard_map/ppermute | solution.py:23
  78.2 4.9 %copy-start.2 = (f32[7,1792,256]{2,1,0:T(8,128)}, f32[7,1792,256]{2,1,0:T(8,128)S(1)}, u32[]{:S(2)}) copy-start(f32[7,1792,256]{2,1,0:T(8,128)S(1)} %fusion) | copy-start | bytes 38535172
  127.8 2.9 copy-start.12
  127.8 2.9 copy-start.24
  141.6 4.3 collective-permute-start.6
  146.2 3.4 copy-start.5
  146.2 3.4 copy-start.19
  418.8 10.7 %copy-start.28 = (f32[256,128]{1,0:T(8,128)S(1)}, f32[256,128]{1,0:T(8,128)}, u32[]{:S(2)}) copy-start(f32[256,128]{1,0:T(8,128)} %get-tuple-element.11) | copy-start | bytes 393220
  418.8 11.4 %copy-start.29 = (f32[128,128]{1,0:T(8,128)S(1)}, f32[128,128]{1,0:T(8,128)}, u32[]{:S(2)}) copy-start(f32[128,128]{1,0:T(8,128)} %get-tuple-element.12) | copy-start | bytes 196612
  418.8 12.1 %copy-start.1 = (bf16[256,128]{1,0:T(8,128)(2,1)S(1)}, bf16[256,128]{1,0:T(8,128)(2,1)}, u32[]{:S(2)}) copy-start(bf16[256,128]{1,0:T(8,128)(2,1)} %param.13) | copy-start | bytes 196612
  (24 other events, 38.8 us)
Sparse Core Ops, SparseCore 0:
  151.7 262.9 all-reduce.9
where the time goes:
time: 443 us; the launch traced here: 438 us
  waiting for transfers between devices  217 us (49%)
  local copies, waits for them, and re-layouts  68.4 us (15%)
  blocking collectives  47 us (11%)
  matrix products  36.6 us (8%)
  other arithmetic  30.9 us (7%)
  starting transfers between devices  23.2 us (5%)
  between operations  15.5 us (3%)
    psum x1, waiting for transfers between devices, body(): lax.psum((conv1_term, conv2_term, context_term, up_term, skip_term, out_t...  214 us
    psum x1, blocking collectives, body(): lax.psum((conv1_term, conv2_term, context_term, up_term, skip_term, out_t...  47 us
    dot_general x44, matrix products, product(): jnp.einsum(pattern, lhs_array, rhs_array, preferred_element_type=jnp.floa...  36.3 us
    concatenate x9, local copies, waits for them, and re-layouts, context_back(): jnp.concatenate([bordered_map[leading_row:leading_row + slab_height, (6 -...  30.7 us
    unnamed x112, local copies, waits for them, and re-layouts  29 us
    div x6, other arithmetic, body(): scaled = tuple((running / pixel_count for running in summed))  16.7 us
    ppermute x2, starting transfers between devices, padded(): before = lax.ppermute(last, axis, up)  10.4 us
    ppermute x3, starting transfers between devices, shifted(): return lax.ppermute(block, axis, route)  10.2 us
  transfers between devices with their start and end apart: 8, of which 3 were waited for; matrix products, arithmetic and copies ran while one was open for 4% of the time, Pallas kernels for 0%

commit v1 on v0

v1 whole, which is shorter than its diff:
```python
import functools

import jax
import jax.numpy as jnp
from jax import lax
from jax.experimental import pallas as pl
from jax.experimental.pallas import tpu as pltpu
from jax.sharding import PartitionSpec as P

K = 8
COLUMN_SPREAD = 16
TAPS = 7
BOTH = ("tile", "dp")
VMEM = pl.BlockSpec(memory_space=pltpu.VMEM)
SMEM = pl.BlockSpec(memory_space=pltpu.SMEM)
ANY = pl.BlockSpec(memory_space=pl.ANY)

LIGHT = pl.CostEstimate(flops=1000, bytes_accessed=1000, transcendentals=0)


def params(mebibytes):
    return pltpu.CompilerParams(vmem_limit_bytes=mebibytes * 1024 * 1024)


def flip(value, tile_mask, dp_mask):
    tiles, slabs = lax.axis_size("tile"), lax.axis_size("dp")
    route = [
        (t * slabs + z, (t ^ tile_mask) * slabs + (z ^ dp_mask))
        for t in range(tiles)
        for z in range(slabs)
    ]
    return lax.ppermute(value, BOTH, route)


def bits(count):
    return count.bit_length() - 1


def position():
    t, z = lax.axis_index("tile"), lax.axis_index("dp")
    return t, z, (z & 1) ^ ((z >> 1) & 1)


def row_pairs(rows):
    out = []
    for first in range(0, rows, 2):
        pair = [i for i in (first, first + 1) if i < rows]
        low = max(0, pair[0] - 3)
        high = min(rows, pair[-1] + 4)
        out.append((pair, low, high))
    return out


def wgrad_kernel(chips, rows, width, block, place, *refs):
    masks = 2 * chips
    own, other = refs[:masks], refs[masks : 2 * masks]
    out, features, wide, stacked, total = refs[2 * masks :]
    chip, core = place[0] >> 1, place[0] & 1
    columns = 2 * chips * width
    for m in range(masks):
        slab, mask = m // chips, m % chips
        for k in range(2):
            tile = 2 * (chip ^ mask) + (core ^ k)
            at = pl.multiple_of(tile * width, width)
            for i in range(rows):
                start = (rows * (width + k * block)) + i * block
                features[slab, i, pl.ds(at, width), :] = (own, other)[k][m][
                    i * width : (i + 1) * width, :
                ]
                wide[slab, i, :, pl.ds(pl.multiple_of(at + 128, 128), width)] = own[m][
                    start : start + block, :
                ].astype(jnp.float32)
    for slab in range(2):
        for i in range(rows):
            edge = jnp.zeros((block, 128), jnp.float32)
            wide[slab, i, :, 0:128] = edge
            wide[slab, i, :, 128 + columns : 256 + columns] = edge
            for b in range(TAPS):
                start = 128 - (b - 3) * COLUMN_SPREAD
                stacked[slab, i, b * block : (b + 1) * block, :] = wide[
                    slab, i, :, start : start + columns
                ].astype(jnp.bfloat16)
    total[...] = jnp.zeros_like(total)
    for slab in range(2):
        for pair, low, high in row_pairs(rows):
            lhs = stacked[slab, low:high].reshape((high - low) * TAPS * block, columns)
            rhs = jnp.concatenate([features[slab, i] for i in pair], axis=-1)
            result = jnp.dot(lhs, rhs, preferred_element_type=jnp.float32)
            for n, i in enumerate(pair):
                for j in range(low, high):
                    a = i - j + 3
                    if 0 <= a < TAPS:
                        total[a] += result[
                            (j - low) * TAPS * block : (j - low + 1) * TAPS * block,
                            n * 128 : (n + 1) * 128,
                        ]
    out[...] = total[...].reshape(out.shape).astype(jnp.bfloat16)


def wgrad(place, own, other, chips, rows, width, block):
    columns = 2 * chips * width
    return pl.pallas_call(
        functools.partial(wgrad_kernel, chips, rows, width, block),
        out_shape=jax.ShapeDtypeStruct((TAPS * TAPS * block, 128), jnp.bfloat16),
        in_specs=[SMEM] + [VMEM] * (2 * len(own)),
        out_specs=VMEM,
        scratch_shapes=[
            pltpu.VMEM((2, rows, columns, 128), jnp.bfloat16),
            pltpu.VMEM((2, rows, block, columns + 256), jnp.float32),
            pltpu.VMEM((2, rows, TAPS * block, columns), jnp.bfloat16),
            pltpu.VMEM((TAPS, TAPS * block, 128), jnp.float32),
        ],
        compiler_params=params(56),
        cost_estimate=LIGHT,
        name="context_term",
    )(place, *own, *other)


def pack_kernel(chips, rows, width, block, place, features, mine, theirs, *messages):
    half = place[1]
    for m, message in enumerate(messages):
        mask = m % chips
        at = pl.multiple_of((half ^ (m // chips)) * 128, 128)
        for i in range(rows):
            message[i * width : (i + 1) * width, :] = features[i, :, pl.ds(at, 128)]
            for k, part in enumerate((mine, theirs)):
                start = rows * (width + k * block) + i * block
                message[start : start + block, :] = part[mask, i]


def pack(place, features, mine, theirs):
    rows, width = features.shape[0], features.shape[1]
    chips, block = mine.shape[0], mine.shape[2]
    shape = jax.ShapeDtypeStruct((rows * (width + 2 * block), 128), jnp.bfloat16)
    return pl.pallas_call(
        functools.partial(pack_kernel, chips, rows, width, block),
        out_shape=[shape] * (2 * chips),
        in_specs=[SMEM] + [VMEM] * 3,
        out_specs=[VMEM] * (2 * chips),
        compiler_params=params(56),
        cost_estimate=LIGHT,
        name="pack",
    )(place, features, mine, theirs)


def unpack_kernel(orders, bounds, chips, block, place, *refs):
    parts = len(orders)
    sources = [refs[4 * p : 4 * p + 4] for p in range(parts)]
    out = refs[4 * parts]
    gathered, ready, sems = refs[4 * parts + 1 :]
    tile, half = place[0], place[1]
    chip, core = tile >> 1, tile & 1
    ones = [lax.broadcasted_iota(jnp.int32, (128, 128), n) for n in range(2)]
    identity = (ones[0] == ones[1]).astype(jnp.bfloat16)
    batches = [
        (p, n, min(4, bounds[p + 1] - n))
        for p in range(parts)
        for n in range(bounds[p], bounds[p + 1], 4)
    ]

    def copy(n):
        _, start, count = batches[n]
        return pltpu.make_async_copy(
            ready.at[n % 2, 0:count], out.at[start : start + count], sems.at[n % 2]
        )

    for n, (p, start, count) in enumerate(batches):
        entries = sources[p][0].shape[0]
        for s in range(4):
            for i in range(entries):
                index = i + entries * (s % 2)
                mask = sum(1 << d for q, d in enumerate(orders[p]) if (index >> q) & 1)
                whose = 2 * (chip ^ (mask % chips)) + (core ^ (s // 2))
                for g in range(count):
                    at = (start - bounds[p] + g) * block
                    gathered[
                        n % 2,
                        g,
                        half ^ (mask // chips),
                        pl.ds(pl.multiple_of(whose * block, block), block),
                        :,
                    ] = sources[p][s][i, at : at + block, :]
        if n >= 2:
            copy(n - 2).wait()
        for g in range(count):
            for u in range(2):
                ready[n % 2, g, u * 128 : (u + 1) * 128, :] = dot(
                    identity, gathered[n % 2, g, u], NT
                )
        copy(n).start()
    for n in range(max(0, len(batches) - 2), len(batches)):
        copy(n).wait()


def unpack(place, sources, orders, bounds, chips, block):
    wide = 2 * chips * block
    operands = [array for group in sources for array in group]
    return pl.pallas_call(
        functools.partial(unpack_kernel, orders, bounds, chips, block),
        out_shape=jax.ShapeDtypeStruct((TAPS * TAPS, 256, wide), jnp.float32),
        in_specs=[SMEM] + [VMEM] * len(operands),
        out_specs=ANY,
        scratch_shapes=[
            pltpu.VMEM((2, 4, 2, wide, 128), jnp.bfloat16),
            pltpu.VMEM((2, 4, 256, wide), jnp.float32),
            pltpu.SemaphoreType.DMA((2,)),
        ],
        compiler_params=params(56),
        cost_estimate=LIGHT,
        name="context_out",
    )(place, *operands)


def fold_small(packed, chips, first):
    t, _, half = position()
    steps = [(1, 0, t & 1)]
    for d in range(bits(chips)):
        steps.append((2 << d, 0, (t >> (d + 1)) & 1))
    steps.append((0, 1, half))
    for tile_mask, dp_mask, bit in steps:
        pairs = packed.reshape(2, packed.shape[0] // 2, 128)
        mine = lax.dynamic_index_in_dim(pairs, bit, 0, False)
        theirs = lax.dynamic_index_in_dim(pairs, 1 - bit, 0, False).astype(jnp.bfloat16)
        packed = mine + flip(theirs, tile_mask, dp_mask).astype(jnp.float32)
        if tile_mask == 1:
            packed, first = lax.optimization_barrier((packed, first))
    return packed.astype(jnp.bfloat16), first


def sum_and_share(term, small, place, chips, block, scale, results, packed_rows):
    dims = bits(chips) + 1
    groups = TAPS * TAPS
    bounds = [groups * p // dims for p in range(dims + 1)]
    parts = [term[bounds[p] * block : bounds[p + 1] * block] for p in range(dims)]
    parts.append(small)
    totals, mask = [part.astype(jnp.float32) for part in parts], 3
    while mask < lax.axis_size("dp"):
        parts = [total.astype(jnp.bfloat16) for total in totals]
        others = [flip(part, 0, mask) for part in parts]
        others, results = lax.optimization_barrier((others, results))
        totals = [
            part.astype(jnp.float32) + other.astype(jnp.float32)
            for part, other in zip(parts, others)
        ]
        mask = 4 if mask == 3 else 2 * mask
    totals[-2:] = [jnp.concatenate(totals[-2:])]
    parts = [(total * scale).astype(jnp.bfloat16)[None] for total in totals]
    orders = [[(p + q) % dims for q in range(dims)] for p in range(dims)]

    def across(value, dim):
        return flip(value, 2 << dim, 0) if dim < dims - 1 else flip(value, 0, 1)

    for q in range(dims - 1):
        others = [across(part, orders[p][q]) for p, part in enumerate(parts)]
        others = lax.optimization_barrier(others)
        parts = [jnp.concatenate(pair) for pair in zip(parts, others)]
    last = [across(part, orders[p][-1]) for p, part in enumerate(parts)]
    near = [flip(part, 1, 0) for part in parts]
    far = [flip(part, 1, 0) for part in last]
    sources = list(zip(parts, last, near, far))
    target = unpack(place, sources, orders, bounds, chips, block)
    sources = sources[-1]
    return target, unpack_small(place, sources, orders[-1], chips, packed_rows), results


def dot(lhs, rhs, dims=((1,), (0,))):
    return lax.dot_general(lhs, rhs, (dims, ((), ())), preferred_element_type=jnp.float32)


NT = ((1,), (1,))
TN = ((0,), (0,))


def encode_kernel(image, halo, weight1, weight2, taps, slope1, features, slope2, odd):
    rows, pairs = image.shape[0] // 2, image.shape[1]
    empty = jnp.zeros((pairs + 16, 256), jnp.bfloat16)

    def line(n):
        if n < 0:
            return empty
        return jnp.concatenate([halo[n], image[n]], axis=0)

    lhs = jnp.concatenate(
        [
            jnp.concatenate([line(2 * i + a - 1) for i in range(rows)], axis=0)
            for a in range(3)
        ],
        axis=1,
    )
    none = jnp.zeros((64, 128), jnp.bfloat16)
    rhs = []
    for a in range(3):
        for_odd = jnp.concatenate([none, weight1[a]], axis=0)
        for_even = jnp.concatenate([weight1[a, 64:], none, none], axis=0)
        for_next = jnp.concatenate([none, none, none, weight1[a, :64]], axis=0)
        rhs.append(jnp.concatenate([for_odd, for_even, for_next], axis=1))
    result = dot(lhs, jnp.concatenate(rhs, axis=0)).reshape(rows, pairs + 16, 384)
    odd[...] = result[:, :, 256:384]
    even_pre = result[:, 16:, 128:256] + odd[:, 15 : 15 + pairs, :]
    gate = jax.nn.sigmoid(even_pre)
    value = even_pre * gate
    taps[:, :, 128:256] = value.astype(jnp.bfloat16)
    slope1[:, :, 0:128] = gate + value * (1.0 - gate)
    odd_pre = result[:, :, 0:128]
    gate = jax.nn.sigmoid(odd_pre)
    value = odd_pre * gate
    odd[...] = value
    taps[:, :, 256:384] = value[:, 16:].astype(jnp.bfloat16)
    slope1[:, :, 128:256] = (gate + value * (1.0 - gate))[:, 16:]
    taps[:, :, 0:128] = odd[:, 15 : 15 + pairs, :].astype(jnp.bfloat16)
    empty = jnp.zeros((pairs, 384), jnp.bfloat16)
    lhs = jnp.concatenate(
        [
            jnp.concatenate(
                [
                    empty if 2 * i + a < 1 else taps[2 * i + a - 1]
                    for i in range(rows // 2)
                ],
                axis=0,
            )
            for a in range(3)
        ],
        axis=1,
    )
    pre = dot(lhs, weight2[...].reshape(1152, 256))
    gate = jax.nn.sigmoid(pre)
    value = pre * gate
    features[...] = value.astype(jnp.bfloat16).reshape(features.shape)
    slope2[...] = (gate + value * (1.0 - gate)).reshape(slope2.shape)


def encode(image, halo, weight1, weight2):
    rows, pairs = image.shape[0] // 2, image.shape[1]
    bf16, f32 = jnp.bfloat16, jnp.float32
    return pl.pallas_call(
        encode_kernel,
        out_shape=[
            jax.ShapeDtypeStruct((rows, pairs, 384), bf16),
            jax.ShapeDtypeStruct((rows, pairs, 256), f32),
            jax.ShapeDtypeStruct((rows // 2, pairs, 256), bf16),
            jax.ShapeDtypeStruct((rows // 2, pairs, 256), f32),
        ],
        in_specs=[VMEM] * 4,
        out_specs=[VMEM] * 4,
        scratch_shapes=[pltpu.VMEM((rows, pairs + 16, 128), f32)],
        compiler_params=params(56),
        cost_estimate=LIGHT,
        name="encode",
    )(image, halo, weight1, weight2)


def widen(wide, left, middle, right):
    width = middle.shape[1]
    wide[:, 0:48, :] = left[...]
    wide[:, 48 : 48 + width, :] = middle[...]
    wide[:, 48 + width : 96 + width, :] = right[...]


def decode_kernel(
    chips,
    block,
    place,
    left,
    features,
    right,
    weight,
    taps,
    labels,
    up,
    skip,
    classes,
    logits,
    gradient,
    mine,
    theirs,
    context,
    pooled,
    grad_decoder,
    out_term,
    wide,
    total,
    turned,
):
    rows, width = features.shape[0], features.shape[1]
    step = pl.program_id(0)

    @pl.when(step == 0)
    def _():
        widen(wide, left, features, right)
        total[...] = jnp.zeros_like(total)

    for a in range(TAPS):

        @pl.when(step == a)
        def _(a=a):
            low, high = max(0, 3 - a), min(rows, rows + 3 - a)
            lhs = jnp.concatenate(
                [
                    wide[
                        low + a - 3 : high + a - 3,
                        b * COLUMN_SPREAD : b * COLUMN_SPREAD + width,
                        :,
                    ].reshape((high - low) * width, 256)
                    for b in range(TAPS)
                ],
                axis=1,
            )
            total[low * width : high * width, :] += dot(lhs, weight[0])

    @pl.when(step == TAPS - 1)
    def _():
        pixels = rows * width
        pre = total[...]
        gate = jax.nn.sigmoid(pre)
        value = pre * gate
        total[...] = gate + value * (1.0 - gate)
        mixed = features[...].reshape(pixels, 256).astype(jnp.float32) + value
        mixed = mixed.astype(jnp.bfloat16)
        context[...] = mixed
        coarse = dot(mixed, up[...])
        pool = jnp.zeros((pixels, 128), jnp.float32)
        outer = jnp.zeros((K, 128), jnp.float32)
        kinds = lax.broadcasted_iota(jnp.int32, (K, pixels), 0).astype(jnp.float32)
        source, place_at = [lax.broadcasted_iota(jnp.int32, (256, 256), n) for n in range(2)]
        split = (source == 2 * (place_at & 127) + (place_at >> 7)).astype(jnp.bfloat16)
        parted = dot(labels[...].astype(jnp.float32).astype(jnp.bfloat16), split)
        for p in range(2):
            for q in range(2):
                fine = jnp.concatenate(
                    [taps[2 * i + q, :, 128 + 128 * p : 256 + 128 * p] for i in range(rows)],
                    axis=0,
                )
                pre = dot(fine, skip[...]) + coarse
                gate = jax.nn.sigmoid(pre)
                value = pre * gate
                decoded = value.astype(jnp.bfloat16)
                scores = dot(classes[...], decoded, NT)
                logits[p, q] = scores
                wanted = jnp.concatenate(
                    [
                        parted[2 * i + q : 2 * i + q + 1, p * 128 : (p + 1) * 128]
                        for i in range(rows)
                    ],
                    axis=1,
                )
                target = (kinds == wanted).astype(jnp.float32)
                grad = (jax.nn.sigmoid(scores) - target).astype(jnp.bfloat16)
                outer += dot(grad, decoded)
                back = dot(grad, classes[...], TN) * (gate + value * (1.0 - gate))
                back = back.astype(jnp.bfloat16)
                grad_decoder[p, q] = back
                pool += back.astype(jnp.float32)
        out_term[...] = outer
        small = pool.astype(jnp.bfloat16)
        pooled[...] = small
        result = dot(small, up[...], NT) * total[...]
        gradient[...] = result.astype(jnp.bfloat16).reshape(gradient.shape)
        for i in range(rows):
            line = result[i * width : (i + 1) * width].T.astype(jnp.bfloat16)
            turned[:, i] = line.reshape(2 * chips, block, width)
        chip, core = place[0] >> 1, place[0] & 1
        for mask in range(chips):
            mine[mask] = turned[2 * (chip ^ mask) + core]
            theirs[mask] = turned[2 * (chip ^ mask) + 1 - core]


def whole(shape):
    return pl.BlockSpec(shape, lambda n: (0,) * len(shape))


def decode(place, left, features, right, weight, taps, labels, up, skip, classes, chips):
    rows, width = features.shape[0], features.shape[1]
    pixels = rows * width
    block = 128 // chips
    bf16, f32 = jnp.bfloat16, jnp.float32
    operands = (left, features, right, weight, taps, labels, up, skip, classes)
    specs = [whole(x.shape) for x in operands]
    specs[3] = pl.BlockSpec((1, *weight.shape[1:]), lambda n: (n, 0, 0))
    outs = [
        jax.ShapeDtypeStruct((2, 2, K, pixels), f32),
        jax.ShapeDtypeStruct((rows, width, 256), bf16),
        jax.ShapeDtypeStruct((chips, rows, block, width), bf16),
        jax.ShapeDtypeStruct((chips, rows, block, width), bf16),
        jax.ShapeDtypeStruct((pixels, 256), bf16),
        jax.ShapeDtypeStruct((pixels, 128), bf16),
        jax.ShapeDtypeStruct((2, 2, pixels, 128), bf16),
        jax.ShapeDtypeStruct((K, 128), f32),
    ]
    return pl.pallas_call(
        functools.partial(decode_kernel, chips, block),
        out_shape=outs,
        grid=(TAPS,),
        in_specs=[SMEM, *specs],
        out_specs=[whole(x.shape) for x in outs],
        scratch_shapes=[
            pltpu.VMEM((rows, width + 96, 256), bf16),
            pltpu.VMEM((pixels, 256), f32),
            pltpu.VMEM((2 * chips, rows, block, width), bf16),
        ],
        compiler_params=params(56),
        cost_estimate=LIGHT,
        name="decode",
    )(place, *operands)


def back_kernel(
    left,
    gradient,
    right,
    weight,
    pooled,
    up,
    slope2,
    taps,
    grad_decoder,
    skip,
    weight2,
    context,
    partial,
    edge,
    term2,
    up_term,
    skip_term,
    wide,
    total,
    before,
):
    rows, width = gradient.shape[0], gradient.shape[1]
    pixels = rows * width
    step = pl.program_id(0)

    @pl.when(step == 0)
    def _():
        widen(wide, left, gradient, right)
        total[...] = dot(pooled[...], up[...], NT)

    for a in range(TAPS):

        @pl.when(step == a)
        def _(a=a):
            low, high = max(0, a - 3), min(rows, rows + a - 3)
            result = None
            for b in range(TAPS):
                at = (6 - b) * COLUMN_SPREAD
                lhs = wide[low - a + 3 : high - a + 3, at : at + width, :]
                lhs = lhs.reshape((high - low) * width, 256)
                one = dot(lhs, weight[0, b * 256 : (b + 1) * 256, :], NT)
                result = one if result is None else result + one
            total[low * width : high * width, :] += result

    @pl.when(step == TAPS - 1)
    def _():
        grad = (total[...] * slope2[...].reshape(pixels, 256)).astype(jnp.bfloat16)
        up_term[...] = dot(context[...], pooled[...], TN)
        backs = []
        for a in range(3):
            first = 1 if a == 0 else 0
            lhs = jnp.concatenate(
                [taps[2 * i + a - 1] for i in range(first, rows)], axis=0
            )
            term2[a] = dot(lhs, grad[first * width :], TN)
            backs.append(dot(grad, weight2[a], NT))
        skips = jnp.zeros((128, 128), jnp.float32)
        for p in range(2):
            for q in range(2):
                fine = jnp.concatenate(
                    [taps[2 * i + q, :, 128 + 128 * p : 256 + 128 * p] for i in range(rows)],
                    axis=0,
                )
                skips += dot(fine, grad_decoder[p, q], TN)
                through = dot(grad_decoder[p, q], skip[...], NT)
                for i in range(rows):
                    partial[2 * i + q, :, p * 128 : (p + 1) * 128] = through[
                        i * width : (i + 1) * width
                    ]
        skip_term[...] = skips
        before[:, width : width + 8, :] = jnp.zeros((2 * rows, 8, 128), jnp.float32)
        for i in range(rows):
            here = slice(i * width, (i + 1) * width)
            even = backs[1][here]
            odd = backs[2][here]
            if i + 1 < rows:
                odd = odd + backs[0][(i + 1) * width : (i + 2) * width]
            for q, line in enumerate((even, odd)):
                before[2 * i + q, 0:width, :] = line[:, 0:128]
                partial[2 * i + q, :, 0:128] += line[:, 128:256]
                partial[2 * i + q, :, 128:256] += (
                    line[:, 256:384] + before[2 * i + q, 1 : width + 1, :]
                )
        edge[...] = before[:, 0:1, :]


def back(left, gradient, right, weight, pooled, up, slope2, taps, grads, skip, weight2, context):
    rows, width = gradient.shape[0], gradient.shape[1]
    pixels = rows * width
    bf16, f32 = jnp.bfloat16, jnp.float32
    operands = (
        left, gradient, right, weight, pooled, up, slope2, taps, grads, skip, weight2, context,
    )
    specs = [whole(x.shape) for x in operands]
    specs[3] = pl.BlockSpec((1, *weight.shape[1:]), lambda n: (n, 0, 0))
    outs = [
        jax.ShapeDtypeStruct((2 * rows, width, 256), f32),
        jax.ShapeDtypeStruct((2 * rows, 1, 128), f32),
        jax.ShapeDtypeStruct((3, 384, 256), f32),
        jax.ShapeDtypeStruct((256, 128), f32),
        jax.ShapeDtypeStruct((128, 128), f32),
    ]
    return pl.pallas_call(
        back_kernel,
        out_shape=outs,
        grid=(TAPS,),
        in_specs=specs,
        out_specs=[whole(x.shape) for x in outs],
        scratch_shapes=[
            pltpu.VMEM((rows, width + 96, 256), bf16),
            pltpu.VMEM((pixels, 256), f32),
            pltpu.VMEM((2 * rows, width + 8, 128), f32),
        ],
        compiler_params=params(56),
        cost_estimate=LIGHT,
        name="back",
    )(*operands)


def finish_kernel(
    partial, returned, slope1, image, halo, term2, up_term, skip_term, out_term, out, packed, shifted_up
):
    rows, width = partial.shape[0], partial.shape[1]
    last = lax.broadcasted_iota(jnp.int32, (rows, width, 128), 1) == width - 1
    even = partial[:, :, 0:128]
    odd = partial[:, :, 128:256] + jnp.where(last, returned[...], 0.0)
    for i in range(rows):
        out[i, pl.ds(0, width, stride=2), :] = even[i]
        out[i, pl.ds(1, width, stride=2), :] = odd[i]
    even = even * slope1[:, :, 0:128]
    odd = (odd * slope1[:, :, 128:256]).astype(jnp.bfloat16)
    shifted_up[:, 0:16, :] = jnp.zeros((rows, 16, 128), jnp.float32)
    shifted_up[:, width + 8 : width + 16, :] = jnp.zeros((rows, 8, 128), jnp.float32)
    shifted_up[:, 15 : 15 + width, :] = even
    even = even.astype(jnp.bfloat16)
    moved = shifted_up[...].astype(jnp.bfloat16)
    rhs = jnp.concatenate([odd, even, moved[:, 16:]], axis=2)
    for a in range(3):
        first = 1 if a == 0 else 0
        lines = [2 * i + a - 1 for i in range(first, rows)]
        lhs = jnp.concatenate([image[n] for n in lines], axis=0)
        result = dot(lhs, rhs[first:].reshape((rows - first) * width, 384), TN)
        side = jnp.concatenate([halo[n] for n in lines], axis=0)
        outer = dot(side, moved[first:, 0:16].reshape((rows - first) * 16, 128), TN)
        at = 192 * a
        packed[at : at + 64, :] = (
            result[192:256, 256:384] + outer[192:256] + result[64:128, 0:128]
        )
        packed[at + 64 : at + 128, :] = result[0:64, 128:256] + result[128:192, 0:128]
        packed[at + 128 : at + 192, :] = result[64:128, 128:256] + result[192:256, 0:128]
        for n in range(2):
            at = 576 + 384 * (2 * a + n)
            packed[at : at + 384, :] = term2[a, :, n * 128 : (n + 1) * 128]
    packed[2880:3136, :] = up_term[...]
    packed[3136:3264, :] = skip_term[...]
    packed[3264:3272, :] = out_term[...]
    packed[3272:, :] = jnp.zeros((packed.shape[0] - 3272, 128), jnp.float32)


def finish(partial, returned, slope1, image, halo, terms, packed_rows):
    rows, width = partial.shape[0], partial.shape[1]
    f32 = jnp.float32
    return pl.pallas_call(
        finish_kernel,
        out_shape=[
            jax.ShapeDtypeStruct((rows, 2 * width, 128), f32),
            jax.ShapeDtypeStruct((packed_rows, 128), f32),
        ],
        in_specs=[VMEM] * 9,
        out_specs=[VMEM] * 2,
        scratch_shapes=[pltpu.VMEM((rows, width + 16, 128), f32)],
        compiler_params=params(56),
        cost_estimate=LIGHT,
        name="finish",
    )(partial, returned, slope1, image, halo, *terms)


def small_kernel(order, chips, place, *refs):
    sources, packed = refs[:4], refs[-1]
    conv1, conv2, up, skip, out = refs[4:-1]
    tile, half = place[0], place[1]
    chip, core = tile >> 1, tile & 1
    depth = packed.shape[0] // (4 * chips)
    dims = len(order)
    entries, height = sources[0].shape[0], sources[0].shape[1]
    for s in range(4):
        for i in range(entries):
            index = i + entries * (s % 2)
            mask = sum(1 << d for q, d in enumerate(order) if (index >> q) & 1)
            whose = chip ^ (mask % chips)
            at = core ^ (s // 2)
            for d in range(dims - 1):
                at = 2 * at + ((whose >> d) & 1)
            at = 2 * at + (half ^ (mask // chips))
            packed[pl.ds(pl.multiple_of(at * depth, depth), depth), :] = sources[s][
                i, height - depth :, :
            ].astype(jnp.float32)
    for a in range(3):
        conv1[a] = packed[192 * a : 192 * a + 192, :]
        for n in range(2):
            at = 576 + 384 * (2 * a + n)
            conv2[a, :, n * 128 : (n + 1) * 128] = packed[at : at + 384, :]
    up[...] = packed[2880:3136, :]
    skip[...] = packed[3136:3264, :]
    out[...] = packed[3264:3272, :]


def unpack_small(place, sources, order, chips, packed_rows):
    f32 = jnp.float32
    shapes = [(3, 192, 128), (3, 384, 256), (256, 128), (128, 128), (K, 128)]
    return pl.pallas_call(
        functools.partial(small_kernel, order, chips),
        out_shape=[jax.ShapeDtypeStruct(shape, f32) for shape in shapes],
        in_specs=[SMEM] + [VMEM] * 4,
        out_specs=[VMEM] * 5,
        scratch_shapes=[pltpu.VMEM((packed_rows, 128), f32)],
        compiler_params=params(56),
        cost_estimate=LIGHT,
        name="small_out",
    )(place, *sources)


def moved(block, distance):
    tiles = lax.axis_size("tile")
    route = [(i, i + distance) for i in range(tiles) if 0 <= i + distance < tiles]
    return lax.ppermute(block, "tile", route)


def edges(value):
    return moved(value[:, -48:], 1), moved(value[:, :48], -1)


def body(
    scan_pixels,
    labels,
    conv1_weight,
    conv2_weight,
    context_weight,
    up_weight,
    skip_weight,
    class_weight,
):
    bf16 = jnp.bfloat16
    tiles = lax.axis_size("tile")
    chips = tiles // 2
    t, _, half = position()
    place = jnp.stack([t, half]).astype(jnp.int32)
    lines, line_pairs, _ = scan_pixels[0].shape
    rows, width = lines // 4, line_pairs // 2
    corner = moved(scan_pixels[0, :, -2:, :].reshape(lines, 1, 256), 1)
    halo = jnp.concatenate([jnp.zeros((lines, 15, 256), bf16), corner], axis=1)
    image = scan_pixels[0].reshape(lines, width, 256)
    taps, slope1, features, slope2 = encode(image, halo, conv1_weight, conv2_weight)
    left, right = edges(features)
    logits, gradient, mine, theirs, context, pooled, grads, out_term = decode(
        place, left, features, right, context_weight, taps, labels[0],
        up_weight, skip_weight, class_weight, chips,
    )
    messages = pack(place, features, mine, flip(theirs, 1, 0))
    gradient, messages = lax.optimization_barrier((gradient, messages))
    own = [
        part if m == 0 else flip(part, 2 * (m % chips), m // chips)
        for m, part in enumerate(messages)
    ]
    left, right = edges(gradient)
    partial, edge, conv2_term, up_term, skip_term = back(
        left, gradient, right, context_weight, pooled, up_weight, slope2, taps, grads,
        skip_weight, conv2_weight, context,
    )
    returned = moved(edge, -1)
    partial, own = lax.optimization_barrier((partial, own))
    other = [flip(part, 1, 0) for part in own]
    packed_rows = -(-3272 // (64 * chips)) * 64 * chips
    grad_features, packed = finish(
        partial, returned, slope1, image, halo,
        (conv2_term, up_term, skip_term, out_term), packed_rows,
    )
    logits = logits.reshape(2, 2, K, rows, width).transpose(2, 3, 1, 4, 0)
    logits = logits.reshape(1, K, 2 * rows, 2 * width)
    grad_features = grad_features[None]
    scale = 1.0 / (lax.axis_size("dp") * tiles * 4 * rows * width)
    block = mine.shape[2]
    context_term = wgrad(place, own, other, chips, rows, width, block)
    folded, context_term = fold_small(packed, chips, context_term)
    grad_context, small, (logits, grad_features) = sum_and_share(
        context_term, folded, place, chips, block, scale, (logits, grad_features), packed_rows
    )
    return (
        logits,
        grad_features,
        small[0],
        small[1],
        grad_context.reshape(context_weight.shape),
        small[2],
        small[3],
        small[4],
    )


def solution(mesh):
    in_specs = (P("dp", None, "tile", None), P("dp", None, "tile"), P(), P(), P(), P(), P(), P())
    out_specs = (
        P("dp", None, None, "tile"),
        P("dp", None, "tile", None),
        P(),
        P(),
        P(),
        P(),
        P(),
        P(),
    )
    return jax.shard_map(body, mesh=mesh, in_specs=in_specs, out_specs=out_specs, check_vma=False)
```

time: 443 us -> 188 us (0.42)
  waiting for transfers between devices: 217 us -> 43.4 us
  Pallas kernels: 0 us -> 57.6 us
  local copies, waits for them, and re-layouts: 68.4 us -> 15.1 us
  blocking collectives: 47 us -> 0 us
  starting transfers between devices: 23.2 us -> 67.6 us
  matrix products: 36.6 us -> 0 us
  other arithmetic: 30.9 us -> 2.04 us
  between operations: 15.5 us -> 1.28 us
    psum x1 -> x0, waiting for transfers between devices: 214 us -> none  [body(): lax.psum((conv1_term, conv2_term, context_term, up_term, skip_term, out_t...]
    pallas_call x0 -> x8, Pallas kernels: none -> 57.6 us  [the longest x1 11.8 us: unpack(): pl.pallas_call(functools.partial(unpack_kernel, orders, bounds, chips, bl...]
    psum x1 -> x0, blocking collectives: 47 us -> none  [body(): lax.psum((conv1_term, conv2_term, context_term, up_term, skip_term, out_t...]
    ppermute x7 -> x45, starting transfers between devices: 23.1 us -> 67.6 us  [the longest x39 54.7 us: flip(): return lax.ppermute(value, BOTH, route)]
    ppermute x7 -> x45, waiting for transfers between devices: 2.33 us -> 43.4 us  [the longest x39 42.6 us: flip(): return lax.ppermute(value, BOTH, route)]
    dot_general x44 -> x0, matrix products: 36.3 us -> none  [product(): jnp.einsum(pattern, lhs_array, rhs_array, preferred_element_type=jnp.floa...]
    concatenate x12 -> x1, local copies, waits for them, and re-layouts: 31.7 us -> 0.71 us  [body(): halo = jnp.concatenate([jnp.zeros((lines, 15, 256), bf16), corner], axis=1)]
    unnamed x112 -> x62, local copies, waits for them, and re-layouts: 29 us -> 6.5 us
  transfers between devices with their start and end apart: 8 -> 45, of which waited for: 3 -> 16; matrix products, arithmetic and copies ran while one was open for 4% -> 5% of each run, Pallas kernels for 0% -> 14%
where the time goes in v1:
time: 188 us; the launch traced here: 187 us
  starting transfers between devices  67.6 us (36%)
  Pallas kernels  57.6 us (31%)
  waiting for transfers between devices  43.4 us (23%)
  local copies, waits for them, and re-layouts  15.1 us (8%)
  other arithmetic  2.04 us (1%)
    ppermute x39, starting transfers between devices, flip(): return lax.ppermute(value, BOTH, route)  54.7 us
    ppermute x39, waiting for transfers between devices, flip(): return lax.ppermute(value, BOTH, route)  42.6 us
    ppermute x6, starting transfers between devices, moved(): return lax.ppermute(block, 'tile', route)  12.9 us
    pallas_call x1, Pallas kernels, unpack(): pl.pallas_call(functools.partial(unpack_kernel, orders, bounds, chips, bl...  11.8 us
    pallas_call x1, Pallas kernels, back(): pl.pallas_call(back_kernel, out_shape=outs, grid=(TAPS,), in_specs=specs,...  11.7 us
    pallas_call x1, Pallas kernels, decode(): pl.pallas_call(functools.partial(decode_kernel, chips, block), out_shape=...  11.4 us
    pallas_call x1, Pallas kernels, wgrad(): pl.pallas_call(functools.partial(wgrad_kernel, chips, rows, width, block)...  6.73 us
    unnamed x62, local copies, waits for them, and re-layouts  6.5 us
  transfers between devices with their start and end apart: 45, of which 16 were waited for; matrix products, arithmetic and copies ran while one was open for 5% of the time, Pallas kernels for 14%

profile of v1, /device:TPU:0, one launch (start us, length us, event | category | flops | bytes accessed | tf_op | source)
XLA Modules:
  0.0 186.9 jit_solution(17841519176776836603)
XLA Ops:
  1.4 2.4 %collective-permute-start = (bf16[20,1,256]{2,1,0:T(2,128)(2,1)S(1)}, bf16[20,1,256]{2,1,0:T(2,128)(2,1)S(1)}, u32[]{:S(2)}, u32[]{:S(2)}) collective-permute-start(bf16[20,1,256]{2,1,0:T(2,128)(2,1)S(1)} %reshape_squeeze.8), channel_id=1, source_target_pairs={{0,4},{4,8},{8,12},{12,16},{16,20},{20,24},{24,28},{1,5},{5,9},{9,... | collective-permute-start | bytes 30728 | tf_op jit(solution)/shard_map/ppermute | solution.py:732
  3.8 3.2 %reshape_squeeze.6.image = bf16[20,128,256]{2,1,0:T(8,128)(2,1)} reshape(bf16[1,20,256,128]{3,2,1,0:T(8,128)(2,1)} %param.8) | data formatting | bytes 2621440 | tf_op jit(solution)/shard_map/reshape;squeeze | solution.py:758
  7.7 5.2 %encode.1 = (bf16[10,128,384]{2,1,0:T(8,128)(2,1)}, f32[10,128,256]{2,1,0:T(8,128)}, bf16[5,128,256]{2,1,0:T(8,128)(2,1)}, f32[5,128,256]{2,1,0:T(8,128)}) custom-call(bf16[20,128,256]{2,1,0:T(8,128)(2,1)} %reshape_squeeze.6.image, bf16[20,16,256]{2,1,0:T(8,128)(2,1)} %concatenate.38.halo, bf16[3,192,128]{2,1,0:T(8,128)(2,1)} %weight1.1, ...), custom_call_target="tpu_custom_call" | custom-call | flops 1000 | bytes 1000 | tf_op jit(solution)/shard_map/encode/pallas_call | solution.py:335
  13.9 4.5 %collective-permute-start.1 = (bf16[5,48,256]{2,1,0:T(8,128)(2,1)S(1)}, bf16[5,48,256]{2,1,0:T(8,128)(2,1)S(1)}, u32[]{:S(2)}, u32[]{:S(2)}) collective-permute-start(bf16[5,48,256]{2,1,0:T(8,128)(2,1)S(1)} %get-tuple-element.151), channel_id=1, source_target_pairs={{0,4},{4,8},{8,12},{12,16},{16,20},{20,24},{24,28},{1,5},{5,9},{9,... | collective-permute-start | bytes 368648 | tf_op jit(solution)/shard_map/ppermute | solution.py:732
  22.3 11.4 %decode.1 = (f32[2,2,8,640]{3,2,1,0:T(8,128)}, bf16[5,128,256]{2,1,0:T(8,128)(2,1)}, bf16[4,5,32,128]{3,2,1,0:T(8,128)(2,1)}, bf16[4,5,32,128]{3,2,1,0:T(8,128)(...) custom-call(s32[2]{0:T(128)} %pad_add_fusion.place, ...), custom_call_target="tpu_custom_call" | custom-call | flops 1000 | bytes 1000 | tf_op jit(solution)/shard_map/decode/pallas_call | solution.py:489
  33.6 3.0 %collective-permute-start.3 = (bf16[4,5,32,128]{3,2,1,0:T(8,128)(2,1)}, bf16[4,5,32,128]{3,2,1,0:T(8,128)(2,1)S(1)}, u32[]{:S(2)}, u32[]{:S(2)}) collective-permute-start(bf16[4,5,32,128]{3,2,1,0:T(8,128)(2,1)} %get-tuple-element.76), channel_id=1, source_target_pairs={{0,4},{1,5},{2,6},{3,7},{4,0},{5,1},{6,2},{7,3},{8,12},{9,13},{10,... | collective-permute-start | bytes 491528 | tf_op jit(solution)/shard_map/ppermute | solution.py:32
  38.5 2.5 %pack.1 = (bf16[960,128]{1,0:T(8,128)(2,1)}, bf16[960,128]{1,0:T(8,128)(2,1)}, bf16[960,128]{1,0:T(8,128)(2,1)}, bf16[960,128]{1,0:T(8,128)(2,1)}, bf16[960,128]...) custom-call(s32[2]{0:T(128)} %pad_add_fusion.place, ...), custom_call_target="tpu_custom_call" | custom-call | flops 1000 | bytes 1000 | tf_op jit(solution)/shard_map/pack/pallas_call | solution.py:135
  41.0 4.3 %collective-permute-start.10 = (bf16[960,128]{1,0:T(8,128)(2,1)}, bf16[960,128]{1,0:T(8,128)(2,1)S(1)}, u32[]{:S(2)}, u32[]{:S(2)}) collective-permute-start(bf16[960,128]{1,0:T(8,128)(2,1)} %get-tuple-element.96), channel_id=1, source_target_pairs={{0,9},{1,8},{2,11},{3,10},{4,13},{5,12},{6,15},{7,14},{8,1},{9,0},... | collective-permute-start | bytes 737288 | tf_op jit(solution)/shard_map/ppermute | solution.py:32
  46.3 2.0 %collective-permute-start.4 = (bf16[5,48,256]{2,1,0:T(8,128)(2,1)S(1)}, bf16[5,48,256]{2,1,0:T(8,128)(2,1)S(1)}, u32[]{:S(2)}, u32[]{:S(2)}) collective-permute-start(bf16[5,48,256]{2,1,0:T(8,128)(2,1)S(1)} %get-tuple-element.149), channel_id=1, source_target_pairs={{0,4},{4,8},{8,12},{12,16},{16,20},{20,24},{24,28},{1,5},{5,9},{9,... | collective-permute-start | bytes 368648 | tf_op jit(solution)/shard_map/ppermute | solution.py:732
  49.8 4.4 %collective-permute-start.12 = (bf16[960,128]{1,0:T(8,128)(2,1)}, bf16[960,128]{1,0:T(8,128)(2,1)S(1)}, u32[]{:S(2)}, u32[]{:S(2)}) collective-permute-start(bf16[960,128]{1,0:T(8,128)(2,1)} %get-tuple-element.98), channel_id=1, source_target_pairs={{0,25},{1,24},{2,27},{3,26},{4,29},{5,28},{6,31},{7,30},{8,17},{9,... | collective-permute-start | bytes 737288 | tf_op jit(solution)/shard_map/ppermute | solution.py:32
  54.2 3.2 %collective-permute-start.6 = (bf16[960,128]{1,0:T(8,128)(2,1)}, bf16[960,128]{1,0:T(8,128)(2,1)S(1)}, u32[]{:S(2)}, u32[]{:S(2)}) collective-permute-start(bf16[960,128]{1,0:T(8,128)(2,1)} %get-tuple-element.92), channel_id=1, source_target_pairs={{0,8},{1,9},{2,10},{3,11},{4,12},{5,13},{6,14},{7,15},{8,0},{9,1},... | collective-permute-start | bytes 737288 | tf_op jit(solution)/shard_map/ppermute | solution.py:32
  57.5 5.6 %collective-permute-start.7 = (bf16[960,128]{1,0:T(8,128)(2,1)}, bf16[960,128]{1,0:T(8,128)(2,1)S(1)}, u32[]{:S(2)}, u32[]{:S(2)}) collective-permute-start(bf16[960,128]{1,0:T(8,128)(2,1)} %get-tuple-element.93), channel_id=1, source_target_pairs={{0,16},{1,17},{2,18},{3,19},{4,20},{5,21},{6,22},{7,23},{8,24},{9,... | collective-permute-start | bytes 737288 | tf_op jit(solution)/shard_map/ppermute | solution.py:32
  63.1 2.3 %collective-permute-start.9 = (bf16[960,128]{1,0:T(8,128)(2,1)}, bf16[960,128]{1,0:T(8,128)(2,1)S(1)}, u32[]{:S(2)}, u32[]{:S(2)}) collective-permute-start(bf16[960,128]{1,0:T(8,128)(2,1)} %get-tuple-element.95), channel_id=1, source_target_pairs={{0,1},{1,0},{2,3},{3,2},{4,5},{5,4},{6,7},{7,6},{8,9},{9,8},{10,11... | collective-permute-start | bytes 737288 | tf_op jit(solution)/shard_map/ppermute | solution.py:32
  65.4 11.7 %back.1 = (f32[10,128,256]{2,1,0:T(8,128)}, f32[10,1,128]{2,1,0:T(1,128)}, f32[3,384,256]{2,1,0:T(8,128)}, f32[256,128]{1,0:T(8,128)}, f32[128,128]{1,0:T(8,128)}) custom-call(bf16[5,48,256]{2,1,0:T(8,128)(2,1)} %copy-done.23, bf16[5,128,256]{2,1,0:T(8,128)(2,1)} %get-tuple-element.85.gradient, bf16[5,48,256]{2,1,0:T(8,128)(2,1)} %copy-done.24, ...), custom_call_target="tpu_custom_call" | custom-call | flops 1000 | bytes 1000 | tf_op jit(solution)/shard_map/back/pallas_call | solution.py:609
  78.5 3.0 %collective-permute-start.15 = (bf16[960,128]{1,0:T(8,128)(2,1)S(1)}, bf16[960,128]{1,0:T(8,128)(2,1)S(1)}, u32[]{:S(2)}, u32[]{:S(2)}) collective-permute-start(bf16[960,128]{1,0:T(8,128)(2,1)S(1)} %copy-done.6), channel_id=1, source_target_pairs={{0,4},{1,5},{2,6},{3,7},{4,0},{5,1},{6,2},{7,3},{8,12},{9,13},{10,... | collective-permute-start | bytes 737288 | tf_op jit(solution)/shard_map/ppermute | solution.py:32
  82.8 5.1 %finish.1 = (f32[10,256,128]{2,1,0:T(8,128)}, f32[3328,128]{1,0:T(8,128)}) custom-call(f32[10,128,256]{2,1,0:T(8,128)} %get-tuple-element.99.partial, f32[10,1,128]{2,1,0:T(1,128)} %copy-done.29, f32[10,128,256]{2,1,0:T(8,128)} %get-tuple-element.101.slope1, bf16[20,128,256]{2,1,0:T(8,128)(2,1)} %reshape_squeeze.6.image, ...), custom_call_target="tpu_custom_call" | custom-call | flops 1000 | bytes 1000 | tf_op jit(solution)/shard_map/finish/pallas_call | solution.py:669
  89.1 2.4 %collective-permute-start.14 = (bf16[1664,128]{1,0:T(8,128)(2,1)S(1)}, bf16[1664,128]{1,0:T(8,128)(2,1)S(1)}, u32[]{:S(2)}, u32[]{:S(2)}) collective-permute-start(bf16[1664,128]{1,0:T(8,128)(2,1)S(1)} %fusion), channel_id=1, source_target_pairs={{0,4},{1,5},{2,6},{3,7},{4,0},{5,1},{6,2},{7,3},{8,12},{9,13},{10,... | collective-permute-start | bytes 1277960 | tf_op jit(solution)/shard_map/ppermute | solution.py:32
  95.9 6.7 %context_term.1 = bf16[1568,128]{1,0:T(8,128)(2,1)} custom-call(s32[2]{0:T(128)} %pad_add_fusion.place, bf16[960,128]{1,0:T(8,128)(2,1)} %get-tuple-element.107.refs_0_, bf16[960,128]{1,0:T(8,128)(2,1)} %copy-done.10, bf16[960,128]{1,0:T(8,128)(2,1)} %copy-done.11, bf16[960,128]{1,0:T(8,128)(2,1)} %copy-done.12, bf16[960,128]{1,0:T(8,128)(2,1)} %copy-done.13, ...), custom_call_target="tpu_custom_call" | custom-call | flops 1000 | bytes 1000 | tf_op jit(solution)/shard_map/context_term/pallas_call | solution.py:102
  103.0 7.1 %collective-permute-done.26 = bf16[832,128]{1,0:T(8,128)(2,1)S(1)} collective-permute-done((bf16[832,128]{1,0:T(8,128)(2,1)S(1)}, bf16[832,128]{1,0:T(8,128)(2,1)S(1)}, u32[]{:S(2)}, u32[]{:S(2)}) %collective-permute-start.26) | collective-permute-done | bytes 213024 | tf_op jit(solution)/shard_map/ppermute | solution.py:32
  110.6 4.3 %collective-permute-done.27 = bf16[416,128]{1,0:T(8,128)(2,1)S(1)} collective-permute-done((bf16[416,128]{1,0:T(8,128)(2,1)S(1)}, bf16[416,128]{1,0:T(8,128)(2,1)S(1)}, u32[]{:S(2)}, u32[]{:S(2)}) %collective-permute-start.27) | collective-permute-done | bytes 106528 | tf_op jit(solution)/shard_map/ppermute | solution.py:32
  115.6 3.7 %collective-permute-start.23 = (bf16[512,128]{1,0:T(8,128)(2,1)S(1)}, bf16[512,128]{1,0:T(8,128)(2,1)S(1)}, u32[]{:S(2)}, u32[]{:S(2)}) collective-permute-start(bf16[512,128]{1,0:T(8,128)(2,1)S(1)} %get-tuple-element.147), channel_id=1, source_target_pairs={{0,3},{1,2},{2,1},{3,0},{4,7},{5,6},{6,5},{7,4},{8,11},{9,10},{10,... | collective-permute-start | bytes 393224 | tf_op jit(solution)/shard_map/ppermute | solution.py:32
  119.4 3.6 %collective-permute-start.25 = (bf16[544,128]{1,0:T(8,128)(2,1)S(1)}, bf16[544,128]{1,0:T(8,128)(2,1)S(1)}, u32[]{:S(2)}, u32[]{:S(2)}) collective-permute-start(bf16[544,128]{1,0:T(8,128)(2,1)S(1)} %slice.31), channel_id=1, source_target_pairs={{0,3},{1,2},{2,1},{3,0},{4,7},{5,6},{6,5},{7,4},{8,11},{9,10},{10,... | collective-permute-start | bytes 417800 | tf_op jit(solution)/shard_map/ppermute | solution.py:32
  125.2 2.3 %collective-permute-done.24 = bf16[512,128]{1,0:T(8,128)(2,1)S(1)} collective-permute-done((bf16[512,128]{1,0:T(8,128)(2,1)S(1)}, bf16[512,128]{1,0:T(8,128)(2,1)S(1)}, u32[]{:S(2)}, u32[]{:S(2)}) %collective-permute-start.24) | collective-permute-done | bytes 131104 | tf_op jit(solution)/shard_map/ppermute | solution.py:32
  127.5 1.6 collective-permute-done.25
  129.8 7.5 %collective-permute-start.32 = (bf16[1,752,128]{2,1,0:T(8,128)(2,1)S(1)}, bf16[1,752,128]{2,1,0:T(8,128)(2,1)S(1)}, u32[]{:S(2)}, u32[]{:S(2)}) collective-permute-start(bf16[1,752,128]{2,1,0:T(8,128)(2,1)S(1)} %fusion.1), channel_id=1, source_target_pairs={{0,1},{1,0},{2,3},{3,2},{4,5},{5,4},{6,7},{7,6},{8,9},{9,8},{10,11... | collective-permute-start | bytes 577544 | tf_op jit(solution)/shard_map/ppermute | solution.py:32
  138.4 4.0 %collective-permute-done.30 = bf16[1,512,128]{2,1,0:T(8,128)(2,1)S(1)} collective-permute-done((bf16[1,512,128]{2,1,0:T(8,128)(2,1)S(1)}, bf16[1,512,128]{2,1,0:T(8,128)(2,1)S(1)}, u32[]{:S(2)}, u32[]{:S(2)}) %collective-permute-start.30) | collective-permute-done | bytes 131104 | tf_op jit(solution)/shard_map/ppermute | solution.py:32
  143.0 1.6 collective-permute-start.35
  145.2 5.9 %collective-permute-done.34 = bf16[2,512,128]{2,1,0:T(8,128)(2,1)S(1)} collective-permute-done((bf16[2,512,128]{2,1,0:T(8,128)(2,1)S(1)}, bf16[2,512,128]{2,1,0:T(8,128)(2,1)S(1)}, u32[]{:S(2)}, u32[]{:S(2)}) %collective-permute-start.34) | collective-permute-done | bytes 262176 | tf_op jit(solution)/shard_map/ppermute | solution.py:32
  153.9 2.8 %collective-permute-start.39 = (bf16[4,512,128]{2,1,0:T(8,128)(2,1)}, bf16[4,512,128]{2,1,0:T(8,128)(2,1)}, u32[]{:S(2)}, u32[]{:S(2)}) collective-permute-start(bf16[4,512,128]{2,1,0:T(8,128)(2,1)} %pad_maximum_fusion.1.refs_0_), channel_id=1, source_target_pairs={{0,1},{1,0},{2,3},{3,2},{4,5},{5,4},{6,7},{7,6},{8,9},{9,8},{10,11... | collective-permute-start | bytes 1572872 | tf_op jit(solution)/shard_map/ppermute | solution.py:32
  156.7 11.0 %collective-permute-done.36.refs_1_.refs_9_ = bf16[4,752,128]{2,1,0:T(8,128)(2,1)S(1)} collective-permute-done((bf16[4,752,128]{2,1,0:T(8,128)(2,1)S(1)}, bf16[4,752,128]{2,1,0:T(8,128)(2,1)S(1)}, u32[]{:S(2)}, u32[]{:S(2)}) %collective-permute-start.36) | collective-permute-done | bytes 770080 | tf_op jit(solution)/shard_map/ppermute | solution.py:32
  171.8 3.2 %small_out.1 = (f32[3,192,128]{2,1,0:T(8,128)}, f32[3,384,256]{2,1,0:T(8,128)}, f32[256,128]{1,0:T(8,128)}, f32[128,128]{1,0:T(8,128)}, f32[8,128]{1,0:T(8,128)}) custom-call(s32[2]{0:T(128)} %pad_add_fusion.place, bf16[4,752,128]{2,1,0:T(8,128)(2,1)} %copy-done, bf16[4,752,128]{2,1,0:T(8,128)(2,1)} %copy-done.2, bf16[4,752,128]{2,1,0:T(8,128)(2,1)} %copy-done.3, ...), custom_call_target="tpu_custom_call" | custom-call | flops 1000 | bytes 1000 | tf_op jit(solution)/shard_map/small_out/pallas_call | solution.py:717
  175.0 11.8 %context_out.1 = f32[49,256,256]{2,1,0:T(8,128)} custom-call(s32[2]{0:T(128)} %pad_add_fusion.place, bf16[4,512,128]{2,1,0:T(8,128)(2,1)} %pad_maximum_fusion.1.refs_0_, bf16[4,512,128]{2,1,0:T(8,128)(2,1)} %collective-permute-done.39.refs_1_, bf16[4,512,128]{2,1,0:T(8,128)(2,1)} %collective-permute-done.40.refs_2_, ...), custom_call_target="tpu_custom_call" | custom-call | flops 1000 | bytes 1000 | tf_op jit(solution)/shard_map/context_out/pallas_call | solution.py:198
  (156 shorter events, 32.2 us)
Async XLA Ops:
  13.9 7.1 %collective-permute-start.1 = (bf16[5,48,256]{2,1,0:T(8,128)(2,1)S(1)}, bf16[5,48,256]{2,1,0:T(8,128)(2,1)S(1)}, u32[]{:S(2)}, u32[]{:S(2)}) collective-permute-start(bf16[5,48,256]{2,1,0:T(8,128)(2,1)S(1)} %get-tuple-element.151), channel_id=1, source_target_pairs={{0,4},{4,8},{8,12},{12,16},{16,20},{20,24},{24,28},{1,5},{5,9},{9,... | collective-permute-start | bytes 368648 | tf_op jit(solution)/shard_map/ppermute | solution.py:732
  41.0 22.0 %collective-permute-start.10 = (bf16[960,128]{1,0:T(8,128)(2,1)}, bf16[960,128]{1,0:T(8,128)(2,1)S(1)}, u32[]{:S(2)}, u32[]{:S(2)}) collective-permute-start(bf16[960,128]{1,0:T(8,128)(2,1)} %get-tuple-element.96), channel_id=1, source_target_pairs={{0,9},{1,8},{2,11},{3,10},{4,13},{5,12},{6,15},{7,14},{8,1},{9,0},... | collective-permute-start | bytes 737288 | tf_op jit(solution)/shard_map/ppermute | solution.py:32
  45.4 17.7 %collective-permute-start.11 = (bf16[960,128]{1,0:T(8,128)(2,1)}, bf16[960,128]{1,0:T(8,128)(2,1)S(1)}, u32[]{:S(2)}, u32[]{:S(2)}) collective-permute-start(bf16[960,128]{1,0:T(8,128)(2,1)} %get-tuple-element.97), channel_id=1, source_target_pairs={{0,17},{1,16},{2,19},{3,18},{4,21},{5,20},{6,23},{7,22},{8,25},{9,... | collective-permute-start | bytes 737288 | tf_op jit(solution)/shard_map/ppermute | solution.py:32
  46.3 7.9 %collective-permute-start.4 = (bf16[5,48,256]{2,1,0:T(8,128)(2,1)S(1)}, bf16[5,48,256]{2,1,0:T(8,128)(2,1)S(1)}, u32[]{:S(2)}, u32[]{:S(2)}) collective-permute-start(bf16[5,48,256]{2,1,0:T(8,128)(2,1)S(1)} %get-tuple-element.149), channel_id=1, source_target_pairs={{0,4},{4,8},{8,12},{12,16},{16,20},{20,24},{24,28},{1,5},{5,9},{9,... | collective-permute-start | bytes 368648 | tf_op jit(solution)/shard_map/ppermute | solution.py:732
  48.3 9.1 %collective-permute-start.5 = (bf16[5,48,256]{2,1,0:T(8,128)(2,1)S(1)}, bf16[5,48,256]{2,1,0:T(8,128)(2,1)S(1)}, u32[]{:S(2)}, u32[]{:S(2)}) collective-permute-start(bf16[5,48,256]{2,1,0:T(8,128)(2,1)S(1)} %get-tuple-element.148), channel_id=1, source_target_pairs={{4,0},{8,4},{12,8},{16,12},{20,16},{24,20},{28,24},{5,1},{9,5},{13... | collective-permute-start | bytes 368648 | tf_op jit(solution)/shard_map/ppermute | solution.py:732
  49.8 27.3 %collective-permute-start.12 = (bf16[960,128]{1,0:T(8,128)(2,1)}, bf16[960,128]{1,0:T(8,128)(2,1)S(1)}, u32[]{:S(2)}, u32[]{:S(2)}) collective-permute-start(bf16[960,128]{1,0:T(8,128)(2,1)} %get-tuple-element.98), channel_id=1, source_target_pairs={{0,25},{1,24},{2,27},{3,26},{4,29},{5,28},{6,31},{7,30},{8,17},{9,... | collective-permute-start | bytes 737288 | tf_op jit(solution)/shard_map/ppermute | solution.py:32
  54.2 24.2 %collective-permute-start.6 = (bf16[960,128]{1,0:T(8,128)(2,1)}, bf16[960,128]{1,0:T(8,128)(2,1)S(1)}, u32[]{:S(2)}, u32[]{:S(2)}) collective-permute-start(bf16[960,128]{1,0:T(8,128)(2,1)} %get-tuple-element.92), channel_id=1, source_target_pairs={{0,8},{1,9},{2,10},{3,11},{4,12},{5,13},{6,14},{7,15},{8,0},{9,1},... | collective-permute-start | bytes 737288 | tf_op jit(solution)/shard_map/ppermute | solution.py:32
  57.5 21.0 %collective-permute-start.7 = (bf16[960,128]{1,0:T(8,128)(2,1)}, bf16[960,128]{1,0:T(8,128)(2,1)S(1)}, u32[]{:S(2)}, u32[]{:S(2)}) collective-permute-start(bf16[960,128]{1,0:T(8,128)(2,1)} %get-tuple-element.93), channel_id=1, source_target_pairs={{0,16},{1,17},{2,18},{3,19},{4,20},{5,21},{6,22},{7,23},{8,24},{9,... | collective-permute-start | bytes 737288 | tf_op jit(solution)/shard_map/ppermute | solution.py:32
  63.1 15.4 %collective-permute-start.8 = (bf16[960,128]{1,0:T(8,128)(2,1)}, bf16[960,128]{1,0:T(8,128)(2,1)S(1)}, u32[]{:S(2)}, u32[]{:S(2)}) collective-permute-start(bf16[960,128]{1,0:T(8,128)(2,1)} %get-tuple-element.94), channel_id=1, source_target_pairs={{0,24},{1,25},{2,26},{3,27},{4,28},{5,29},{6,30},{7,31},{8,16},{9,... | collective-permute-start | bytes 737288 | tf_op jit(solution)/shard_map/ppermute | solution.py:32
  63.1 15.4 %collective-permute-start.9 = (bf16[960,128]{1,0:T(8,128)(2,1)}, bf16[960,128]{1,0:T(8,128)(2,1)S(1)}, u32[]{:S(2)}, u32[]{:S(2)}) collective-permute-start(bf16[960,128]{1,0:T(8,128)(2,1)} %get-tuple-element.95), channel_id=1, source_target_pairs={{0,1},{1,0},{2,3},{3,2},{4,5},{5,4},{6,7},{7,6},{8,9},{9,8},{10,11... | collective-permute-start | bytes 737288 | tf_op jit(solution)/shard_map/ppermute | solution.py:32
  78.5 13.0 %collective-permute-start.15 = (bf16[960,128]{1,0:T(8,128)(2,1)S(1)}, bf16[960,128]{1,0:T(8,128)(2,1)S(1)}, u32[]{:S(2)}, u32[]{:S(2)}) collective-permute-start(bf16[960,128]{1,0:T(8,128)(2,1)S(1)} %copy-done.6), channel_id=1, source_target_pairs={{0,4},{1,5},{2,6},{3,7},{4,0},{5,1},{6,2},{7,3},{8,12},{9,13},{10,... | collective-permute-start | bytes 737288 | tf_op jit(solution)/shard_map/ppermute | solution.py:32
  81.5 10.2 %collective-permute-start.16 = (bf16[960,128]{1,0:T(8,128)(2,1)S(1)}, bf16[960,128]{1,0:T(8,128)(2,1)S(1)}, u32[]{:S(2)}, u32[]{:S(2)}) collective-permute-start(bf16[960,128]{1,0:T(8,128)(2,1)S(1)} %collective-permute-done.6.refs_1_), channel_id=1, source_target_pairs={{0,4},{1,5},{2,6},{3,7},{4,0},{5,1},{6,2},{7,3},{8,12},{9,13},{10,... | collective-permute-start | bytes 737288 | tf_op jit(solution)/shard_map/ppermute | solution.py:32
  81.6 10.6 %collective-permute-start.17 = (bf16[960,128]{1,0:T(8,128)(2,1)S(1)}, bf16[960,128]{1,0:T(8,128)(2,1)S(1)}, u32[]{:S(2)}, u32[]{:S(2)}) collective-permute-start(bf16[960,128]{1,0:T(8,128)(2,1)S(1)} %collective-permute-done.7.refs_2_), channel_id=1, source_target_pairs={{0,4},{1,5},{2,6},{3,7},{4,0},{5,1},{6,2},{7,3},{8,12},{9,13},{10,... | collective-permute-start | bytes 737288 | tf_op jit(solution)/shard_map/ppermute | solution.py:32
  82.0 10.3 %collective-permute-start.18 = (bf16[960,128]{1,0:T(8,128)(2,1)S(1)}, bf16[960,128]{1,0:T(8,128)(2,1)S(1)}, u32[]{:S(2)}, u32[]{:S(2)}) collective-permute-start(bf16[960,128]{1,0:T(8,128)(2,1)S(1)} %collective-permute-done.8.refs_3_), channel_id=1, source_target_pairs={{0,4},{1,5},{2,6},{3,7},{4,0},{5,1},{6,2},{7,3},{8,12},{9,13},{10,... | collective-permute-start | bytes 737288 | tf_op jit(solution)/shard_map/ppermute | solution.py:32
  89.1 13.5 %collective-permute-start.14 = (bf16[1664,128]{1,0:T(8,128)(2,1)S(1)}, bf16[1664,128]{1,0:T(8,128)(2,1)S(1)}, u32[]{:S(2)}, u32[]{:S(2)}) collective-permute-start(bf16[1664,128]{1,0:T(8,128)(2,1)S(1)} %fusion), channel_id=1, source_target_pairs={{0,4},{1,5},{2,6},{3,7},{4,0},{5,1},{6,2},{7,3},{8,12},{9,13},{10,... | collective-permute-start | bytes 1277960 | tf_op jit(solution)/shard_map/ppermute | solution.py:32
  102.8 7.4 %collective-permute-start.26 = (bf16[832,128]{1,0:T(8,128)(2,1)S(1)}, bf16[832,128]{1,0:T(8,128)(2,1)S(1)}, u32[]{:S(2)}, u32[]{:S(2)}) collective-permute-start(bf16[832,128]{1,0:T(8,128)(2,1)S(1)} %fusion.2), channel_id=1, source_target_pairs={{0,8},{1,9},{2,10},{3,11},{4,12},{5,13},{6,14},{7,15},{8,0},{9,1},... | collective-permute-start | bytes 638984 | tf_op jit(solution)/shard_map/ppermute | solution.py:32
  115.0 8.1 %collective-permute-start.28 = (bf16[208,128]{1,0:T(8,128)(2,1)S(1)}, bf16[208,128]{1,0:T(8,128)(2,1)S(1)}, u32[]{:S(2)}, u32[]{:S(2)}) collective-permute-start(bf16[208,128]{1,0:T(8,128)(2,1)S(1)} %fusion.7), channel_id=1, source_target_pairs={{0,1},{1,0},{2,3},{3,2},{4,5},{5,4},{6,7},{7,6},{8,9},{9,8},{10,11... | collective-permute-start | bytes 159752 | tf_op jit(solution)/shard_map/ppermute | solution.py:32
  115.6 9.6 %collective-permute-start.23 = (bf16[512,128]{1,0:T(8,128)(2,1)S(1)}, bf16[512,128]{1,0:T(8,128)(2,1)S(1)}, u32[]{:S(2)}, u32[]{:S(2)}) collective-permute-start(bf16[512,128]{1,0:T(8,128)(2,1)S(1)} %get-tuple-element.147), channel_id=1, source_target_pairs={{0,3},{1,2},{2,1},{3,0},{4,7},{5,6},{6,5},{7,4},{8,11},{9,10},{10,... | collective-permute-start | bytes 393224 | tf_op jit(solution)/shard_map/ppermute | solution.py:32
  119.3 8.3 %collective-permute-start.24 = (bf16[512,128]{1,0:T(8,128)(2,1)S(1)}, bf16[512,128]{1,0:T(8,128)(2,1)S(1)}, u32[]{:S(2)}, u32[]{:S(2)}) collective-permute-start(bf16[512,128]{1,0:T(8,128)(2,1)S(1)} %get-tuple-element.146), channel_id=1, source_target_pairs={{0,3},{1,2},{2,1},{3,0},{4,7},{5,6},{6,5},{7,4},{8,11},{9,10},{10,... | collective-permute-start | bytes 393224 | tf_op jit(solution)/shard_map/ppermute | solution.py:32
  119.4 9.7 %collective-permute-start.25 = (bf16[544,128]{1,0:T(8,128)(2,1)S(1)}, bf16[544,128]{1,0:T(8,128)(2,1)S(1)}, u32[]{:S(2)}, u32[]{:S(2)}) collective-permute-start(bf16[544,128]{1,0:T(8,128)(2,1)S(1)} %slice.31), channel_id=1, source_target_pairs={{0,3},{1,2},{2,1},{3,0},{4,7},{5,6},{6,5},{7,4},{8,11},{9,10},{10,... | collective-permute-start | bytes 417800 | tf_op jit(solution)/shard_map/ppermute | solution.py:32
  123.1 6.6 %collective-permute-start.29 = (bf16[208,128]{1,0:T(8,128)(2,1)S(1)}, bf16[208,128]{1,0:T(8,128)(2,1)S(1)}, u32[]{:S(2)}, u32[]{:S(2)}) collective-permute-start(bf16[208,128]{1,0:T(8,128)(2,1)S(1)} %fusion.6), channel_id=1, source_target_pairs={{0,3},{1,2},{2,1},{3,0},{4,7},{5,6},{6,5},{7,4},{8,11},{9,10},{10,... | collective-permute-start | bytes 159752 | tf_op jit(solution)/shard_map/ppermute | solution.py:32
  129.8 13.1 %collective-permute-start.32 = (bf16[1,752,128]{2,1,0:T(8,128)(2,1)S(1)}, bf16[1,752,128]{2,1,0:T(8,128)(2,1)S(1)}, u32[]{:S(2)}, u32[]{:S(2)}) collective-permute-start(bf16[1,752,128]{2,1,0:T(8,128)(2,1)S(1)} %fusion.1), channel_id=1, source_target_pairs={{0,1},{1,0},{2,3},{3,2},{4,5},{5,4},{6,7},{7,6},{8,9},{9,8},{10,11... | collective-permute-start | bytes 577544 | tf_op jit(solution)/shard_map/ppermute | solution.py:32
  143.0 9.4 %collective-permute-start.35 = (bf16[2,752,128]{2,1,0:T(8,128)(2,1)S(1)}, bf16[2,752,128]{2,1,0:T(8,128)(2,1)S(1)}, u32[]{:S(2)}, u32[]{:S(2)}) collective-permute-start(bf16[2,752,128]{2,1,0:T(8,128)(2,1)S(1)} %pad_maximum_fusion.3), channel_id=1, source_target_pairs={{0,8},{1,9},{2,10},{3,11},{4,12},{5,13},{6,14},{7,15},{8,0},{9,1},... | collective-permute-start | bytes 1155080 | tf_op jit(solution)/shard_map/ppermute | solution.py:32
  144.6 6.4 %collective-permute-start.34 = (bf16[2,512,128]{2,1,0:T(8,128)(2,1)S(1)}, bf16[2,512,128]{2,1,0:T(8,128)(2,1)S(1)}, u32[]{:S(2)}, u32[]{:S(2)}) collective-permute-start(bf16[2,512,128]{2,1,0:T(8,128)(2,1)S(1)} %pad_maximum_fusion.5), channel_id=1, source_target_pairs={{0,1},{1,0},{2,3},{3,2},{4,5},{5,4},{6,7},{7,6},{8,9},{9,8},{10,11... | collective-permute-start | bytes 786440 | tf_op jit(solution)/shard_map/ppermute | solution.py:32
  144.7 7.6 %collective-permute-start.33 = (bf16[2,512,128]{2,1,0:T(8,128)(2,1)S(1)}, bf16[2,512,128]{2,1,0:T(8,128)(2,1)S(1)}, u32[]{:S(2)}, u32[]{:S(2)}) collective-permute-start(bf16[2,512,128]{2,1,0:T(8,128)(2,1)S(1)} %pad_maximum_fusion.4), channel_id=1, source_target_pairs={{0,16},{1,17},{2,18},{3,19},{4,20},{5,21},{6,22},{7,23},{8,24},{9,... | collective-permute-start | bytes 786440 | tf_op jit(solution)/shard_map/ppermute | solution.py:32
  152.5 15.2 %collective-permute-start.36 = (bf16[4,752,128]{2,1,0:T(8,128)(2,1)S(1)}, bf16[4,752,128]{2,1,0:T(8,128)(2,1)S(1)}, u32[]{:S(2)}, u32[]{:S(2)}) collective-permute-start(bf16[4,752,128]{2,1,0:T(8,128)(2,1)S(1)} %pad_maximum_fusion.refs_0_.refs_8_), channel_id=1, source_target_pairs={{0,16},{1,17},{2,18},{3,19},{4,20},{5,21},{6,22},{7,23},{8,24},{9,... | collective-permute-start | bytes 2310152 | tf_op jit(solution)/shard_map/ppermute | solution.py:32
  152.6 16.8 %collective-permute-start.37 = (bf16[4,752,128]{2,1,0:T(8,128)(2,1)S(1)}, bf16[4,752,128]{2,1,0:T(8,128)(2,1)S(1)}, u32[]{:S(2)}, u32[]{:S(2)}) collective-permute-start(bf16[4,752,128]{2,1,0:T(8,128)(2,1)S(1)} %pad_maximum_fusion.refs_0_.refs_8_), channel_id=1, source_target_pairs={{0,4},{1,5},{2,6},{3,7},{4,0},{5,1},{6,2},{7,3},{8,12},{9,13},{10,... | collective-permute-start | bytes 2310152 | tf_op jit(solution)/shard_map/ppermute | solution.py:32
  152.7 15.5 %collective-permute-start.42 = (bf16[4,512,128]{2,1,0:T(8,128)(2,1)S(1)}, bf16[4,512,128]{2,1,0:T(8,128)(2,1)}, u32[]{:S(2)}, u32[]{:S(2)}) collective-permute-start(bf16[4,512,128]{2,1,0:T(8,128)(2,1)S(1)} %pad_maximum_fusion.2.refs_4_), channel_id=1, source_target_pairs={{0,8},{1,9},{2,10},{3,11},{4,12},{5,13},{6,14},{7,15},{8,0},{9,1},... | collective-permute-start | bytes 1572872 | tf_op jit(solution)/shard_map/ppermute | solution.py:32
  153.9 15.5 %collective-permute-start.39 = (bf16[4,512,128]{2,1,0:T(8,128)(2,1)}, bf16[4,512,128]{2,1,0:T(8,128)(2,1)}, u32[]{:S(2)}, u32[]{:S(2)}) collective-permute-start(bf16[4,512,128]{2,1,0:T(8,128)(2,1)} %pad_maximum_fusion.1.refs_0_), channel_id=1, source_target_pairs={{0,1},{1,0},{2,3},{3,2},{4,5},{5,4},{6,7},{7,6},{8,9},{9,8},{10,11... | collective-permute-start | bytes 1572872 | tf_op jit(solution)/shard_map/ppermute | solution.py:32
  167.7 7.3 %collective-permute-start.43 = (bf16[4,512,128]{2,1,0:T(8,128)(2,1)S(1)}, bf16[4,512,128]{2,1,0:T(8,128)(2,1)}, u32[]{:S(2)}, u32[]{:S(2)}) collective-permute-start(bf16[4,512,128]{2,1,0:T(8,128)(2,1)S(1)} %pad_maximum_fusion.2.refs_4_), channel_id=1, source_target_pairs={{0,4},{1,5},{2,6},{3,7},{4,0},{5,1},{6,2},{7,3},{8,12},{9,13},{10,... | collective-permute-start | bytes 1572872 | tf_op jit(solution)/shard_map/ppermute | solution.py:32
  168.2 6.8 %collective-permute-start.40 = (bf16[4,512,128]{2,1,0:T(8,128)(2,1)}, bf16[4,512,128]{2,1,0:T(8,128)(2,1)}, u32[]{:S(2)}, u32[]{:S(2)}) collective-permute-start(bf16[4,512,128]{2,1,0:T(8,128)(2,1)} %pad_maximum_fusion.1.refs_0_), channel_id=1, source_target_pairs={{0,4},{1,5},{2,6},{3,7},{4,0},{5,1},{6,2},{7,3},{8,12},{9,13},{10,... | collective-permute-start | bytes 1572872 | tf_op jit(solution)/shard_map/ppermute | solution.py:32
  169.4 5.6 %collective-permute-start.44 = (bf16[4,512,128]{2,1,0:T(8,128)(2,1)}, bf16[4,512,128]{2,1,0:T(8,128)(2,1)}, u32[]{:S(2)}, u32[]{:S(2)}) collective-permute-start(bf16[4,512,128]{2,1,0:T(8,128)(2,1)} %collective-permute-done.42.refs_5_), channel_id=1, source_target_pairs={{0,4},{1,5},{2,6},{3,7},{4,0},{5,1},{6,2},{7,3},{8,12},{9,13},{10,... | collective-permute-start | bytes 1572872 | tf_op jit(solution)/shard_map/ppermute | solution.py:32
  (43 other events, 313.3 us)

commit v2 on v1

--- a/solution.py
+++ b/solution.py
@@ -143,25 +143,49 @@
     )(place, features, mine, theirs)
 
 
+def write_small(chips, sources, packed, outs, chip, core, half):
+    conv1, conv2, up, skip, out = outs
+    depth = packed.shape[0] // (4 * chips)
+    for s in range(2):
+        for mask in range(2 * chips):
+            whose = chip ^ (mask % chips)
+            at = core ^ s
+            for d in range(bits(chips)):
+                at = 2 * at + ((whose >> d) & 1)
+            at = 2 * at + (half ^ (mask // chips))
+            packed[pl.ds(pl.multiple_of(at * depth, depth), depth), :] = sources[s][
+                mask
+            ].astype(jnp.float32)
+    for a in range(3):
+        conv1[a] = packed[192 * a : 192 * a + 192, :]
+        for n in range(2):
+            at = 576 + 384 * (2 * a + n)
+            conv2[a, :, n * 128 : (n + 1) * 128] = packed[at : at + 384, :]
+    up[...] = packed[2880:3136, :]
+    skip[...] = packed[3136:3264, :]
+    out[...] = packed[3264:3272, :]
+
+
 def unpack_kernel(orders, bounds, chips, block, place, *refs):
     parts = len(orders)
     sources = [refs[4 * p : 4 * p + 4] for p in range(parts)]
-    out = refs[4 * parts]
-    gathered, ready, sems = refs[4 * parts + 1 :]
+    little = refs[4 * parts : 4 * parts + 2]
+    out, *small = refs[4 * parts + 2 : 4 * parts + 8]
+    gathered, ready, packed, sems = refs[4 * parts + 8 :]
     tile, half = place[0], place[1]
     chip, core = tile >> 1, tile & 1
     ones = [lax.broadcasted_iota(jnp.int32, (128, 128), n) for n in range(2)]
     identity = (ones[0] == ones[1]).astype(jnp.bfloat16)
     batches = [
-        (p, n, min(4, bounds[p + 1] - n))
+        (p, n, min(2, bounds[p + 1] - n))
         for p in range(parts)
-        for n in range(bounds[p], bounds[p + 1], 4)
+        for n in range(bounds[p], bounds[p + 1], 2)
     ]
 
     def copy(n):
         _, start, count = batches[n]
         return pltpu.make_async_copy(
-            ready.at[n % 2, 0:count], out.at[start : start + count], sems.at[n % 2]
+            ready.at[n % 4, 0:count], out.at[start : start + count], sems.at[n % 4]
         )
 
     for n, (p, start, count) in enumerate(batches):
@@ -174,36 +198,40 @@
                 for g in range(count):
                     at = (start - bounds[p] + g) * block
                     gathered[
-                        n % 2,
+                        n % 4,
                         g,
                         half ^ (mask // chips),
                         pl.ds(pl.multiple_of(whose * block, block), block),
                         :,
                     ] = sources[p][s][i, at : at + block, :]
-        if n >= 2:
-            copy(n - 2).wait()
+        if n >= 4:
+            copy(n - 4).wait()
         for g in range(count):
             for u in range(2):
-                ready[n % 2, g, u * 128 : (u + 1) * 128, :] = dot(
-                    identity, gathered[n % 2, g, u], NT
+                ready[n % 4, g, u * 128 : (u + 1) * 128, :] = dot(
+                    identity, gathered[n % 4, g, u], NT
                 )
         copy(n).start()
-    for n in range(max(0, len(batches) - 2), len(batches)):
+    write_small(chips, little, packed, small, chip, core, half)
+    for n in range(max(0, len(batches) - 4), len(batches)):
         copy(n).wait()
 
 
-def unpack(place, sources, orders, bounds, chips, block):
+def unpack(place, sources, small, orders, bounds, chips, block, packed_rows):
     wide = 2 * chips * block
-    operands = [array for group in sources for array in group]
+    operands = [array for group in sources for array in group] + small
+    shapes = [(TAPS * TAPS, 256, wide), (3, 192, 128), (3, 384, 256), (256, 128), (128, 128)]
+    shapes.append((K, 128))
     return pl.pallas_call(
         functools.partial(unpack_kernel, orders, bounds, chips, block),
-        out_shape=jax.ShapeDtypeStruct((TAPS * TAPS, 256, wide), jnp.float32),
+        out_shape=[jax.ShapeDtypeStruct(shape, jnp.float32) for shape in shapes],
         in_specs=[SMEM] + [VMEM] * len(operands),
-        out_specs=ANY,
+        out_specs=[ANY] + [VMEM] * 5,
         scratch_shapes=[
-            pltpu.VMEM((2, 4, 2, wide, 128), jnp.bfloat16),
-            pltpu.VMEM((2, 4, 256, wide), jnp.float32),
-            pltpu.SemaphoreType.DMA((2,)),
+            pltpu.VMEM((4, 2, 2, wide, 128), jnp.bfloat16),
+            pltpu.VMEM((4, 2, 256, wide), jnp.float32),
+            pltpu.VMEM((packed_rows, 128), jnp.float32),
+            pltpu.SemaphoreType.DMA((4,)),
         ],
         compiler_params=params(56),
         cost_estimate=LIGHT,
@@ -232,35 +260,38 @@
     groups = TAPS * TAPS
     bounds = [groups * p // dims for p in range(dims + 1)]
     parts = [term[bounds[p] * block : bounds[p + 1] * block] for p in range(dims)]
-    parts.append(small)
     totals, mask = [part.astype(jnp.float32) for part in parts], 3
+    little = small.astype(jnp.float32)
     while mask < lax.axis_size("dp"):
         parts = [total.astype(jnp.bfloat16) for total in totals]
         others = [flip(part, 0, mask) for part in parts]
-        others, results = lax.optimization_barrier((others, results))
+        others[0], results = lax.optimization_barrier((others[0], results))
         totals = [
             part.astype(jnp.float32) + other.astype(jnp.float32)
             for part, other in zip(parts, others)
         ]
+        small = little.astype(jnp.bfloat16)
+        little = small.astype(jnp.float32) + flip(small, 0, mask).astype(jnp.float32)
         mask = 4 if mask == 3 else 2 * mask
-    totals[-2:] = [jnp.concatenate(totals[-2:])]
     parts = [(total * scale).astype(jnp.bfloat16)[None] for total in totals]
+    small = (little * scale).astype(jnp.bfloat16)[None]
     orders = [[(p + q) % dims for q in range(dims)] for p in range(dims)]
 
     def across(value, dim):
         return flip(value, 2 << dim, 0) if dim < dims - 1 else flip(value, 0, 1)
 
+    for q in range(dims):
+        small = jnp.concatenate([small, across(small, q)])
+    small = [small, flip(small, 1, 0)]
     for q in range(dims - 1):
         others = [across(part, orders[p][q]) for p, part in enumerate(parts)]
-        others = lax.optimization_barrier(others)
         parts = [jnp.concatenate(pair) for pair in zip(parts, others)]
     last = [across(part, orders[p][-1]) for p, part in enumerate(parts)]
     near = [flip(part, 1, 0) for part in parts]
     far = [flip(part, 1, 0) for part in last]
     sources = list(zip(parts, last, near, far))
-    target = unpack(place, sources, orders, bounds, chips, block)
-    sources = sources[-1]
-    return target, unpack_small(place, sources, orders[-1], chips, packed_rows), results
+    target, *small = unpack(place, sources, small, orders, bounds, chips, block, packed_rows)
+    return target, small, results
 
 
 def dot(lhs, rhs, dims=((1,), (0,))):
@@ -681,51 +712,6 @@
     )(partial, returned, slope1, image, halo, *terms)
 
 
-def small_kernel(order, chips, place, *refs):
-    sources, packed = refs[:4], refs[-1]
-    conv1, conv2, up, skip, out = refs[4:-1]
-    tile, half = place[0], place[1]
-    chip, core = tile >> 1, tile & 1
-    depth = packed.shape[0] // (4 * chips)
-    dims = len(order)
-    entries, height = sources[0].shape[0], sources[0].shape[1]
-    for s in range(4):
-        for i in range(entries):
-            index = i + entries * (s % 2)
-            mask = sum(1 << d for q, d in enumerate(order) if (index >> q) & 1)
-            whose = chip ^ (mask % chips)
-            at = core ^ (s // 2)
-            for d in range(dims - 1):
-                at = 2 * at + ((whose >> d) & 1)
-            at = 2 * at + (half ^ (mask // chips))
-            packed[pl.ds(pl.multiple_of(at * depth, depth), depth), :] = sources[s][
-                i, height - depth :, :
-            ].astype(jnp.float32)
-    for a in range(3):
-        conv1[a] = packed[192 * a : 192 * a + 192, :]
-        for n in range(2):
-            at = 576 + 384 * (2 * a + n)
-            conv2[a, :, n * 128 : (n + 1) * 128] = packed[at : at + 384, :]
-    up[...] = packed[2880:3136, :]
-    skip[...] = packed[3136:3264, :]
-    out[...] = packed[3264:3272, :]
-
-
-def unpack_small(place, sources, order, chips, packed_rows):
-    f32 = jnp.float32
-    shapes = [(3, 192, 128), (3, 384, 256), (256, 128), (128, 128), (K, 128)]
-    return pl.pallas_call(
-        functools.partial(small_kernel, order, chips),
-        out_shape=[jax.ShapeDtypeStruct(shape, f32) for shape in shapes],
-        in_specs=[SMEM] + [VMEM] * 4,
-        out_specs=[VMEM] * 5,
-        scratch_shapes=[pltpu.VMEM((packed_rows, 128), f32)],
-        compiler_params=params(56),
-        cost_estimate=LIGHT,
-        name="small_out",
-    )(place, *sources)
-
-
 def moved(block, distance):
     tiles = lax.axis_size("tile")
     route = [(i, i + distance) for i in range(tiles) if 0 <= i + distance < tiles]
@@ -764,10 +750,11 @@
     )
     messages = pack(place, features, mine, flip(theirs, 1, 0))
     gradient, messages = lax.optimization_barrier((gradient, messages))
-    own = [
-        part if m == 0 else flip(part, 2 * (m % chips), m // chips)
-        for m, part in enumerate(messages)
-    ]
+
+    def send(m, message):
+        return flip(message, 2 * (m % chips), m // chips)
+
+    own = [messages[0]] + [send(m, messages[m]) for m in range(1, 2 * chips)]
     left, right = edges(gradient)
     partial, edge, conv2_term, up_term, skip_term = back(
         left, gradient, right, context_weight, pooled, up_weight, slope2, taps, grads,
@@ -781,15 +768,16 @@
         partial, returned, slope1, image, halo,
         (conv2_term, up_term, skip_term, out_term), packed_rows,
     )
+    other, packed = lax.optimization_barrier((other, packed))
+    block = mine.shape[2]
+    context_term = wgrad(place, own, other, chips, rows, width, block)
     logits = logits.reshape(2, 2, K, rows, width).transpose(2, 3, 1, 4, 0)
     logits = logits.reshape(1, K, 2 * rows, 2 * width)
     grad_features = grad_features[None]
     scale = 1.0 / (lax.axis_size("dp") * tiles * 4 * rows * width)
-    block = mine.shape[2]
-    context_term = wgrad(place, own, other, chips, rows, width, block)
     folded, context_term = fold_small(packed, chips, context_term)
-    grad_context, small, (logits, grad_features) = sum_and_share(
-        context_term, folded, place, chips, block, scale, (logits, grad_features), packed_rows
+    grad_context, small, logits = sum_and_share(
+        context_term, folded, place, chips, block, scale, logits, packed_rows
     )
     return (
         logits,

time: 188 us -> 179 us (0.952)
  waiting for transfers between devices: 43.4 us -> 31.9 us
  starting transfers between devices: 67.6 us -> 75.7 us
  Pallas kernels: 57.6 us -> 54.1 us
    ppermute x39 -> x43, waiting for transfers between devices: 42.6 us -> 31.1 us  [flip(): return lax.ppermute(value, BOTH, route)]
    ppermute x39 -> x43, starting transfers between devices: 54.7 us -> 61.1 us  [flip(): return lax.ppermute(value, BOTH, route)]
    pallas_call x1 -> x0, Pallas kernels: 3.2 us -> none  [unpack_small(): pl.pallas_call(functools.partial(small_kernel, order, chips), out_shape=[...]
    unnamed x62 -> x68, local copies, waits for them, and re-layouts: 6.5 us -> 5.74 us
  transfers between devices with their start and end apart: 45 -> 49, of which waited for: 16 -> 14; matrix products, arithmetic and copies ran while one was open for 5% -> 4% of each run, Pallas kernels for 14% -> 13%
where the time goes in v2:
time: 179 us
  starting transfers between devices  75.7 us (42%)
  Pallas kernels  54.1 us (30%)
  waiting for transfers between devices  31.9 us (18%)
  local copies, waits for them, and re-layouts  14.3 us (8%)
    ppermute x43, starting transfers between devices, flip(): return lax.ppermute(value, BOTH, route)  61.1 us
    ppermute x43, waiting for transfers between devices, flip(): return lax.ppermute(value, BOTH, route)  31.1 us
    ppermute x6, starting transfers between devices, moved(): return lax.ppermute(block, 'tile', route)  14.6 us
    pallas_call x1, Pallas kernels, back(): pl.pallas_call(back_kernel, out_shape=outs, grid=(TAPS,), in_specs=specs,...  11.7 us
    pallas_call x1, Pallas kernels, unpack(): pl.pallas_call(functools.partial(unpack_kernel, orders, bounds, chips, bl...  11.4 us
    pallas_call x1, Pallas kernels, decode(): pl.pallas_call(functools.partial(decode_kernel, chips, block), out_shape=...  11.4 us
    pallas_call x1, Pallas kernels, wgrad(): pl.pallas_call(functools.partial(wgrad_kernel, chips, rows, width, block)...  6.86 us
    unnamed x68, local copies, waits for them, and re-layouts  5.74 us
  transfers between devices with their start and end apart: 49, of which 14 were waited for; matrix products, arithmetic and copies ran while one was open for 4% of the time, Pallas kernels for 13%

profile of v2, /device:TPU:0, one launch (start us, length us, event | category | flops | bytes accessed | tf_op | source)
XLA Modules:
  0.0 178.5 jit_solution(7520710303285880413)
XLA Ops:
  1.4 2.4 %collective-permute-start = (bf16[20,1,256]{2,1,0:T(2,128)(2,1)S(1)}, bf16[20,1,256]{2,1,0:T(2,128)(2,1)S(1)}, u32[]{:S(2)}, u32[]{:S(2)}) collective-permute-start(bf16[20,1,256]{2,1,0:T(2,128)(2,1)S(1)} %reshape_squeeze.8), channel_id=1, source_target_pairs={{0,4},{4,8},{8,12},{12,16},{16,20},{20,24},{24,28},{1,5},{5,9},{9,... | collective-permute-start | bytes 30728 | tf_op jit(solution)/shard_map/ppermute | solution.py:718
  3.8 3.2 %reshape_squeeze.6.image = bf16[20,128,256]{2,1,0:T(8,128)(2,1)} reshape(bf16[1,20,256,128]{3,2,1,0:T(8,128)(2,1)} %param.8) | data formatting | bytes 2621440 | tf_op jit(solution)/shard_map/reshape;squeeze | solution.py:744
  7.7 5.2 %encode.1 = (bf16[10,128,384]{2,1,0:T(8,128)(2,1)}, f32[10,128,256]{2,1,0:T(8,128)}, bf16[5,128,256]{2,1,0:T(8,128)(2,1)}, f32[5,128,256]{2,1,0:T(8,128)}) custom-call(bf16[20,128,256]{2,1,0:T(8,128)(2,1)} %reshape_squeeze.6.image, bf16[20,16,256]{2,1,0:T(8,128)(2,1)} %concatenate.35.halo, bf16[3,192,128]{2,1,0:T(8,128)(2,1)} %weight1.1, ...), custom_call_target="tpu_custom_call" | custom-call | flops 1000 | bytes 1000 | tf_op jit(solution)/shard_map/encode/pallas_call | solution.py:366
  15.2 5.1 %collective-permute-start.1 = (bf16[5,48,256]{2,1,0:T(8,128)(2,1)S(1)}, bf16[5,48,256]{2,1,0:T(8,128)(2,1)S(1)}, u32[]{:S(2)}, u32[]{:S(2)}) collective-permute-start(bf16[5,48,256]{2,1,0:T(8,128)(2,1)S(1)} %get-tuple-element.151), channel_id=1, source_target_pairs={{0,4},{4,8},{8,12},{12,16},{16,20},{20,24},{24,28},{1,5},{5,9},{9,... | collective-permute-start | bytes 368648 | tf_op jit(solution)/shard_map/ppermute | solution.py:718
  22.2 11.4 %decode.1 = (f32[2,2,8,640]{3,2,1,0:T(8,128)}, bf16[5,128,256]{2,1,0:T(8,128)(2,1)}, bf16[4,5,32,128]{3,2,1,0:T(8,128)(2,1)}, bf16[4,5,32,128]{3,2,1,0:T(8,128)(...) custom-call(s32[2]{0:T(128)} %pad_add_fusion.place, ...), custom_call_target="tpu_custom_call" | custom-call | flops 1000 | bytes 1000 | tf_op jit(solution)/shard_map/decode/pallas_call | solution.py:520
  33.5 2.4 %collective-permute-start.3 = (bf16[4,5,32,128]{3,2,1,0:T(8,128)(2,1)}, bf16[4,5,32,128]{3,2,1,0:T(8,128)(2,1)S(1)}, u32[]{:S(2)}, u32[]{:S(2)}) collective-permute-start(bf16[4,5,32,128]{3,2,1,0:T(8,128)(2,1)} %get-tuple-element.76), channel_id=1, source_target_pairs={{0,4},{1,5},{2,6},{3,7},{4,0},{5,1},{6,2},{7,3},{8,12},{9,13},{10,... | collective-permute-start | bytes 491528 | tf_op jit(solution)/shard_map/ppermute | solution.py:32
  37.8 2.5 %pack.1 = (bf16[960,128]{1,0:T(8,128)(2,1)}, bf16[960,128]{1,0:T(8,128)(2,1)}, bf16[960,128]{1,0:T(8,128)(2,1)}, bf16[960,128]{1,0:T(8,128)(2,1)}, bf16[960,128]...) custom-call(s32[2]{0:T(128)} %pad_add_fusion.place, ...), custom_call_target="tpu_custom_call" | custom-call | flops 1000 | bytes 1000 | tf_op jit(solution)/shard_map/pack/pallas_call | solution.py:135
  40.3 2.7 %collective-permute-start.6 = (bf16[960,128]{1,0:T(8,128)(2,1)}, bf16[960,128]{1,0:T(8,128)(2,1)S(1)}, u32[]{:S(2)}, u32[]{:S(2)}) collective-permute-start(bf16[960,128]{1,0:T(8,128)(2,1)} %get-tuple-element.92), channel_id=1, source_target_pairs={{0,8},{1,9},{2,10},{3,11},{4,12},{5,13},{6,14},{7,15},{8,0},{9,1},... | collective-permute-start | bytes 737288 | tf_op jit(solution)/shard_map/ppermute | solution.py:32
  43.0 1.8 %collective-permute-start.7 = (bf16[960,128]{1,0:T(8,128)(2,1)}, bf16[960,128]{1,0:T(8,128)(2,1)S(1)}, u32[]{:S(2)}, u32[]{:S(2)}) collective-permute-start(bf16[960,128]{1,0:T(8,128)(2,1)} %get-tuple-element.93), channel_id=1, source_target_pairs={{0,16},{1,17},{2,18},{3,19},{4,20},{5,21},{6,22},{7,23},{8,24},{9,... | collective-permute-start | bytes 737288 | tf_op jit(solution)/shard_map/ppermute | solution.py:32
  47.1 3.2 %collective-permute-start.4 = (bf16[5,48,256]{2,1,0:T(8,128)(2,1)S(1)}, bf16[5,48,256]{2,1,0:T(8,128)(2,1)S(1)}, u32[]{:S(2)}, u32[]{:S(2)}) collective-permute-start(bf16[5,48,256]{2,1,0:T(8,128)(2,1)S(1)} %get-tuple-element.149), channel_id=1, source_target_pairs={{0,4},{4,8},{8,12},{12,16},{16,20},{20,24},{24,28},{1,5},{5,9},{9,... | collective-permute-start | bytes 368648 | tf_op jit(solution)/shard_map/ppermute | solution.py:718
  53.5 3.8 %collective-permute-start.10 = (bf16[960,128]{1,0:T(8,128)(2,1)}, bf16[960,128]{1,0:T(8,128)(2,1)S(1)}, u32[]{:S(2)}, u32[]{:S(2)}) collective-permute-start(bf16[960,128]{1,0:T(8,128)(2,1)} %get-tuple-element.96), channel_id=1, source_target_pairs={{0,9},{1,8},{2,11},{3,10},{4,13},{5,12},{6,15},{7,14},{8,1},{9,0},... | collective-permute-start | bytes 737288 | tf_op jit(solution)/shard_map/ppermute | solution.py:32
  60.3 11.7 %back.1 = (f32[10,128,256]{2,1,0:T(8,128)}, f32[10,1,128]{2,1,0:T(1,128)}, f32[3,384,256]{2,1,0:T(8,128)}, f32[256,128]{1,0:T(8,128)}, f32[128,128]{1,0:T(8,128)}) custom-call(bf16[5,48,256]{2,1,0:T(8,128)(2,1)} %copy-done.27, bf16[5,128,256]{2,1,0:T(8,128)(2,1)} %get-tuple-element.85.gradient, bf16[5,48,256]{2,1,0:T(8,128)(2,1)} %copy-done.26, ...), custom_call_target="tpu_custom_call" | custom-call | flops 1000 | bytes 1000 | tf_op jit(solution)/shard_map/back/pallas_call | solution.py:640
  72.7 5.5 %collective-permute-done.12.refs_7_ = bf16[960,128]{1,0:T(8,128)(2,1)S(1)} collective-permute-done((bf16[960,128]{1,0:T(8,128)(2,1)}, bf16[960,128]{1,0:T(8,128)(2,1)S(1)}, u32[]{:S(2)}, u32[]{:S(2)}) %collective-permute-start.12) | collective-permute-done | bytes 245792 | tf_op jit(solution)/shard_map/ppermute | solution.py:32
  82.0 2.3 %collective-permute-start.17 = (bf16[960,128]{1,0:T(8,128)(2,1)S(1)}, bf16[960,128]{1,0:T(8,128)(2,1)S(1)}, u32[]{:S(2)}, u32[]{:S(2)}) collective-permute-start(bf16[960,128]{1,0:T(8,128)(2,1)S(1)} %collective-permute-done.9.refs_4_), channel_id=1, source_target_pairs={{0,4},{1,5},{2,6},{3,7},{4,0},{5,1},{6,2},{7,3},{8,12},{9,13},{10,... | collective-permute-start | bytes 737288 | tf_op jit(solution)/shard_map/ppermute | solution.py:32
  85.0 5.1 %finish.1 = (f32[10,256,128]{2,1,0:T(8,128)}, f32[3328,128]{1,0:T(8,128)}) custom-call(f32[10,128,256]{2,1,0:T(8,128)} %get-tuple-element.107.partial, f32[10,1,128]{2,1,0:T(1,128)} %copy-done.32, f32[10,128,256]{2,1,0:T(8,128)} %get-tuple-element.109.slope1, bf16[20,128,256]{2,1,0:T(8,128)(2,1)} %reshape_squeeze.6.image, ...), custom_call_target="tpu_custom_call" | custom-call | flops 1000 | bytes 1000 | tf_op jit(solution)/shard_map/finish/pallas_call | solution.py:700
  92.6 6.9 %context_term.1 = bf16[1568,128]{1,0:T(8,128)(2,1)} custom-call(s32[2]{0:T(128)} %pad_add_fusion.place, bf16[960,128]{1,0:T(8,128)(2,1)} %get-tuple-element.99.refs_0_, bf16[960,128]{1,0:T(8,128)(2,1)} %copy-done.10, bf16[960,128]{1,0:T(8,128)(2,1)} %copy-done.11, bf16[960,128]{1,0:T(8,128)(2,1)} %copy-done.12, bf16[960,128]{1,0:T(8,128)(2,1)} %copy-done.13, ...), custom_call_target="tpu_custom_call" | custom-call | flops 1000 | bytes 1000 | tf_op jit(solution)/shard_map/context_term/pallas_call | solution.py:102
  100.5 3.7 %collective-permute-start.23 = (bf16[512,128]{1,0:T(8,128)(2,1)S(1)}, bf16[512,128]{1,0:T(8,128)(2,1)S(1)}, u32[]{:S(2)}, u32[]{:S(2)}) collective-permute-start(bf16[512,128]{1,0:T(8,128)(2,1)S(1)} %get-tuple-element.147), channel_id=1, source_target_pairs={{0,3},{1,2},{2,1},{3,0},{4,7},{5,6},{6,5},{7,4},{8,11},{9,10},{10,... | collective-permute-start | bytes 393224 | tf_op jit(solution)/shard_map/ppermute | solution.py:32
  105.0 3.7 %collective-permute-start.35 = (bf16[544,128]{1,0:T(8,128)(2,1)S(1)}, bf16[544,128]{1,0:T(8,128)(2,1)S(1)}, u32[]{:S(2)}, u32[]{:S(2)}) collective-permute-start(bf16[544,128]{1,0:T(8,128)(2,1)S(1)} %slice.31), channel_id=1, source_target_pairs={{0,3},{1,2},{2,1},{3,0},{4,7},{5,6},{6,5},{7,4},{8,11},{9,10},{10,... | collective-permute-start | bytes 417800 | tf_op jit(solution)/shard_map/ppermute | solution.py:32
  108.7 2.0 %collective-permute-start.41 = (bf16[832,128]{1,0:T(8,128)(2,1)S(1)}, bf16[832,128]{1,0:T(8,128)(2,1)S(1)}, u32[]{:S(2)}, u32[]{:S(2)}) collective-permute-start(bf16[832,128]{1,0:T(8,128)(2,1)S(1)} %fusion.1), channel_id=1, source_target_pairs={{0,8},{1,9},{2,10},{3,11},{4,12},{5,13},{6,14},{7,15},{8,0},{9,1},... | collective-permute-start | bytes 638984 | tf_op jit(solution)/shard_map/ppermute | solution.py:32
  110.8 1.6 collective-permute-done.29
  112.5 1.7 collective-permute-start.30
  114.6 2.0 %collective-permute-done.41 = bf16[832,128]{1,0:T(8,128)(2,1)S(1)} collective-permute-done((bf16[832,128]{1,0:T(8,128)(2,1)S(1)}, bf16[832,128]{1,0:T(8,128)(2,1)S(1)}, u32[]{:S(2)}, u32[]{:S(2)}) %collective-permute-start.41) | collective-permute-done | bytes 213024 | tf_op jit(solution)/shard_map/ppermute | solution.py:32
  118.4 5.9 %collective-permute-start.36 = (bf16[1,544,128]{2,1,0:T(8,128)(2,1)S(1)}, bf16[1,544,128]{2,1,0:T(8,128)(2,1)S(1)}, u32[]{:S(2)}, u32[]{:S(2)}) collective-permute-start(bf16[1,544,128]{2,1,0:T(8,128)(2,1)S(1)} %fusion.2), channel_id=1, source_target_pairs={{0,1},{1,0},{2,3},{3,2},{4,5},{5,4},{6,7},{7,6},{8,9},{9,8},{10,11... | collective-permute-start | bytes 417800 | tf_op jit(solution)/shard_map/ppermute | solution.py:32
  124.4 2.7 %collective-permute-start.43 = (bf16[208,128]{1,0:T(8,128)(2,1)S(1)}, bf16[208,128]{1,0:T(8,128)(2,1)S(1)}, u32[]{:S(2)}, u32[]{:S(2)}) collective-permute-start(bf16[208,128]{1,0:T(8,128)(2,1)S(1)} %fusion.7), channel_id=1, source_target_pairs={{0,1},{1,0},{2,3},{3,2},{4,5},{5,4},{6,7},{7,6},{8,9},{9,8},{10,11... | collective-permute-start | bytes 159752 | tf_op jit(solution)/shard_map/ppermute | solution.py:32
  127.1 2.0 %collective-permute-start.25 = (bf16[2,512,128]{2,1,0:T(8,128)(2,1)S(1)}, bf16[2,512,128]{2,1,0:T(8,128)(2,1)S(1)}, u32[]{:S(2)}, u32[]{:S(2)}) collective-permute-start(bf16[2,512,128]{2,1,0:T(8,128)(2,1)S(1)} %pad_maximum_fusion.5), channel_id=1, source_target_pairs={{0,16},{1,17},{2,18},{3,19},{4,20},{5,21},{6,22},{7,23},{8,24},{9,... | collective-permute-start | bytes 786440 | tf_op jit(solution)/shard_map/ppermute | solution.py:32
  129.2 2.5 %collective-permute-start.44 = (bf16[208,128]{1,0:T(8,128)(2,1)S(1)}, bf16[208,128]{1,0:T(8,128)(2,1)S(1)}, u32[]{:S(2)}, u32[]{:S(2)}) collective-permute-start(bf16[208,128]{1,0:T(8,128)(2,1)S(1)} %fusion.6), channel_id=1, source_target_pairs={{0,3},{1,2},{2,1},{3,0},{4,7},{5,6},{6,5},{7,4},{8,11},{9,10},{10,... | collective-permute-start | bytes 159752 | tf_op jit(solution)/shard_map/ppermute | solution.py:32
  131.8 1.9 %collective-permute-start.37 = (bf16[2,544,128]{2,1,0:T(8,128)(2,1)S(1)}, bf16[2,544,128]{2,1,0:T(8,128)(2,1)S(1)}, u32[]{:S(2)}, u32[]{:S(2)}) collective-permute-start(bf16[2,544,128]{2,1,0:T(8,128)(2,1)S(1)} %pad_maximum_fusion.4), channel_id=1, source_target_pairs={{0,8},{1,9},{2,10},{3,11},{4,12},{5,13},{6,14},{7,15},{8,0},{9,1},... | collective-permute-start | bytes 835592 | tf_op jit(solution)/shard_map/ppermute | solution.py:32
  135.4 2.0 %collective-permute-start.45 = (bf16[1,208,128]{2,1,0:T(8,128)(2,1)S(1)}, bf16[1,208,128]{2,1,0:T(8,128)(2,1)S(1)}, u32[]{:S(2)}, u32[]{:S(2)}) collective-permute-start(bf16[1,208,128]{2,1,0:T(8,128)(2,1)S(1)} %fusion.8), channel_id=1, source_target_pairs={{0,8},{1,9},{2,10},{3,11},{4,12},{5,13},{6,14},{7,15},{8,0},{9,1},... | collective-permute-start | bytes 159752 | tf_op jit(solution)/shard_map/ppermute | solution.py:32
  139.6 2.0 %collective-permute-start.46 = (bf16[2,208,128]{2,1,0:T(8,128)(2,1)S(1)}, bf16[2,208,128]{2,1,0:T(8,128)(2,1)S(1)}, u32[]{:S(2)}, u32[]{:S(2)}) collective-permute-start(bf16[2,208,128]{2,1,0:T(8,128)(2,1)S(1)} %pad_maximum_fusion.8), channel_id=1, source_target_pairs={{0,16},{1,17},{2,18},{3,19},{4,20},{5,21},{6,22},{7,23},{8,24},{9,... | collective-permute-start | bytes 319496 | tf_op jit(solution)/shard_map/ppermute | solution.py:32
  145.5 2.4 %collective-permute-start.32 = (bf16[4,512,128]{2,1,0:T(8,128)(2,1)S(1)}, bf16[4,512,128]{2,1,0:T(8,128)(2,1)}, u32[]{:S(2)}, u32[]{:S(2)}) collective-permute-start(bf16[4,512,128]{2,1,0:T(8,128)(2,1)S(1)} %pad_maximum_fusion.2.refs_4_), channel_id=1, source_target_pairs={{0,8},{1,9},{2,10},{3,11},{4,12},{5,13},{6,14},{7,15},{8,0},{9,1},... | collective-permute-start | bytes 1572872 | tf_op jit(solution)/shard_map/ppermute | solution.py:32
  147.8 12.8 %collective-permute-done.47 = bf16[4,208,128]{2,1,0:T(8,128)(2,1)S(1)} collective-permute-done((bf16[4,208,128]{2,1,0:T(8,128)(2,1)S(1)}, bf16[4,208,128]{2,1,0:T(8,128)(2,1)S(1)}, u32[]{:S(2)}, u32[]{:S(2)}) %collective-permute-start.47) | collective-permute-done | bytes 213024 | tf_op jit(solution)/shard_map/ppermute | solution.py:32
  167.0 11.4 %context_out.1 = (f32[49,256,256]{2,1,0:T(8,128)}, f32[3,192,128]{2,1,0:T(8,128)}, f32[3,384,256]{2,1,0:T(8,128)}, f32[256,128]{1,0:T(8,128)}, f32[128,128]{1,0:T(8,128)}, /*index=5*/f32[8,128]{1,0:T(8,128)}) custom-call(s32[2]{0:T(128)} %pad_add_fusion.place, bf16[4,512,128]{2,1,0:T(8,128)(2,1)} %copy-done.2, ...), custom_call_target="tpu_custom_call" | custom-call | flops 1000 | bytes 1000 | tf_op jit(solution)/shard_map/context_out/pallas_call | solution.py:225
  (171 shorter events, 41.6 us)
Async XLA Ops:
  13.9 7.6 %collective-permute-start.2 = (bf16[5,48,256]{2,1,0:T(8,128)(2,1)S(1)}, bf16[5,48,256]{2,1,0:T(8,128)(2,1)S(1)}, u32[]{:S(2)}, u32[]{:S(2)}) collective-permute-start(bf16[5,48,256]{2,1,0:T(8,128)(2,1)S(1)} %get-tuple-element.150), channel_id=1, source_target_pairs={{4,0},{8,4},{12,8},{16,12},{20,16},{24,20},{28,24},{5,1},{9,5},{13... | collective-permute-start | bytes 368648 | tf_op jit(solution)/shard_map/ppermute | solution.py:718
  15.2 6.3 %collective-permute-start.1 = (bf16[5,48,256]{2,1,0:T(8,128)(2,1)S(1)}, bf16[5,48,256]{2,1,0:T(8,128)(2,1)S(1)}, u32[]{:S(2)}, u32[]{:S(2)}) collective-permute-start(bf16[5,48,256]{2,1,0:T(8,128)(2,1)S(1)} %get-tuple-element.151), channel_id=1, source_target_pairs={{0,4},{4,8},{8,12},{12,16},{16,20},{20,24},{24,28},{1,5},{5,9},{9,... | collective-permute-start | bytes 368648 | tf_op jit(solution)/shard_map/ppermute | solution.py:718
  40.3 17.0 %collective-permute-start.6 = (bf16[960,128]{1,0:T(8,128)(2,1)}, bf16[960,128]{1,0:T(8,128)(2,1)S(1)}, u32[]{:S(2)}, u32[]{:S(2)}) collective-permute-start(bf16[960,128]{1,0:T(8,128)(2,1)} %get-tuple-element.92), channel_id=1, source_target_pairs={{0,8},{1,9},{2,10},{3,11},{4,12},{5,13},{6,14},{7,15},{8,0},{9,1},... | collective-permute-start | bytes 737288 | tf_op jit(solution)/shard_map/ppermute | solution.py:32
  43.0 15.9 %collective-permute-start.7 = (bf16[960,128]{1,0:T(8,128)(2,1)}, bf16[960,128]{1,0:T(8,128)(2,1)S(1)}, u32[]{:S(2)}, u32[]{:S(2)}) collective-permute-start(bf16[960,128]{1,0:T(8,128)(2,1)} %get-tuple-element.93), channel_id=1, source_target_pairs={{0,16},{1,17},{2,18},{3,19},{4,20},{5,21},{6,22},{7,23},{8,24},{9,... | collective-permute-start | bytes 737288 | tf_op jit(solution)/shard_map/ppermute | solution.py:32
  47.1 6.3 %collective-permute-start.4 = (bf16[5,48,256]{2,1,0:T(8,128)(2,1)S(1)}, bf16[5,48,256]{2,1,0:T(8,128)(2,1)S(1)}, u32[]{:S(2)}, u32[]{:S(2)}) collective-permute-start(bf16[5,48,256]{2,1,0:T(8,128)(2,1)S(1)} %get-tuple-element.149), channel_id=1, source_target_pairs={{0,4},{4,8},{8,12},{12,16},{16,20},{20,24},{24,28},{1,5},{5,9},{9,... | collective-permute-start | bytes 368648 | tf_op jit(solution)/shard_map/ppermute | solution.py:718
  50.4 21.6 %collective-permute-start.8 = (bf16[960,128]{1,0:T(8,128)(2,1)}, bf16[960,128]{1,0:T(8,128)(2,1)S(1)}, u32[]{:S(2)}, u32[]{:S(2)}) collective-permute-start(bf16[960,128]{1,0:T(8,128)(2,1)} %get-tuple-element.94), channel_id=1, source_target_pairs={{0,24},{1,25},{2,26},{3,27},{4,28},{5,29},{6,30},{7,31},{8,16},{9,... | collective-permute-start | bytes 737288 | tf_op jit(solution)/shard_map/ppermute | solution.py:32
  51.9 20.1 %collective-permute-start.9 = (bf16[960,128]{1,0:T(8,128)(2,1)}, bf16[960,128]{1,0:T(8,128)(2,1)S(1)}, u32[]{:S(2)}, u32[]{:S(2)}) collective-permute-start(bf16[960,128]{1,0:T(8,128)(2,1)} %get-tuple-element.95), channel_id=1, source_target_pairs={{0,1},{1,0},{2,3},{3,2},{4,5},{5,4},{6,7},{7,6},{8,9},{9,8},{10,11... | collective-permute-start | bytes 737288 | tf_op jit(solution)/shard_map/ppermute | solution.py:32
  53.5 18.5 %collective-permute-start.10 = (bf16[960,128]{1,0:T(8,128)(2,1)}, bf16[960,128]{1,0:T(8,128)(2,1)S(1)}, u32[]{:S(2)}, u32[]{:S(2)}) collective-permute-start(bf16[960,128]{1,0:T(8,128)(2,1)} %get-tuple-element.96), channel_id=1, source_target_pairs={{0,9},{1,8},{2,11},{3,10},{4,13},{5,12},{6,15},{7,14},{8,1},{9,0},... | collective-permute-start | bytes 737288 | tf_op jit(solution)/shard_map/ppermute | solution.py:32
  57.3 15.3 %collective-permute-start.11 = (bf16[960,128]{1,0:T(8,128)(2,1)}, bf16[960,128]{1,0:T(8,128)(2,1)S(1)}, u32[]{:S(2)}, u32[]{:S(2)}) collective-permute-start(bf16[960,128]{1,0:T(8,128)(2,1)} %get-tuple-element.97), channel_id=1, source_target_pairs={{0,17},{1,16},{2,19},{3,18},{4,21},{5,20},{6,23},{7,22},{8,25},{9,... | collective-permute-start | bytes 737288 | tf_op jit(solution)/shard_map/ppermute | solution.py:32
  58.9 19.3 %collective-permute-start.12 = (bf16[960,128]{1,0:T(8,128)(2,1)}, bf16[960,128]{1,0:T(8,128)(2,1)S(1)}, u32[]{:S(2)}, u32[]{:S(2)}) collective-permute-start(bf16[960,128]{1,0:T(8,128)(2,1)} %get-tuple-element.98), channel_id=1, source_target_pairs={{0,25},{1,24},{2,27},{3,26},{4,29},{5,28},{6,31},{7,30},{8,17},{9,... | collective-permute-start | bytes 737288 | tf_op jit(solution)/shard_map/ppermute | solution.py:32
  78.2 6.2 %collective-permute-start.13 = (bf16[960,128]{1,0:T(8,128)(2,1)S(1)}, bf16[960,128]{1,0:T(8,128)(2,1)S(1)}, u32[]{:S(2)}, u32[]{:S(2)}) collective-permute-start(bf16[960,128]{1,0:T(8,128)(2,1)S(1)} %copy-done.9), channel_id=1, source_target_pairs={{0,4},{1,5},{2,6},{3,7},{4,0},{5,1},{6,2},{7,3},{8,12},{9,13},{10,... | collective-permute-start | bytes 737288 | tf_op jit(solution)/shard_map/ppermute | solution.py:32
  78.2 6.2 %collective-permute-start.14 = (bf16[960,128]{1,0:T(8,128)(2,1)S(1)}, bf16[960,128]{1,0:T(8,128)(2,1)S(1)}, u32[]{:S(2)}, u32[]{:S(2)}) collective-permute-start(bf16[960,128]{1,0:T(8,128)(2,1)S(1)} %collective-permute-done.6.refs_1_), channel_id=1, source_target_pairs={{0,4},{1,5},{2,6},{3,7},{4,0},{5,1},{6,2},{7,3},{8,12},{9,13},{10,... | collective-permute-start | bytes 737288 | tf_op jit(solution)/shard_map/ppermute | solution.py:32
  78.7 6.2 %collective-permute-start.15 = (bf16[960,128]{1,0:T(8,128)(2,1)S(1)}, bf16[960,128]{1,0:T(8,128)(2,1)S(1)}, u32[]{:S(2)}, u32[]{:S(2)}) collective-permute-start(bf16[960,128]{1,0:T(8,128)(2,1)S(1)} %collective-permute-done.7.refs_2_), channel_id=1, source_target_pairs={{0,4},{1,5},{2,6},{3,7},{4,0},{5,1},{6,2},{7,3},{8,12},{9,13},{10,... | collective-permute-start | bytes 737288 | tf_op jit(solution)/shard_map/ppermute | solution.py:32
  80.1 10.1 %collective-permute-start.16 = (bf16[960,128]{1,0:T(8,128)(2,1)S(1)}, bf16[960,128]{1,0:T(8,128)(2,1)S(1)}, u32[]{:S(2)}, u32[]{:S(2)}) collective-permute-start(bf16[960,128]{1,0:T(8,128)(2,1)S(1)} %collective-permute-done.8.refs_3_), channel_id=1, source_target_pairs={{0,4},{1,5},{2,6},{3,7},{4,0},{5,1},{6,2},{7,3},{8,12},{9,13},{10,... | collective-permute-start | bytes 737288 | tf_op jit(solution)/shard_map/ppermute | solution.py:32
  82.0 8.1 %collective-permute-start.17 = (bf16[960,128]{1,0:T(8,128)(2,1)S(1)}, bf16[960,128]{1,0:T(8,128)(2,1)S(1)}, u32[]{:S(2)}, u32[]{:S(2)}) collective-permute-start(bf16[960,128]{1,0:T(8,128)(2,1)S(1)} %collective-permute-done.9.refs_4_), channel_id=1, source_target_pairs={{0,4},{1,5},{2,6},{3,7},{4,0},{5,1},{6,2},{7,3},{8,12},{9,13},{10,... | collective-permute-start | bytes 737288 | tf_op jit(solution)/shard_map/ppermute | solution.py:32
  92.1 7.4 %collective-permute-start.22 = (bf16[1664,128]{1,0:T(8,128)(2,1)S(1)}, bf16[1664,128]{1,0:T(8,128)(2,1)S(1)}, u32[]{:S(2)}, u32[]{:S(2)}) collective-permute-start(bf16[1664,128]{1,0:T(8,128)(2,1)S(1)} %fusion), channel_id=1, source_target_pairs={{0,4},{1,5},{2,6},{3,7},{4,0},{5,1},{6,2},{7,3},{8,12},{9,13},{10,... | collective-permute-start | bytes 1277960 | tf_op jit(solution)/shard_map/ppermute | solution.py:32
  100.5 10.3 %collective-permute-start.23 = (bf16[512,128]{1,0:T(8,128)(2,1)S(1)}, bf16[512,128]{1,0:T(8,128)(2,1)S(1)}, u32[]{:S(2)}, u32[]{:S(2)}) collective-permute-start(bf16[512,128]{1,0:T(8,128)(2,1)S(1)} %get-tuple-element.147), channel_id=1, source_target_pairs={{0,3},{1,2},{2,1},{3,0},{4,7},{5,6},{6,5},{7,4},{8,11},{9,10},{10,... | collective-permute-start | bytes 393224 | tf_op jit(solution)/shard_map/ppermute | solution.py:32
  104.2 8.2 %collective-permute-start.29 = (bf16[512,128]{1,0:T(8,128)(2,1)S(1)}, bf16[512,128]{1,0:T(8,128)(2,1)S(1)}, u32[]{:S(2)}, u32[]{:S(2)}) collective-permute-start(bf16[512,128]{1,0:T(8,128)(2,1)S(1)} %get-tuple-element.146), channel_id=1, source_target_pairs={{0,3},{1,2},{2,1},{3,0},{4,7},{5,6},{6,5},{7,4},{8,11},{9,10},{10,... | collective-permute-start | bytes 393224 | tf_op jit(solution)/shard_map/ppermute | solution.py:32
  105.0 13.3 %collective-permute-start.35 = (bf16[544,128]{1,0:T(8,128)(2,1)S(1)}, bf16[544,128]{1,0:T(8,128)(2,1)S(1)}, u32[]{:S(2)}, u32[]{:S(2)}) collective-permute-start(bf16[544,128]{1,0:T(8,128)(2,1)S(1)} %slice.31), channel_id=1, source_target_pairs={{0,3},{1,2},{2,1},{3,0},{4,7},{5,6},{6,5},{7,4},{8,11},{9,10},{10,... | collective-permute-start | bytes 417800 | tf_op jit(solution)/shard_map/ppermute | solution.py:32
  108.7 7.9 %collective-permute-start.41 = (bf16[832,128]{1,0:T(8,128)(2,1)S(1)}, bf16[832,128]{1,0:T(8,128)(2,1)S(1)}, u32[]{:S(2)}, u32[]{:S(2)}) collective-permute-start(bf16[832,128]{1,0:T(8,128)(2,1)S(1)} %fusion.1), channel_id=1, source_target_pairs={{0,8},{1,9},{2,10},{3,11},{4,12},{5,13},{6,14},{7,15},{8,0},{9,1},... | collective-permute-start | bytes 638984 | tf_op jit(solution)/shard_map/ppermute | solution.py:32
  112.5 24.9 %collective-permute-start.30 = (bf16[1,512,128]{2,1,0:T(8,128)(2,1)S(1)}, bf16[1,512,128]{2,1,0:T(8,128)(2,1)S(1)}, u32[]{:S(2)}, u32[]{:S(2)}) collective-permute-start(bf16[1,512,128]{2,1,0:T(8,128)(2,1)S(1)} %get-tuple-element.144), channel_id=1, source_target_pairs={{0,16},{1,17},{2,18},{3,19},{4,20},{5,21},{6,22},{7,23},{8,24},{9,... | collective-permute-start | bytes 393224 | tf_op jit(solution)/shard_map/ppermute | solution.py:32
  114.2 12.9 %collective-permute-start.24 = (bf16[1,512,128]{2,1,0:T(8,128)(2,1)S(1)}, bf16[1,512,128]{2,1,0:T(8,128)(2,1)S(1)}, u32[]{:S(2)}, u32[]{:S(2)}) collective-permute-start(bf16[1,512,128]{2,1,0:T(8,128)(2,1)S(1)} %get-tuple-element.145), channel_id=1, source_target_pairs={{0,8},{1,9},{2,10},{3,11},{4,12},{5,13},{6,14},{7,15},{8,0},{9,1},... | collective-permute-start | bytes 393224 | tf_op jit(solution)/shard_map/ppermute | solution.py:32
  116.7 7.6 %collective-permute-start.42 = (bf16[416,128]{1,0:T(8,128)(2,1)S(1)}, bf16[416,128]{1,0:T(8,128)(2,1)S(1)}, u32[]{:S(2)}, u32[]{:S(2)}) collective-permute-start(bf16[416,128]{1,0:T(8,128)(2,1)S(1)} %fusion.5), channel_id=1, source_target_pairs={{0,16},{1,17},{2,18},{3,19},{4,20},{5,21},{6,22},{7,23},{8,24},{9,... | collective-permute-start | bytes 319496 | tf_op jit(solution)/shard_map/ppermute | solution.py:32
  118.4 13.3 %collective-permute-start.36 = (bf16[1,544,128]{2,1,0:T(8,128)(2,1)S(1)}, bf16[1,544,128]{2,1,0:T(8,128)(2,1)S(1)}, u32[]{:S(2)}, u32[]{:S(2)}) collective-permute-start(bf16[1,544,128]{2,1,0:T(8,128)(2,1)S(1)} %fusion.2), channel_id=1, source_target_pairs={{0,1},{1,0},{2,3},{3,2},{4,5},{5,4},{6,7},{7,6},{8,9},{9,8},{10,11... | collective-permute-start | bytes 417800 | tf_op jit(solution)/shard_map/ppermute | solution.py:32
  127.1 14.5 %collective-permute-start.25 = (bf16[2,512,128]{2,1,0:T(8,128)(2,1)S(1)}, bf16[2,512,128]{2,1,0:T(8,128)(2,1)S(1)}, u32[]{:S(2)}, u32[]{:S(2)}) collective-permute-start(bf16[2,512,128]{2,1,0:T(8,128)(2,1)S(1)} %pad_maximum_fusion.5), channel_id=1, source_target_pairs={{0,16},{1,17},{2,18},{3,19},{4,20},{5,21},{6,22},{7,23},{8,24},{9,... | collective-permute-start | bytes 786440 | tf_op jit(solution)/shard_map/ppermute | solution.py:32
  131.8 10.8 %collective-permute-start.37 = (bf16[2,544,128]{2,1,0:T(8,128)(2,1)S(1)}, bf16[2,544,128]{2,1,0:T(8,128)(2,1)S(1)}, u32[]{:S(2)}, u32[]{:S(2)}) collective-permute-start(bf16[2,544,128]{2,1,0:T(8,128)(2,1)S(1)} %pad_maximum_fusion.4), channel_id=1, source_target_pairs={{0,8},{1,9},{2,10},{3,11},{4,12},{5,13},{6,14},{7,15},{8,0},{9,1},... | collective-permute-start | bytes 835592 | tf_op jit(solution)/shard_map/ppermute | solution.py:32
  137.4 8.0 %collective-permute-start.31 = (bf16[2,512,128]{2,1,0:T(8,128)(2,1)S(1)}, bf16[2,512,128]{2,1,0:T(8,128)(2,1)S(1)}, u32[]{:S(2)}, u32[]{:S(2)}) collective-permute-start(bf16[2,512,128]{2,1,0:T(8,128)(2,1)S(1)} %pad_maximum_fusion.6), channel_id=1, source_target_pairs={{0,1},{1,0},{2,3},{3,2},{4,5},{5,4},{6,7},{7,6},{8,9},{9,8},{10,11... | collective-permute-start | bytes 786440 | tf_op jit(solution)/shard_map/ppermute | solution.py:32
  141.7 19.0 %collective-permute-start.27 = (bf16[4,512,128]{2,1,0:T(8,128)(2,1)S(1)}, bf16[4,512,128]{2,1,0:T(8,128)(2,1)S(1)}, u32[]{:S(2)}, u32[]{:S(2)}) collective-permute-start(bf16[4,512,128]{2,1,0:T(8,128)(2,1)S(1)} %pad_maximum_fusion.1.refs_0_), channel_id=1, source_target_pairs={{0,4},{1,5},{2,6},{3,7},{4,0},{5,1},{6,2},{7,3},{8,12},{9,13},{10,... | collective-permute-start | bytes 1572872 | tf_op jit(solution)/shard_map/ppermute | solution.py:32
  141.8 19.5 %collective-permute-start.26 = (bf16[4,512,128]{2,1,0:T(8,128)(2,1)S(1)}, bf16[4,512,128]{2,1,0:T(8,128)(2,1)}, u32[]{:S(2)}, u32[]{:S(2)}) collective-permute-start(bf16[4,512,128]{2,1,0:T(8,128)(2,1)S(1)} %pad_maximum_fusion.1.refs_0_), channel_id=1, source_target_pairs={{0,1},{1,0},{2,3},{3,2},{4,5},{5,4},{6,7},{7,6},{8,9},{9,8},{10,11... | collective-permute-start | bytes 1572872 | tf_op jit(solution)/shard_map/ppermute | solution.py:32
  142.6 18.6 %collective-permute-start.38 = (bf16[4,544,128]{2,1,0:T(8,128)(2,1)S(1)}, bf16[4,544,128]{2,1,0:T(8,128)(2,1)}, u32[]{:S(2)}, u32[]{:S(2)}) collective-permute-start(bf16[4,544,128]{2,1,0:T(8,128)(2,1)S(1)} %pad_maximum_fusion.refs_8_), channel_id=1, source_target_pairs={{0,16},{1,17},{2,18},{3,19},{4,20},{5,21},{6,22},{7,23},{8,24},{9,... | collective-permute-start | bytes 1671176 | tf_op jit(solution)/shard_map/ppermute | solution.py:32
  144.5 16.2 %collective-permute-start.47 = (bf16[4,208,128]{2,1,0:T(8,128)(2,1)S(1)}, bf16[4,208,128]{2,1,0:T(8,128)(2,1)S(1)}, u32[]{:S(2)}, u32[]{:S(2)}) collective-permute-start(bf16[4,208,128]{2,1,0:T(8,128)(2,1)S(1)} %pad_maximum_fusion.7), channel_id=1, source_target_pairs={{0,1},{1,0},{2,3},{3,2},{4,5},{5,4},{6,7},{7,6},{8,9},{9,8},{10,11... | collective-permute-start | bytes 638984 | tf_op jit(solution)/shard_map/ppermute | solution.py:32
  145.5 16.3 %collective-permute-start.32 = (bf16[4,512,128]{2,1,0:T(8,128)(2,1)S(1)}, bf16[4,512,128]{2,1,0:T(8,128)(2,1)}, u32[]{:S(2)}, u32[]{:S(2)}) collective-permute-start(bf16[4,512,128]{2,1,0:T(8,128)(2,1)S(1)} %pad_maximum_fusion.2.refs_4_), channel_id=1, source_target_pairs={{0,8},{1,9},{2,10},{3,11},{4,12},{5,13},{6,14},{7,15},{8,0},{9,1},... | collective-permute-start | bytes 1572872 | tf_op jit(solution)/shard_map/ppermute | solution.py:32
  (50 other events, 364.0 us)

commit v3 on v2

--- a/solution.py
+++ b/solution.py
@@ -171,10 +171,16 @@
     sources = [refs[4 * p : 4 * p + 4] for p in range(parts)]
     little = refs[4 * parts : 4 * parts + 2]
     out, *small = refs[4 * parts + 2 : 4 * parts + 8]
-    gathered, ready, packed, sems = refs[4 * parts + 8 :]
+    gathered, ready, packed, sems, loaded, *held = refs[4 * parts + 8 :]
+    loads = [
+        pltpu.make_async_copy(refs[n], held[n], loaded.at[n]) for n in range(4 * parts)
+    ]
+    for load in loads:
+        load.start()
+    sources = [held[4 * p : 4 * p + 4] for p in range(parts)]
     tile, half = place[0], place[1]
     chip, core = tile >> 1, tile & 1
-    ones = [lax.broadcasted_iota(jnp.int32, (128, 128), n) for n in range(2)]
+    ones = [lax.broadcasted_iota(jnp.int32, (256, 256), n) for n in range(2)]
     identity = (ones[0] == ones[1]).astype(jnp.bfloat16)
     batches = [
         (p, n, min(2, bounds[p + 1] - n))
@@ -189,6 +195,9 @@
         )
 
     for n, (p, start, count) in enumerate(batches):
+        if start == bounds[p]:
+            for load in loads[4 * p : 4 * p + 4]:
+                load.wait()
         entries = sources[p][0].shape[0]
         for s in range(4):
             for i in range(entries):
@@ -200,17 +209,13 @@
                     gathered[
                         n % 4,
                         g,
-                        half ^ (mask // chips),
                         pl.ds(pl.multiple_of(whose * block, block), block),
-                        :,
+                        pl.ds(pl.multiple_of((half ^ (mask // chips)) * 128, 128), 128),
                     ] = sources[p][s][i, at : at + block, :]
         if n >= 4:
             copy(n - 4).wait()
         for g in range(count):
-            for u in range(2):
-                ready[n % 4, g, u * 128 : (u + 1) * 128, :] = dot(
-                    identity, gathered[n % 4, g, u], NT
-                )
+            ready[n % 4, g] = dot(identity, gathered[n % 4, g], NT)
         copy(n).start()
     write_small(chips, little, packed, small, chip, core, half)
     for n in range(max(0, len(batches) - 4), len(batches)):
@@ -225,13 +230,15 @@
     return pl.pallas_call(
         functools.partial(unpack_kernel, orders, bounds, chips, block),
         out_shape=[jax.ShapeDtypeStruct(shape, jnp.float32) for shape in shapes],
-        in_specs=[SMEM] + [VMEM] * len(operands),
+        in_specs=[SMEM] + [ANY] * (len(operands) - 2) + [VMEM] * 2,
         out_specs=[ANY] + [VMEM] * 5,
         scratch_shapes=[
-            pltpu.VMEM((4, 2, 2, wide, 128), jnp.bfloat16),
+            pltpu.VMEM((4, 2, wide, 256), jnp.bfloat16),
             pltpu.VMEM((4, 2, 256, wide), jnp.float32),
             pltpu.VMEM((packed_rows, 128), jnp.float32),
             pltpu.SemaphoreType.DMA((4,)),
+            pltpu.SemaphoreType.DMA((len(operands) - 2,)),
+            *[pltpu.VMEM(x.shape, x.dtype) for x in operands[:-2]],
         ],
         compiler_params=params(56),
         cost_estimate=LIGHT,

time: 179 us -> 179 us (level)
  no operation moved by 1% of the time
where the time goes in v3:
time: 179 us
  starting transfers between devices  75.7 us (42%)
  Pallas kernels  54.3 us (30%)
  waiting for transfers between devices  31.9 us (18%)
  local copies, waits for them, and re-layouts  14.3 us (8%)
    ppermute x43, starting transfers between devices, flip(): return lax.ppermute(value, BOTH, route)  61.1 us
    ppermute x43, waiting for transfers between devices, flip(): return lax.ppermute(value, BOTH, route)  31.1 us
    ppermute x6, starting transfers between devices, moved(): return lax.ppermute(block, 'tile', route)  14.6 us
    pallas_call x1, Pallas kernels, back(): pl.pallas_call(back_kernel, out_shape=outs, grid=(TAPS,), in_specs=specs,...  11.7 us
    pallas_call x1, Pallas kernels, unpack(): pl.pallas_call(functools.partial(unpack_kernel, orders, bounds, chips, bl...  11.5 us
    pallas_call x1, Pallas kernels, decode(): pl.pallas_call(functools.partial(decode_kernel, chips, block), out_shape=...  11.4 us
    pallas_call x1, Pallas kernels, wgrad(): pl.pallas_call(functools.partial(wgrad_kernel, chips, rows, width, block)...  6.86 us
    unnamed x68, local copies, waits for them, and re-layouts  5.74 us
  transfers between devices with their start and end apart: 49, of which 14 were waited for; matrix products, arithmetic and copies ran while one was open for 4% of the time, Pallas kernels for 13%

profile of v3, /device:TPU:0, one launch (start us, length us, event | category | flops | bytes accessed | tf_op | source)
XLA Modules:
  0.0 178.7 jit_solution(2965668296895610373)
XLA Ops:
  1.4 2.4 %collective-permute-start = (bf16[20,1,256]{2,1,0:T(2,128)(2,1)S(1)}, bf16[20,1,256]{2,1,0:T(2,128)(2,1)S(1)}, u32[]{:S(2)}, u32[]{:S(2)}) collective-permute-start(bf16[20,1,256]{2,1,0:T(2,128)(2,1)S(1)} %reshape_squeeze.8), channel_id=1, source_target_pairs={{0,4},{4,8},{8,12},{12,16},{16,20},{20,24},{24,28},{1,5},{5,9},{9,... | collective-permute-start | bytes 30728 | tf_op jit(solution)/shard_map/ppermute | solution.py:725
  3.8 3.2 %reshape_squeeze.6.image = bf16[20,128,256]{2,1,0:T(8,128)(2,1)} reshape(bf16[1,20,256,128]{3,2,1,0:T(8,128)(2,1)} %param.8) | data formatting | bytes 2621440 | tf_op jit(solution)/shard_map/reshape;squeeze | solution.py:751
  7.7 5.2 %encode.1 = (bf16[10,128,384]{2,1,0:T(8,128)(2,1)}, f32[10,128,256]{2,1,0:T(8,128)}, bf16[5,128,256]{2,1,0:T(8,128)(2,1)}, f32[5,128,256]{2,1,0:T(8,128)}) custom-call(bf16[20,128,256]{2,1,0:T(8,128)(2,1)} %reshape_squeeze.6.image, bf16[20,16,256]{2,1,0:T(8,128)(2,1)} %concatenate.35.halo, bf16[3,192,128]{2,1,0:T(8,128)(2,1)} %weight1.1, ...), custom_call_target="tpu_custom_call" | custom-call | flops 1000 | bytes 1000 | tf_op jit(solution)/shard_map/encode/pallas_call | solution.py:373
  15.2 5.1 %collective-permute-start.1 = (bf16[5,48,256]{2,1,0:T(8,128)(2,1)S(1)}, bf16[5,48,256]{2,1,0:T(8,128)(2,1)S(1)}, u32[]{:S(2)}, u32[]{:S(2)}) collective-permute-start(bf16[5,48,256]{2,1,0:T(8,128)(2,1)S(1)} %get-tuple-element.151), channel_id=1, source_target_pairs={{0,4},{4,8},{8,12},{12,16},{16,20},{20,24},{24,28},{1,5},{5,9},{9,... | collective-permute-start | bytes 368648 | tf_op jit(solution)/shard_map/ppermute | solution.py:725
  22.2 11.4 %decode.1 = (f32[2,2,8,640]{3,2,1,0:T(8,128)}, bf16[5,128,256]{2,1,0:T(8,128)(2,1)}, bf16[4,5,32,128]{3,2,1,0:T(8,128)(2,1)}, bf16[4,5,32,128]{3,2,1,0:T(8,128)(...) custom-call(s32[2]{0:T(128)} %pad_add_fusion.place, ...), custom_call_target="tpu_custom_call" | custom-call | flops 1000 | bytes 1000 | tf_op jit(solution)/shard_map/decode/pallas_call | solution.py:527
  33.5 2.4 %collective-permute-start.3 = (bf16[4,5,32,128]{3,2,1,0:T(8,128)(2,1)}, bf16[4,5,32,128]{3,2,1,0:T(8,128)(2,1)S(1)}, u32[]{:S(2)}, u32[]{:S(2)}) collective-permute-start(bf16[4,5,32,128]{3,2,1,0:T(8,128)(2,1)} %get-tuple-element.76), channel_id=1, source_target_pairs={{0,4},{1,5},{2,6},{3,7},{4,0},{5,1},{6,2},{7,3},{8,12},{9,13},{10,... | collective-permute-start | bytes 491528 | tf_op jit(solution)/shard_map/ppermute | solution.py:32
  37.8 2.5 %pack.1 = (bf16[960,128]{1,0:T(8,128)(2,1)}, bf16[960,128]{1,0:T(8,128)(2,1)}, bf16[960,128]{1,0:T(8,128)(2,1)}, bf16[960,128]{1,0:T(8,128)(2,1)}, bf16[960,128]...) custom-call(s32[2]{0:T(128)} %pad_add_fusion.place, ...), custom_call_target="tpu_custom_call" | custom-call | flops 1000 | bytes 1000 | tf_op jit(solution)/shard_map/pack/pallas_call | solution.py:135
  40.3 2.7 %collective-permute-start.6 = (bf16[960,128]{1,0:T(8,128)(2,1)}, bf16[960,128]{1,0:T(8,128)(2,1)S(1)}, u32[]{:S(2)}, u32[]{:S(2)}) collective-permute-start(bf16[960,128]{1,0:T(8,128)(2,1)} %get-tuple-element.92), channel_id=1, source_target_pairs={{0,8},{1,9},{2,10},{3,11},{4,12},{5,13},{6,14},{7,15},{8,0},{9,1},... | collective-permute-start | bytes 737288 | tf_op jit(solution)/shard_map/ppermute | solution.py:32
  43.0 1.8 %collective-permute-start.7 = (bf16[960,128]{1,0:T(8,128)(2,1)}, bf16[960,128]{1,0:T(8,128)(2,1)S(1)}, u32[]{:S(2)}, u32[]{:S(2)}) collective-permute-start(bf16[960,128]{1,0:T(8,128)(2,1)} %get-tuple-element.93), channel_id=1, source_target_pairs={{0,16},{1,17},{2,18},{3,19},{4,20},{5,21},{6,22},{7,23},{8,24},{9,... | collective-permute-start | bytes 737288 | tf_op jit(solution)/shard_map/ppermute | solution.py:32
  47.1 3.2 %collective-permute-start.4 = (bf16[5,48,256]{2,1,0:T(8,128)(2,1)S(1)}, bf16[5,48,256]{2,1,0:T(8,128)(2,1)S(1)}, u32[]{:S(2)}, u32[]{:S(2)}) collective-permute-start(bf16[5,48,256]{2,1,0:T(8,128)(2,1)S(1)} %get-tuple-element.149), channel_id=1, source_target_pairs={{0,4},{4,8},{8,12},{12,16},{16,20},{20,24},{24,28},{1,5},{5,9},{9,... | collective-permute-start | bytes 368648 | tf_op jit(solution)/shard_map/ppermute | solution.py:725
  53.5 3.8 %collective-permute-start.10 = (bf16[960,128]{1,0:T(8,128)(2,1)}, bf16[960,128]{1,0:T(8,128)(2,1)S(1)}, u32[]{:S(2)}, u32[]{:S(2)}) collective-permute-start(bf16[960,128]{1,0:T(8,128)(2,1)} %get-tuple-element.96), channel_id=1, source_target_pairs={{0,9},{1,8},{2,11},{3,10},{4,13},{5,12},{6,15},{7,14},{8,1},{9,0},... | collective-permute-start | bytes 737288 | tf_op jit(solution)/shard_map/ppermute | solution.py:32
  60.3 11.7 %back.1 = (f32[10,128,256]{2,1,0:T(8,128)}, f32[10,1,128]{2,1,0:T(1,128)}, f32[3,384,256]{2,1,0:T(8,128)}, f32[256,128]{1,0:T(8,128)}, f32[128,128]{1,0:T(8,128)}) custom-call(bf16[5,48,256]{2,1,0:T(8,128)(2,1)} %copy-done.27, bf16[5,128,256]{2,1,0:T(8,128)(2,1)} %get-tuple-element.85.gradient, bf16[5,48,256]{2,1,0:T(8,128)(2,1)} %copy-done.26, ...), custom_call_target="tpu_custom_call" | custom-call | flops 1000 | bytes 1000 | tf_op jit(solution)/shard_map/back/pallas_call | solution.py:647
  72.7 5.5 %collective-permute-done.12.refs_7_ = bf16[960,128]{1,0:T(8,128)(2,1)S(1)} collective-permute-done((bf16[960,128]{1,0:T(8,128)(2,1)}, bf16[960,128]{1,0:T(8,128)(2,1)S(1)}, u32[]{:S(2)}, u32[]{:S(2)}) %collective-permute-start.12) | collective-permute-done | bytes 245792 | tf_op jit(solution)/shard_map/ppermute | solution.py:32
  82.0 2.3 %collective-permute-start.17 = (bf16[960,128]{1,0:T(8,128)(2,1)S(1)}, bf16[960,128]{1,0:T(8,128)(2,1)S(1)}, u32[]{:S(2)}, u32[]{:S(2)}) collective-permute-start(bf16[960,128]{1,0:T(8,128)(2,1)S(1)} %collective-permute-done.9.refs_4_), channel_id=1, source_target_pairs={{0,4},{1,5},{2,6},{3,7},{4,0},{5,1},{6,2},{7,3},{8,12},{9,13},{10,... | collective-permute-start | bytes 737288 | tf_op jit(solution)/shard_map/ppermute | solution.py:32
  85.0 5.1 %finish.1 = (f32[10,256,128]{2,1,0:T(8,128)}, f32[3328,128]{1,0:T(8,128)}) custom-call(f32[10,128,256]{2,1,0:T(8,128)} %get-tuple-element.107.partial, f32[10,1,128]{2,1,0:T(1,128)} %copy-done.32, f32[10,128,256]{2,1,0:T(8,128)} %get-tuple-element.109.slope1, bf16[20,128,256]{2,1,0:T(8,128)(2,1)} %reshape_squeeze.6.image, ...), custom_call_target="tpu_custom_call" | custom-call | flops 1000 | bytes 1000 | tf_op jit(solution)/shard_map/finish/pallas_call | solution.py:707
  92.6 6.9 %context_term.1 = bf16[1568,128]{1,0:T(8,128)(2,1)} custom-call(s32[2]{0:T(128)} %pad_add_fusion.place, bf16[960,128]{1,0:T(8,128)(2,1)} %get-tuple-element.99.refs_0_, bf16[960,128]{1,0:T(8,128)(2,1)} %copy-done.10, bf16[960,128]{1,0:T(8,128)(2,1)} %copy-done.11, bf16[960,128]{1,0:T(8,128)(2,1)} %copy-done.12, bf16[960,128]{1,0:T(8,128)(2,1)} %copy-done.13, ...), custom_call_target="tpu_custom_call" | custom-call | flops 1000 | bytes 1000 | tf_op jit(solution)/shard_map/context_term/pallas_call | solution.py:102
  100.5 3.7 %collective-permute-start.23 = (bf16[512,128]{1,0:T(8,128)(2,1)S(1)}, bf16[512,128]{1,0:T(8,128)(2,1)S(1)}, u32[]{:S(2)}, u32[]{:S(2)}) collective-permute-start(bf16[512,128]{1,0:T(8,128)(2,1)S(1)} %get-tuple-element.147), channel_id=1, source_target_pairs={{0,3},{1,2},{2,1},{3,0},{4,7},{5,6},{6,5},{7,4},{8,11},{9,10},{10,... | collective-permute-start | bytes 393224 | tf_op jit(solution)/shard_map/ppermute | solution.py:32
  105.0 3.7 %collective-permute-start.35 = (bf16[544,128]{1,0:T(8,128)(2,1)S(1)}, bf16[544,128]{1,0:T(8,128)(2,1)S(1)}, u32[]{:S(2)}, u32[]{:S(2)}) collective-permute-start(bf16[544,128]{1,0:T(8,128)(2,1)S(1)} %slice.31), channel_id=1, source_target_pairs={{0,3},{1,2},{2,1},{3,0},{4,7},{5,6},{6,5},{7,4},{8,11},{9,10},{10,... | collective-permute-start | bytes 417800 | tf_op jit(solution)/shard_map/ppermute | solution.py:32
  108.7 2.0 %collective-permute-start.41 = (bf16[832,128]{1,0:T(8,128)(2,1)S(1)}, bf16[832,128]{1,0:T(8,128)(2,1)S(1)}, u32[]{:S(2)}, u32[]{:S(2)}) collective-permute-start(bf16[832,128]{1,0:T(8,128)(2,1)S(1)} %fusion.1), channel_id=1, source_target_pairs={{0,8},{1,9},{2,10},{3,11},{4,12},{5,13},{6,14},{7,15},{8,0},{9,1},... | collective-permute-start | bytes 638984 | tf_op jit(solution)/shard_map/ppermute | solution.py:32
  110.8 1.6 collective-permute-done.29
  112.5 1.7 collective-permute-start.30
  114.6 2.0 %collective-permute-done.41 = bf16[832,128]{1,0:T(8,128)(2,1)S(1)} collective-permute-done((bf16[832,128]{1,0:T(8,128)(2,1)S(1)}, bf16[832,128]{1,0:T(8,128)(2,1)S(1)}, u32[]{:S(2)}, u32[]{:S(2)}) %collective-permute-start.41) | collective-permute-done | bytes 213024 | tf_op jit(solution)/shard_map/ppermute | solution.py:32
  118.4 5.9 %collective-permute-start.36 = (bf16[1,544,128]{2,1,0:T(8,128)(2,1)S(1)}, bf16[1,544,128]{2,1,0:T(8,128)(2,1)S(1)}, u32[]{:S(2)}, u32[]{:S(2)}) collective-permute-start(bf16[1,544,128]{2,1,0:T(8,128)(2,1)S(1)} %fusion.2), channel_id=1, source_target_pairs={{0,1},{1,0},{2,3},{3,2},{4,5},{5,4},{6,7},{7,6},{8,9},{9,8},{10,11... | collective-permute-start | bytes 417800 | tf_op jit(solution)/shard_map/ppermute | solution.py:32
  124.4 2.7 %collective-permute-start.43 = (bf16[208,128]{1,0:T(8,128)(2,1)S(1)}, bf16[208,128]{1,0:T(8,128)(2,1)S(1)}, u32[]{:S(2)}, u32[]{:S(2)}) collective-permute-start(bf16[208,128]{1,0:T(8,128)(2,1)S(1)} %fusion.7), channel_id=1, source_target_pairs={{0,1},{1,0},{2,3},{3,2},{4,5},{5,4},{6,7},{7,6},{8,9},{9,8},{10,11... | collective-permute-start | bytes 159752 | tf_op jit(solution)/shard_map/ppermute | solution.py:32
  127.1 2.0 %collective-permute-start.25 = (bf16[2,512,128]{2,1,0:T(8,128)(2,1)S(1)}, bf16[2,512,128]{2,1,0:T(8,128)(2,1)S(1)}, u32[]{:S(2)}, u32[]{:S(2)}) collective-permute-start(bf16[2,512,128]{2,1,0:T(8,128)(2,1)S(1)} %pad_maximum_fusion.5), channel_id=1, source_target_pairs={{0,16},{1,17},{2,18},{3,19},{4,20},{5,21},{6,22},{7,23},{8,24},{9,... | collective-permute-start | bytes 786440 | tf_op jit(solution)/shard_map/ppermute | solution.py:32
  129.2 2.5 %collective-permute-start.44 = (bf16[208,128]{1,0:T(8,128)(2,1)S(1)}, bf16[208,128]{1,0:T(8,128)(2,1)S(1)}, u32[]{:S(2)}, u32[]{:S(2)}) collective-permute-start(bf16[208,128]{1,0:T(8,128)(2,1)S(1)} %fusion.6), channel_id=1, source_target_pairs={{0,3},{1,2},{2,1},{3,0},{4,7},{5,6},{6,5},{7,4},{8,11},{9,10},{10,... | collective-permute-start | bytes 159752 | tf_op jit(solution)/shard_map/ppermute | solution.py:32
  131.8 1.9 %collective-permute-start.37 = (bf16[2,544,128]{2,1,0:T(8,128)(2,1)S(1)}, bf16[2,544,128]{2,1,0:T(8,128)(2,1)S(1)}, u32[]{:S(2)}, u32[]{:S(2)}) collective-permute-start(bf16[2,544,128]{2,1,0:T(8,128)(2,1)S(1)} %pad_maximum_fusion.4), channel_id=1, source_target_pairs={{0,8},{1,9},{2,10},{3,11},{4,12},{5,13},{6,14},{7,15},{8,0},{9,1},... | collective-permute-start | bytes 835592 | tf_op jit(solution)/shard_map/ppermute | solution.py:32
  135.4 2.0 %collective-permute-start.45 = (bf16[1,208,128]{2,1,0:T(8,128)(2,1)S(1)}, bf16[1,208,128]{2,1,0:T(8,128)(2,1)S(1)}, u32[]{:S(2)}, u32[]{:S(2)}) collective-permute-start(bf16[1,208,128]{2,1,0:T(8,128)(2,1)S(1)} %fusion.8), channel_id=1, source_target_pairs={{0,8},{1,9},{2,10},{3,11},{4,12},{5,13},{6,14},{7,15},{8,0},{9,1},... | collective-permute-start | bytes 159752 | tf_op jit(solution)/shard_map/ppermute | solution.py:32
  139.6 2.0 %collective-permute-start.46 = (bf16[2,208,128]{2,1,0:T(8,128)(2,1)S(1)}, bf16[2,208,128]{2,1,0:T(8,128)(2,1)S(1)}, u32[]{:S(2)}, u32[]{:S(2)}) collective-permute-start(bf16[2,208,128]{2,1,0:T(8,128)(2,1)S(1)} %pad_maximum_fusion.8), channel_id=1, source_target_pairs={{0,16},{1,17},{2,18},{3,19},{4,20},{5,21},{6,22},{7,23},{8,24},{9,... | collective-permute-start | bytes 319496 | tf_op jit(solution)/shard_map/ppermute | solution.py:32
  145.5 2.4 %collective-permute-start.32 = (bf16[4,512,128]{2,1,0:T(8,128)(2,1)S(1)}, bf16[4,512,128]{2,1,0:T(8,128)(2,1)}, u32[]{:S(2)}, u32[]{:S(2)}) collective-permute-start(bf16[4,512,128]{2,1,0:T(8,128)(2,1)S(1)} %pad_maximum_fusion.2.refs_4_), channel_id=1, source_target_pairs={{0,8},{1,9},{2,10},{3,11},{4,12},{5,13},{6,14},{7,15},{8,0},{9,1},... | collective-permute-start | bytes 1572872 | tf_op jit(solution)/shard_map/ppermute | solution.py:32
  147.8 12.8 %collective-permute-done.47 = bf16[4,208,128]{2,1,0:T(8,128)(2,1)S(1)} collective-permute-done((bf16[4,208,128]{2,1,0:T(8,128)(2,1)S(1)}, bf16[4,208,128]{2,1,0:T(8,128)(2,1)S(1)}, u32[]{:S(2)}, u32[]{:S(2)}) %collective-permute-start.47) | collective-permute-done | bytes 213024 | tf_op jit(solution)/shard_map/ppermute | solution.py:32
  167.0 11.5 %context_out.1 = (f32[49,256,256]{2,1,0:T(8,128)}, f32[3,192,128]{2,1,0:T(8,128)}, f32[3,384,256]{2,1,0:T(8,128)}, f32[256,128]{1,0:T(8,128)}, f32[128,128]{1,0:T(8,128)}, /*index=5*/f32[8,128]{1,0:T(8,128)}) custom-call(s32[2]{0:T(128)} %pad_add_fusion.place, bf16[4,512,128]{2,1,0:T(8,128)(2,1)} %copy-done.2, ...), custom_call_target="tpu_custom_call" | custom-call | flops 1000 | bytes 1000 | tf_op jit(solution)/shard_map/context_out/pallas_call | solution.py:230
  (171 shorter events, 41.6 us)
Async XLA Ops:
  13.9 7.6 %collective-permute-start.2 = (bf16[5,48,256]{2,1,0:T(8,128)(2,1)S(1)}, bf16[5,48,256]{2,1,0:T(8,128)(2,1)S(1)}, u32[]{:S(2)}, u32[]{:S(2)}) collective-permute-start(bf16[5,48,256]{2,1,0:T(8,128)(2,1)S(1)} %get-tuple-element.150), channel_id=1, source_target_pairs={{4,0},{8,4},{12,8},{16,12},{20,16},{24,20},{28,24},{5,1},{9,5},{13... | collective-permute-start | bytes 368648 | tf_op jit(solution)/shard_map/ppermute | solution.py:725
  15.2 6.3 %collective-permute-start.1 = (bf16[5,48,256]{2,1,0:T(8,128)(2,1)S(1)}, bf16[5,48,256]{2,1,0:T(8,128)(2,1)S(1)}, u32[]{:S(2)}, u32[]{:S(2)}) collective-permute-start(bf16[5,48,256]{2,1,0:T(8,128)(2,1)S(1)} %get-tuple-element.151), channel_id=1, source_target_pairs={{0,4},{4,8},{8,12},{12,16},{16,20},{20,24},{24,28},{1,5},{5,9},{9,... | collective-permute-start | bytes 368648 | tf_op jit(solution)/shard_map/ppermute | solution.py:725
  40.3 17.0 %collective-permute-start.6 = (bf16[960,128]{1,0:T(8,128)(2,1)}, bf16[960,128]{1,0:T(8,128)(2,1)S(1)}, u32[]{:S(2)}, u32[]{:S(2)}) collective-permute-start(bf16[960,128]{1,0:T(8,128)(2,1)} %get-tuple-element.92), channel_id=1, source_target_pairs={{0,8},{1,9},{2,10},{3,11},{4,12},{5,13},{6,14},{7,15},{8,0},{9,1},... | collective-permute-start | bytes 737288 | tf_op jit(solution)/shard_map/ppermute | solution.py:32
  43.0 15.9 %collective-permute-start.7 = (bf16[960,128]{1,0:T(8,128)(2,1)}, bf16[960,128]{1,0:T(8,128)(2,1)S(1)}, u32[]{:S(2)}, u32[]{:S(2)}) collective-permute-start(bf16[960,128]{1,0:T(8,128)(2,1)} %get-tuple-element.93), channel_id=1, source_target_pairs={{0,16},{1,17},{2,18},{3,19},{4,20},{5,21},{6,22},{7,23},{8,24},{9,... | collective-permute-start | bytes 737288 | tf_op jit(solution)/shard_map/ppermute | solution.py:32
  47.1 6.3 %collective-permute-start.4 = (bf16[5,48,256]{2,1,0:T(8,128)(2,1)S(1)}, bf16[5,48,256]{2,1,0:T(8,128)(2,1)S(1)}, u32[]{:S(2)}, u32[]{:S(2)}) collective-permute-start(bf16[5,48,256]{2,1,0:T(8,128)(2,1)S(1)} %get-tuple-element.149), channel_id=1, source_target_pairs={{0,4},{4,8},{8,12},{12,16},{16,20},{20,24},{24,28},{1,5},{5,9},{9,... | collective-permute-start | bytes 368648 | tf_op jit(solution)/shard_map/ppermute | solution.py:725
  50.4 21.6 %collective-permute-start.8 = (bf16[960,128]{1,0:T(8,128)(2,1)}, bf16[960,128]{1,0:T(8,128)(2,1)S(1)}, u32[]{:S(2)}, u32[]{:S(2)}) collective-permute-start(bf16[960,128]{1,0:T(8,128)(2,1)} %get-tuple-element.94), channel_id=1, source_target_pairs={{0,24},{1,25},{2,26},{3,27},{4,28},{5,29},{6,30},{7,31},{8,16},{9,... | collective-permute-start | bytes 737288 | tf_op jit(solution)/shard_map/ppermute | solution.py:32
  51.9 20.1 %collective-permute-start.9 = (bf16[960,128]{1,0:T(8,128)(2,1)}, bf16[960,128]{1,0:T(8,128)(2,1)S(1)}, u32[]{:S(2)}, u32[]{:S(2)}) collective-permute-start(bf16[960,128]{1,0:T(8,128)(2,1)} %get-tuple-element.95), channel_id=1, source_target_pairs={{0,1},{1,0},{2,3},{3,2},{4,5},{5,4},{6,7},{7,6},{8,9},{9,8},{10,11... | collective-permute-start | bytes 737288 | tf_op jit(solution)/shard_map/ppermute | solution.py:32
  53.5 18.5 %collective-permute-start.10 = (bf16[960,128]{1,0:T(8,128)(2,1)}, bf16[960,128]{1,0:T(8,128)(2,1)S(1)}, u32[]{:S(2)}, u32[]{:S(2)}) collective-permute-start(bf16[960,128]{1,0:T(8,128)(2,1)} %get-tuple-element.96), channel_id=1, source_target_pairs={{0,9},{1,8},{2,11},{3,10},{4,13},{5,12},{6,15},{7,14},{8,1},{9,0},... | collective-permute-start | bytes 737288 | tf_op jit(solution)/shard_map/ppermute | solution.py:32
  57.3 15.3 %collective-permute-start.11 = (bf16[960,128]{1,0:T(8,128)(2,1)}, bf16[960,128]{1,0:T(8,128)(2,1)S(1)}, u32[]{:S(2)}, u32[]{:S(2)}) collective-permute-start(bf16[960,128]{1,0:T(8,128)(2,1)} %get-tuple-element.97), channel_id=1, source_target_pairs={{0,17},{1,16},{2,19},{3,18},{4,21},{5,20},{6,23},{7,22},{8,25},{9,... | collective-permute-start | bytes 737288 | tf_op jit(solution)/shard_map/ppermute | solution.py:32
  58.9 19.3 %collective-permute-start.12 = (bf16[960,128]{1,0:T(8,128)(2,1)}, bf16[960,128]{1,0:T(8,128)(2,1)S(1)}, u32[]{:S(2)}, u32[]{:S(2)}) collective-permute-start(bf16[960,128]{1,0:T(8,128)(2,1)} %get-tuple-element.98), channel_id=1, source_target_pairs={{0,25},{1,24},{2,27},{3,26},{4,29},{5,28},{6,31},{7,30},{8,17},{9,... | collective-permute-start | bytes 737288 | tf_op jit(solution)/shard_map/ppermute | solution.py:32
  78.2 6.2 %collective-permute-start.13 = (bf16[960,128]{1,0:T(8,128)(2,1)S(1)}, bf16[960,128]{1,0:T(8,128)(2,1)S(1)}, u32[]{:S(2)}, u32[]{:S(2)}) collective-permute-start(bf16[960,128]{1,0:T(8,128)(2,1)S(1)} %copy-done.9), channel_id=1, source_target_pairs={{0,4},{1,5},{2,6},{3,7},{4,0},{5,1},{6,2},{7,3},{8,12},{9,13},{10,... | collective-permute-start | bytes 737288 | tf_op jit(solution)/shard_map/ppermute | solution.py:32
  78.2 6.2 %collective-permute-start.14 = (bf16[960,128]{1,0:T(8,128)(2,1)S(1)}, bf16[960,128]{1,0:T(8,128)(2,1)S(1)}, u32[]{:S(2)}, u32[]{:S(2)}) collective-permute-start(bf16[960,128]{1,0:T(8,128)(2,1)S(1)} %collective-permute-done.6.refs_1_), channel_id=1, source_target_pairs={{0,4},{1,5},{2,6},{3,7},{4,0},{5,1},{6,2},{7,3},{8,12},{9,13},{10,... | collective-permute-start | bytes 737288 | tf_op jit(solution)/shard_map/ppermute | solution.py:32
  78.7 6.2 %collective-permute-start.15 = (bf16[960,128]{1,0:T(8,128)(2,1)S(1)}, bf16[960,128]{1,0:T(8,128)(2,1)S(1)}, u32[]{:S(2)}, u32[]{:S(2)}) collective-permute-start(bf16[960,128]{1,0:T(8,128)(2,1)S(1)} %collective-permute-done.7.refs_2_), channel_id=1, source_target_pairs={{0,4},{1,5},{2,6},{3,7},{4,0},{5,1},{6,2},{7,3},{8,12},{9,13},{10,... | collective-permute-start | bytes 737288 | tf_op jit(solution)/shard_map/ppermute | solution.py:32
  80.1 10.1 %collective-permute-start.16 = (bf16[960,128]{1,0:T(8,128)(2,1)S(1)}, bf16[960,128]{1,0:T(8,128)(2,1)S(1)}, u32[]{:S(2)}, u32[]{:S(2)}) collective-permute-start(bf16[960,128]{1,0:T(8,128)(2,1)S(1)} %collective-permute-done.8.refs_3_), channel_id=1, source_target_pairs={{0,4},{1,5},{2,6},{3,7},{4,0},{5,1},{6,2},{7,3},{8,12},{9,13},{10,... | collective-permute-start | bytes 737288 | tf_op jit(solution)/shard_map/ppermute | solution.py:32
  82.0 8.1 %collective-permute-start.17 = (bf16[960,128]{1,0:T(8,128)(2,1)S(1)}, bf16[960,128]{1,0:T(8,128)(2,1)S(1)}, u32[]{:S(2)}, u32[]{:S(2)}) collective-permute-start(bf16[960,128]{1,0:T(8,128)(2,1)S(1)} %collective-permute-done.9.refs_4_), channel_id=1, source_target_pairs={{0,4},{1,5},{2,6},{3,7},{4,0},{5,1},{6,2},{7,3},{8,12},{9,13},{10,... | collective-permute-start | bytes 737288 | tf_op jit(solution)/shard_map/ppermute | solution.py:32
  92.1 7.4 %collective-permute-start.22 = (bf16[1664,128]{1,0:T(8,128)(2,1)S(1)}, bf16[1664,128]{1,0:T(8,128)(2,1)S(1)}, u32[]{:S(2)}, u32[]{:S(2)}) collective-permute-start(bf16[1664,128]{1,0:T(8,128)(2,1)S(1)} %fusion), channel_id=1, source_target_pairs={{0,4},{1,5},{2,6},{3,7},{4,0},{5,1},{6,2},{7,3},{8,12},{9,13},{10,... | collective-permute-start | bytes 1277960 | tf_op jit(solution)/shard_map/ppermute | solution.py:32
  100.5 10.3 %collective-permute-start.23 = (bf16[512,128]{1,0:T(8,128)(2,1)S(1)}, bf16[512,128]{1,0:T(8,128)(2,1)S(1)}, u32[]{:S(2)}, u32[]{:S(2)}) collective-permute-start(bf16[512,128]{1,0:T(8,128)(2,1)S(1)} %get-tuple-element.147), channel_id=1, source_target_pairs={{0,3},{1,2},{2,1},{3,0},{4,7},{5,6},{6,5},{7,4},{8,11},{9,10},{10,... | collective-permute-start | bytes 393224 | tf_op jit(solution)/shard_map/ppermute | solution.py:32
  104.2 8.2 %collective-permute-start.29 = (bf16[512,128]{1,0:T(8,128)(2,1)S(1)}, bf16[512,128]{1,0:T(8,128)(2,1)S(1)}, u32[]{:S(2)}, u32[]{:S(2)}) collective-permute-start(bf16[512,128]{1,0:T(8,128)(2,1)S(1)} %get-tuple-element.146), channel_id=1, source_target_pairs={{0,3},{1,2},{2,1},{3,0},{4,7},{5,6},{6,5},{7,4},{8,11},{9,10},{10,... | collective-permute-start | bytes 393224 | tf_op jit(solution)/shard_map/ppermute | solution.py:32
  105.0 13.3 %collective-permute-start.35 = (bf16[544,128]{1,0:T(8,128)(2,1)S(1)}, bf16[544,128]{1,0:T(8,128)(2,1)S(1)}, u32[]{:S(2)}, u32[]{:S(2)}) collective-permute-start(bf16[544,128]{1,0:T(8,128)(2,1)S(1)} %slice.31), channel_id=1, source_target_pairs={{0,3},{1,2},{2,1},{3,0},{4,7},{5,6},{6,5},{7,4},{8,11},{9,10},{10,... | collective-permute-start | bytes 417800 | tf_op jit(solution)/shard_map/ppermute | solution.py:32
  108.7 7.9 %collective-permute-start.41 = (bf16[832,128]{1,0:T(8,128)(2,1)S(1)}, bf16[832,128]{1,0:T(8,128)(2,1)S(1)}, u32[]{:S(2)}, u32[]{:S(2)}) collective-permute-start(bf16[832,128]{1,0:T(8,128)(2,1)S(1)} %fusion.1), channel_id=1, source_target_pairs={{0,8},{1,9},{2,10},{3,11},{4,12},{5,13},{6,14},{7,15},{8,0},{9,1},... | collective-permute-start | bytes 638984 | tf_op jit(solution)/shard_map/ppermute | solution.py:32
  112.5 24.9 %collective-permute-start.30 = (bf16[1,512,128]{2,1,0:T(8,128)(2,1)S(1)}, bf16[1,512,128]{2,1,0:T(8,128)(2,1)S(1)}, u32[]{:S(2)}, u32[]{:S(2)}) collective-permute-start(bf16[1,512,128]{2,1,0:T(8,128)(2,1)S(1)} %get-tuple-element.144), channel_id=1, source_target_pairs={{0,16},{1,17},{2,18},{3,19},{4,20},{5,21},{6,22},{7,23},{8,24},{9,... | collective-permute-start | bytes 393224 | tf_op jit(solution)/shard_map/ppermute | solution.py:32
  114.2 12.9 %collective-permute-start.24 = (bf16[1,512,128]{2,1,0:T(8,128)(2,1)S(1)}, bf16[1,512,128]{2,1,0:T(8,128)(2,1)S(1)}, u32[]{:S(2)}, u32[]{:S(2)}) collective-permute-start(bf16[1,512,128]{2,1,0:T(8,128)(2,1)S(1)} %get-tuple-element.145), channel_id=1, source_target_pairs={{0,8},{1,9},{2,10},{3,11},{4,12},{5,13},{6,14},{7,15},{8,0},{9,1},... | collective-permute-start | bytes 393224 | tf_op jit(solution)/shard_map/ppermute | solution.py:32
  116.7 7.6 %collective-permute-start.42 = (bf16[416,128]{1,0:T(8,128)(2,1)S(1)}, bf16[416,128]{1,0:T(8,128)(2,1)S(1)}, u32[]{:S(2)}, u32[]{:S(2)}) collective-permute-start(bf16[416,128]{1,0:T(8,128)(2,1)S(1)} %fusion.5), channel_id=1, source_target_pairs={{0,16},{1,17},{2,18},{3,19},{4,20},{5,21},{6,22},{7,23},{8,24},{9,... | collective-permute-start | bytes 319496 | tf_op jit(solution)/shard_map/ppermute | solution.py:32
  118.4 13.3 %collective-permute-start.36 = (bf16[1,544,128]{2,1,0:T(8,128)(2,1)S(1)}, bf16[1,544,128]{2,1,0:T(8,128)(2,1)S(1)}, u32[]{:S(2)}, u32[]{:S(2)}) collective-permute-start(bf16[1,544,128]{2,1,0:T(8,128)(2,1)S(1)} %fusion.2), channel_id=1, source_target_pairs={{0,1},{1,0},{2,3},{3,2},{4,5},{5,4},{6,7},{7,6},{8,9},{9,8},{10,11... | collective-permute-start | bytes 417800 | tf_op jit(solution)/shard_map/ppermute | solution.py:32
  127.1 14.5 %collective-permute-start.25 = (bf16[2,512,128]{2,1,0:T(8,128)(2,1)S(1)}, bf16[2,512,128]{2,1,0:T(8,128)(2,1)S(1)}, u32[]{:S(2)}, u32[]{:S(2)}) collective-permute-start(bf16[2,512,128]{2,1,0:T(8,128)(2,1)S(1)} %pad_maximum_fusion.5), channel_id=1, source_target_pairs={{0,16},{1,17},{2,18},{3,19},{4,20},{5,21},{6,22},{7,23},{8,24},{9,... | collective-permute-start | bytes 786440 | tf_op jit(solution)/shard_map/ppermute | solution.py:32
  131.8 10.8 %collective-permute-start.37 = (bf16[2,544,128]{2,1,0:T(8,128)(2,1)S(1)}, bf16[2,544,128]{2,1,0:T(8,128)(2,1)S(1)}, u32[]{:S(2)}, u32[]{:S(2)}) collective-permute-start(bf16[2,544,128]{2,1,0:T(8,128)(2,1)S(1)} %pad_maximum_fusion.4), channel_id=1, source_target_pairs={{0,8},{1,9},{2,10},{3,11},{4,12},{5,13},{6,14},{7,15},{8,0},{9,1},... | collective-permute-start | bytes 835592 | tf_op jit(solution)/shard_map/ppermute | solution.py:32
  137.4 8.0 %collective-permute-start.31 = (bf16[2,512,128]{2,1,0:T(8,128)(2,1)S(1)}, bf16[2,512,128]{2,1,0:T(8,128)(2,1)S(1)}, u32[]{:S(2)}, u32[]{:S(2)}) collective-permute-start(bf16[2,512,128]{2,1,0:T(8,128)(2,1)S(1)} %pad_maximum_fusion.6), channel_id=1, source_target_pairs={{0,1},{1,0},{2,3},{3,2},{4,5},{5,4},{6,7},{7,6},{8,9},{9,8},{10,11... | collective-permute-start | bytes 786440 | tf_op jit(solution)/shard_map/ppermute | solution.py:32
  141.7 19.0 %collective-permute-start.27 = (bf16[4,512,128]{2,1,0:T(8,128)(2,1)S(1)}, bf16[4,512,128]{2,1,0:T(8,128)(2,1)S(1)}, u32[]{:S(2)}, u32[]{:S(2)}) collective-permute-start(bf16[4,512,128]{2,1,0:T(8,128)(2,1)S(1)} %pad_maximum_fusion.1.refs_0_), channel_id=1, source_target_pairs={{0,4},{1,5},{2,6},{3,7},{4,0},{5,1},{6,2},{7,3},{8,12},{9,13},{10,... | collective-permute-start | bytes 1572872 | tf_op jit(solution)/shard_map/ppermute | solution.py:32
  141.8 19.5 %collective-permute-start.26 = (bf16[4,512,128]{2,1,0:T(8,128)(2,1)S(1)}, bf16[4,512,128]{2,1,0:T(8,128)(2,1)}, u32[]{:S(2)}, u32[]{:S(2)}) collective-permute-start(bf16[4,512,128]{2,1,0:T(8,128)(2,1)S(1)} %pad_maximum_fusion.1.refs_0_), channel_id=1, source_target_pairs={{0,1},{1,0},{2,3},{3,2},{4,5},{5,4},{6,7},{7,6},{8,9},{9,8},{10,11... | collective-permute-start | bytes 1572872 | tf_op jit(solution)/shard_map/ppermute | solution.py:32
  142.6 18.6 %collective-permute-start.38 = (bf16[4,544,128]{2,1,0:T(8,128)(2,1)S(1)}, bf16[4,544,128]{2,1,0:T(8,128)(2,1)}, u32[]{:S(2)}, u32[]{:S(2)}) collective-permute-start(bf16[4,544,128]{2,1,0:T(8,128)(2,1)S(1)} %pad_maximum_fusion.refs_8_), channel_id=1, source_target_pairs={{0,16},{1,17},{2,18},{3,19},{4,20},{5,21},{6,22},{7,23},{8,24},{9,... | collective-permute-start | bytes 1671176 | tf_op jit(solution)/shard_map/ppermute | solution.py:32
  144.5 16.2 %collective-permute-start.47 = (bf16[4,208,128]{2,1,0:T(8,128)(2,1)S(1)}, bf16[4,208,128]{2,1,0:T(8,128)(2,1)S(1)}, u32[]{:S(2)}, u32[]{:S(2)}) collective-permute-start(bf16[4,208,128]{2,1,0:T(8,128)(2,1)S(1)} %pad_maximum_fusion.7), channel_id=1, source_target_pairs={{0,1},{1,0},{2,3},{3,2},{4,5},{5,4},{6,7},{7,6},{8,9},{9,8},{10,11... | collective-permute-start | bytes 638984 | tf_op jit(solution)/shard_map/ppermute | solution.py:32
  145.5 16.3 %collective-permute-start.32 = (bf16[4,512,128]{2,1,0:T(8,128)(2,1)S(1)}, bf16[4,512,128]{2,1,0:T(8,128)(2,1)}, u32[]{:S(2)}, u32[]{:S(2)}) collective-permute-start(bf16[4,512,128]{2,1,0:T(8,128)(2,1)S(1)} %pad_maximum_fusion.2.refs_4_), channel_id=1, source_target_pairs={{0,8},{1,9},{2,10},{3,11},{4,12},{5,13},{6,14},{7,15},{8,0},{9,1},... | collective-permute-start | bytes 1572872 | tf_op jit(solution)/shard_map/ppermute | solution.py:32
  (50 other events, 364.0 us)
